TPU v7x, 32 devices: a whole 2x2x4 slice. The times are simulated.
32 devices in a mesh: dp: 8 (over z, x), fsdp: 4 (over y, core).
Axes of the slice: x: 2, y: 2, z: 4, core: 2. Of those that a mesh axis runs over, the one named last changes fastest.
Arguments:
- act: bfloat16 [8192, 1536], P(('dp', 'fsdp')), may hold values from -6 to 6
- cotangent: bfloat16 [8192, 1536], P(('dp', 'fsdp')), may hold values from -6 to 6
- item_counts: int32 [32], P(('dp', 'fsdp')), may hold values from 0 to 1
- item_lengths: int32 [32], P(('dp', 'fsdp')), may hold values from 128 to 256, as said below
- time_steps: int32 [32], P(('dp', 'fsdp')), may hold values from 0 to 999
- ada_weight: float32 [1536, 4608], P(None, ('dp', 'fsdp')), may hold values from -0.15625 to 0.15625
- ada_first: float32 [1536, 4608], P(None, ('dp', 'fsdp')), may hold values from -0.00015258789 to 0.00015258789
- ada_second: float32 [1536, 4608], P(None, ('dp', 'fsdp')), may hold values from 4.5470155e-11 to 1.8188062e-10
- ada_average: float32 [1536, 4608], P(None, ('dp', 'fsdp')), may hold values from -0.15625 to 0.15625
- in_weight: float32 [1536, 6144], P(None, ('dp', 'fsdp')), may hold values from -0.25515518 to 0.25515518
- in_first: float32 [1536, 6144], P(None, ('dp', 'fsdp')), may hold values from -0.00015258789 to 0.00015258789
- in_second: float32 [1536, 6144], P(None, ('dp', 'fsdp')), may hold values from 4.5470155e-11 to 1.8188062e-10
- in_average: float32 [1536, 6144], P(None, ('dp', 'fsdp')), may hold values from -0.15625 to 0.15625
- x_weight: float32 [3072, 128], P(('dp', 'fsdp')), may hold values from -0.109375 to 0.109375
- x_first: float32 [3072, 128], P(('dp', 'fsdp')), may hold values from -0.00015258789 to 0.00015258789
- x_second: float32 [3072, 128], P(('dp', 'fsdp')), may hold values from 4.5470155e-11 to 1.8188062e-10
- x_average: float32 [3072, 128], P(('dp', 'fsdp')), may hold values from -0.109375 to 0.109375
- dt_weight: float32 [96, 3072], P(None, ('dp', 'fsdp')), may hold values from -0.625 to 0.625
- dt_first: float32 [96, 3072], P(None, ('dp', 'fsdp')), may hold values from -0.00015258789 to 0.00015258789
- dt_second: float32 [96, 3072], P(None, ('dp', 'fsdp')), may hold values from 4.5470155e-11 to 1.8188062e-10
- dt_average: float32 [96, 3072], P(None, ('dp', 'fsdp')), may hold values from -0.625 to 0.625
- chan_table: float32 [23, 3072], P(None, ('dp', 'fsdp')), may hold values from -7 to 3
- chan_first: float32 [23, 3072], P(None, ('dp', 'fsdp')), may hold values from -0.00015258789 to 0.00015258789
- chan_second: float32 [23, 3072], P(None, ('dp', 'fsdp')), may hold values from 4.5470155e-11 to 1.8188062e-10
- chan_average: float32 [23, 3072], P(None, ('dp', 'fsdp')), may hold values from -7 to 3
- out_weight: float32 [3072, 1536], P(('dp', 'fsdp')), may hold values from -0.4375 to 0.4375
- out_first: float32 [3072, 1536], P(('dp', 'fsdp')), may hold values from -0.00015258789 to 0.00015258789
- out_second: float32 [3072, 1536], P(('dp', 'fsdp')), may hold values from 4.5470155e-11 to 1.8188062e-10
- out_average: float32 [3072, 1536], P(('dp', 'fsdp')), may hold values from -0.4375 to 0.4375
Outputs:
- final: float32 [8192, 1536], P(('dp', 'fsdp'))
- act_grad: float32 [8192, 1536], P(('dp', 'fsdp'))
- grad_norm: float32 [], replicated
- ada_first_new: float32 [1536, 4608], P(None, ('dp', 'fsdp'))
- ada_second_new: float32 [1536, 4608], P(None, ('dp', 'fsdp'))
- ada_weight_new: float32 [1536, 4608], P(None, ('dp', 'fsdp'))
- ada_average_new: float32 [1536, 4608], P(None, ('dp', 'fsdp'))
- in_first_new: float32 [1536, 6144], P(None, ('dp', 'fsdp'))
- in_second_new: float32 [1536, 6144], P(None, ('dp', 'fsdp'))
- in_weight_new: float32 [1536, 6144], P(None, ('dp', 'fsdp'))
- in_average_new: float32 [1536, 6144], P(None, ('dp', 'fsdp'))
- x_first_new: float32 [3072, 128], P(('dp', 'fsdp'))
- x_second_new: float32 [3072, 128], P(('dp', 'fsdp'))
- x_weight_new: float32 [3072, 128], P(('dp', 'fsdp'))
- x_average_new: float32 [3072, 128], P(('dp', 'fsdp'))
- dt_first_new: float32 [96, 3072], P(None, ('dp', 'fsdp'))
- dt_second_new: float32 [96, 3072], P(None, ('dp', 'fsdp'))
- dt_weight_new: float32 [96, 3072], P(None, ('dp', 'fsdp'))
- dt_average_new: float32 [96, 3072], P(None, ('dp', 'fsdp'))
- chan_first_new: float32 [23, 3072], P(None, ('dp', 'fsdp'))
- chan_second_new: float32 [23, 3072], P(None, ('dp', 'fsdp'))
- chan_table_new: float32 [23, 3072], P(None, ('dp', 'fsdp'))
- chan_average_new: float32 [23, 3072], P(None, ('dp', 'fsdp'))
- out_first_new: float32 [3072, 1536], P(('dp', 'fsdp'))
- out_second_new: float32 [3072, 1536], P(('dp', 'fsdp'))
- out_weight_new: float32 [3072, 1536], P(('dp', 'fsdp'))
- out_average_new: float32 [3072, 1536], P(('dp', 'fsdp'))
Inputs may be any that keep to these rules, and one draw needn't show every extreme that they name: `item_lengths`: the first item slot of the whole batch is full.
All inputs are finite; a program needn't handle non-finite values.
Results may differ from a plain program's by a relative error of at most 0.012.
The roundings to bfloat16 on the way count: a program that leaves them out, or rounds other values in their place, can miss the bound.
Values may be sent and summed in bfloat16 or wider, within the bound.
No kernel may reach another device: no remote copies, remote signals or barrier semaphores. Data moves between devices by JAX's collectives and lax.ppermute only.
A program may use at most 320 MiB of HBM per device.

v0:
```python
import math

import jax
import jax.numpy as jnp
from jax import lax
from jax.sharding import PartitionSpec as P

D = 1536
E = 3072
N = 16
R = 96
CONV = 4
ITEM = 256
BLOCK = 32
STEP = 10


def product(left, right):
    return jnp.dot(left, right, preferred_element_type=jnp.float32)


def left_outer(left, right):
    return lax.dot_general(
        left, right, (((0,), (0,)), ((), ())), preferred_element_type=jnp.float32
    )


def right_inner(left, right):
    return lax.dot_general(
        left, right, (((1,), (1,)), ((), ())), preferred_element_type=jnp.float32
    )


def embed_time(steps):
    half = D // 2
    freqs = jnp.exp(-math.log(10000.0) * jnp.arange(half, dtype=jnp.float32) / half)
    angles = steps.astype(jnp.float32)[:, None] * freqs[None, :]
    return jax.nn.silu(jnp.concatenate([jnp.cos(angles), jnp.sin(angles)], axis=1))


def modulate(x, mod):
    mean = jnp.mean(x, axis=2, keepdims=True)
    centered = x - mean
    var = jnp.mean(centered * centered, axis=2, keepdims=True)
    normed = centered * lax.rsqrt(var + 1e-06)
    return normed * (1.0 + mod[:, None, D : 2 * D]) + mod[:, None, :D]


def mix_conv(xs, chan):
    padded = jnp.pad(xs, ((0, 0), (CONV - 1, 0), (0, 0)))
    pre = chan[CONV][None, None, :]
    for k in range(CONV):
        pre = pre + padded[:, k : k + ITEM, :] * chan[k][None, None, :]
    return jax.nn.silu(pre)


def finish(x, o, mod):
    return x + mod[:, None, 2 * D :] * o


def selective(u, dtp, bc, z, chan):
    count = u.shape[0]
    blocks = ITEM // BLOCK
    step = jax.nn.softplus(dtp + chan[CONV + 1])
    a_neg = -jnp.exp(chan[CONV + 3 :])

    def split(v):
        return jnp.moveaxis(v.reshape(count, blocks, BLOCK, v.shape[-1]), 1, 0)

    def join(first, second):
        return (first[0] * second[0], second[0] * first[1] + second[1])

    @jax.checkpoint
    def block(state, pieces):
        u_blk, step_blk, b_blk, c_blk = pieces
        decay = jnp.exp(step_blk[:, :, None, :] * a_neg[None, None])
        drive = b_blk[:, :, :, None] * (step_blk * u_blk)[:, :, None, :]
        total_decay, total_drive = lax.associative_scan(join, (decay, drive), axis=1)
        states = total_decay * state[:, None] + total_drive
        outs = jnp.sum(states * c_blk[:, :, :, None], axis=2)
        return (states[:, -1], outs)

    start = jnp.zeros((count, N, E), jnp.float32)
    _, outs = lax.scan(
        block, start, (split(u), split(step), split(bc[..., :N]), split(bc[..., N:]))
    )
    y = jnp.moveaxis(outs, 0, 1).reshape(count, ITEM, E) + chan[CONV + 2] * u
    return y * jax.nn.silu(z)


def on_device(
    act,
    cotangent,
    item_counts,
    item_lengths,
    time_steps,
    ada_weight,
    ada_first,
    ada_second,
    ada_average,
    in_weight,
    in_first,
    in_second,
    in_average,
    x_weight,
    x_first,
    x_second,
    x_average,
    dt_weight,
    dt_first,
    dt_second,
    dt_average,
    chan_table,
    chan_first,
    chan_second,
    chan_average,
    out_weight,
    out_first,
    out_second,
    out_average,
):
    bf = jnp.bfloat16
    count = item_lengths.shape[0]
    rows = count * ITEM
    in_local = in_weight.astype(bf)
    x_local = x_weight.astype(bf)
    dt_local = dt_weight.astype(bf)
    out_local = out_weight.astype(bf)
    ada_full, in_full, x_full, dt_full, chan_full, out_full = (
        lax.all_gather(ada_weight.astype(bf), ("dp", "fsdp"), axis=1, tiled=True),
        lax.all_gather(in_local, ("dp", "fsdp"), axis=1, tiled=True),
        lax.all_gather(x_local, ("dp", "fsdp"), axis=0, tiled=True),
        lax.all_gather(dt_local, ("dp", "fsdp"), axis=1, tiled=True),
        lax.all_gather(chan_table.astype(bf), ("dp", "fsdp"), axis=1, tiled=True),
        lax.all_gather(out_local, ("dp", "fsdp"), axis=0, tiled=True),
    )
    chan = chan_full.astype(jnp.float32)
    live_items = jnp.arange(count, dtype=jnp.int32) < item_counts[0]
    live_rows = jnp.arange(ITEM, dtype=jnp.int32)[None, :] < item_lengths[:, None]
    live = (live_items[:, None] & live_rows).astype(jnp.float32)
    x = act.astype(jnp.float32).reshape(count, ITEM, D)
    cond = embed_time(time_steps).astype(bf)
    mod = product(cond, ada_full)
    h, mod_pull = jax.vjp(modulate, x, mod)
    h_low = h.astype(bf).reshape(rows, D)
    xz = product(h_low, in_full).reshape(count, ITEM, 2 * E)
    u, conv_pull = jax.vjp(mix_conv, xz[..., :E], chan)
    u_low = u.astype(bf).reshape(rows, E)
    proj = product(u_low, x_full)
    rank_low = proj[:, :R].astype(bf)
    dtp = product(rank_low, dt_full).reshape(count, ITEM, E)
    mixed, scan_pull = jax.vjp(
        selective, u, dtp, proj[:, R:].reshape(count, ITEM, 2 * N), xz[..., E:], chan
    )
    mixed_low = mixed.astype(bf).reshape(rows, E)
    o = product(mixed_low, out_full).reshape(count, ITEM, D)
    final, fin_pull = jax.vjp(finish, x, o, mod)
    in_back, x_back, dt_back, out_back = (
        lax.all_gather(in_local, ("dp", "fsdp"), axis=1, tiled=True),
        lax.all_gather(x_local, ("dp", "fsdp"), axis=0, tiled=True),
        lax.all_gather(dt_local, ("dp", "fsdp"), axis=1, tiled=True),
        lax.all_gather(out_local, ("dp", "fsdp"), axis=0, tiled=True),
    )
    dfinal = cotangent.astype(jnp.float32).reshape(count, ITEM, D) * live[..., None]
    dx_res, d_o, dmod_fin = fin_pull(dfinal)
    do_low = d_o.reshape(rows, D).astype(bf)
    grad_out = left_outer(mixed_low, do_low)
    dmixed = right_inner(do_low, out_back).reshape(count, ITEM, E)
    du_scan, ddtp, dbc, dz, dchan_scan = scan_pull(dmixed)
    ddtp_low = ddtp.reshape(rows, E).astype(bf)
    grad_dt = left_outer(rank_low, ddtp_low)
    drank = right_inner(ddtp_low, dt_back)
    dproj_low = jnp.concatenate([drank, dbc.reshape(rows, 2 * N)], axis=1).astype(bf)
    grad_x = left_outer(u_low, dproj_low)
    du = du_scan + right_inner(dproj_low, x_back).reshape(count, ITEM, E)
    dxs, dchan_conv = conv_pull(du)
    dxz_low = jnp.concatenate([dxs, dz], axis=2).reshape(rows, 2 * E).astype(bf)
    grad_in = left_outer(h_low, dxz_low)
    dh = right_inner(dxz_low, in_back).reshape(count, ITEM, D)
    dx_norm, dmod_norm = mod_pull(dh)
    act_grad = (dx_res + dx_norm).reshape(rows, D)
    dmod_low = (dmod_fin + dmod_norm).astype(bf)
    grad_ada = left_outer(cond, dmod_low)
    grad_chan = dchan_scan + dchan_conv
    shares = (
        lax.psum_scatter(grad_ada, ("dp", "fsdp"), scatter_dimension=1, tiled=True),
        lax.psum_scatter(grad_in, ("dp", "fsdp"), scatter_dimension=1, tiled=True),
        lax.psum_scatter(grad_x, ("dp", "fsdp"), scatter_dimension=0, tiled=True),
        lax.psum_scatter(grad_dt, ("dp", "fsdp"), scatter_dimension=1, tiled=True),
        lax.psum_scatter(grad_chan, ("dp", "fsdp"), scatter_dimension=1, tiled=True),
        lax.psum_scatter(grad_out, ("dp", "fsdp"), scatter_dimension=0, tiled=True),
    )
    local = jnp.float32(0.0)
    for g in shares:
        local = local + jnp.sum(g * g)
    total = lax.psum(local, ("dp", "fsdp"))
    grad_norm = jnp.sqrt(total)
    factor = jnp.minimum(1.0, 1.0 / (grad_norm + 1e-06))
    ema_keep = min(0.9999, (1.0 + STEP) / (10.0 + STEP))
    states = (
        (ada_weight, ada_first, ada_second, ada_average),
        (in_weight, in_first, in_second, in_average),
        (x_weight, x_first, x_second, x_average),
        (dt_weight, dt_first, dt_second, dt_average),
        (chan_table, chan_first, chan_second, chan_average),
        (out_weight, out_first, out_second, out_average),
    )
    settings = ((0.03, 0.1), (0.03, 0.1), (0.03, 0.1), (0.03, 0.1), (0.5, 0.0), (0.03, 0.1))
    results = []
    for (weight, first, second, average), g, (learn_rate, weight_decay) in zip(
        states, shares, settings
    ):
        clipped = g * factor
        first = 0.9 * first + 0.1 * clipped
        second = 0.999 * second + 0.001 * clipped * clipped
        first_hat = first / (1.0 - 0.9**STEP)
        second_hat = second / (1.0 - 0.999**STEP)
        weight = weight - learn_rate * (
            first_hat / (jnp.sqrt(second_hat) + 1e-08) + weight_decay * weight
        )
        average = ema_keep * average + (1.0 - ema_keep) * weight
        results.extend([first, second, weight, average])
    return (
        final.reshape(rows, D),
        act_grad,
        grad_norm,
        results[0],
        results[1],
        results[2],
        results[3],
        results[4],
        results[5],
        results[6],
        results[7],
        results[8],
        results[9],
        results[10],
        results[11],
        results[12],
        results[13],
        results[14],
        results[15],
        results[16],
        results[17],
        results[18],
        results[19],
        results[20],
        results[21],
        results[22],
        results[23],
    )


def solution(mesh):
    placed = (
        P(("dp", "fsdp"), None),
        P(("dp", "fsdp"), None),
        P(("dp", "fsdp")),
        P(("dp", "fsdp")),
        P(("dp", "fsdp")),
        P(None, ("dp", "fsdp")),
        P(None, ("dp", "fsdp")),
        P(None, ("dp", "fsdp")),
        P(None, ("dp", "fsdp")),
        P(None, ("dp", "fsdp")),
        P(None, ("dp", "fsdp")),
        P(None, ("dp", "fsdp")),
        P(None, ("dp", "fsdp")),
        P(("dp", "fsdp"), None),
        P(("dp", "fsdp"), None),
        P(("dp", "fsdp"), None),
        P(("dp", "fsdp"), None),
        P(None, ("dp", "fsdp")),
        P(None, ("dp", "fsdp")),
        P(None, ("dp", "fsdp")),
        P(None, ("dp", "fsdp")),
        P(None, ("dp", "fsdp")),
        P(None, ("dp", "fsdp")),
        P(None, ("dp", "fsdp")),
        P(None, ("dp", "fsdp")),
        P(("dp", "fsdp"), None),
        P(("dp", "fsdp"), None),
        P(("dp", "fsdp"), None),
        P(("dp", "fsdp"), None),
    )
    return jax.shard_map(
        on_device,
        mesh=mesh,
        in_specs=placed,
        out_specs=(
            P(("dp", "fsdp"), None),
            P(("dp", "fsdp"), None),
            P(),
            P(None, ("dp", "fsdp")),
            P(None, ("dp", "fsdp")),
            P(None, ("dp", "fsdp")),
            P(None, ("dp", "fsdp")),
            P(None, ("dp", "fsdp")),
            P(None, ("dp", "fsdp")),
            P(None, ("dp", "fsdp")),
            P(None, ("dp", "fsdp")),
            P(("dp", "fsdp"), None),
            P(("dp", "fsdp"), None),
            P(("dp", "fsdp"), None),
            P(("dp", "fsdp"), None),
            P(None, ("dp", "fsdp")),
            P(None, ("dp", "fsdp")),
            P(None, ("dp", "fsdp")),
            P(None, ("dp", "fsdp")),
            P(None, ("dp", "fsdp")),
            P(None, ("dp", "fsdp")),
            P(None, ("dp", "fsdp")),
            P(None, ("dp", "fsdp")),
            P(("dp", "fsdp"), None),
            P(("dp", "fsdp"), None),
            P(("dp", "fsdp"), None),
            P(("dp", "fsdp"), None),
        ),
        check_vma=False,
    )
```

profile of v0, /device:TPU:0, one launch (start us, length us, event | category | flops | bytes accessed | tf_op | source)
XLA Modules:
  0.0 6565.4 jit_solution(8449621588315210453)
XLA Ops:
  13.9 44.3 all-gather
  60.6 42.5 all_gather.26
  103.1 42.0 all_gather.25
  155.5 96.7 %all-gather.7.cloned.1.call-done = bf16[1536,6144]{0,1:T(8,128)(2,1)} async-done(((bf16[1536,192]{0,1:T(8,128)(2,1)}), bf16[1536,6144]{0,1:T(8,128)(2,1)}) %all-gather.7.cloned.1.call-update) | async-done | bytes 18874384 | tf_op jit(solution)/shard_map/all_gather | solution.py:131
  266.1 69.8 %all-gather.9.cloned.1.call-done = bf16[3072,1536]{1,0:T(8,128)(2,1)} async-done(((bf16[96,1536]{1,0:T(8,128)(2,1)}), bf16[3072,1536]{1,0:T(8,128)(2,1)}) %all-gather.9.cloned.1.call-update) | async-done | bytes 9437200 | tf_op jit(solution)/shard_map/all_gather | solution.py:135
  336.0 17.6 multiply_reduce_fusion.11
  365.1 1404.1 %while.39 = (s32[]{:T(128)}, f32[1,16,3072]{2,1,0:T(8,128)}, f32[8,1,32,3072]{3,2,1,0:T(8,128)}, f32[8,1,16,3072]{3,2,1,0:T(8,128)}, f32[8,1,32,3072]{3,2,1,0:T(...) while((s32[]{:T(128)}, f32[1,16,3072]{2,1,0:T(8,128)}, ...), condition=%wide.region_4.5_spmd, body=%wide.region_2.4_spmd.sunk | while | flops 29442048 | bytes 351557152 | solution.py:84
  1775.2 3563.4 %while.40 = (s32[]{:T(128)}, f32[16,3072]{1,0:T(8,128)}, f32[1,16,3072]{2,1,0:T(8,128)}, f32[8,1,32,3072]{3,2,1,0:T(8,128)}, f32[8,1,32,3072]{3,2,1,0:T(8,128)},...) while((s32[]{:T(128)}, f32[16,3072]{1,0:T(8,128)}, ...), condition=%wide.region_12.13_spmd.clone, body=%wide.region_5.12_spmd.clone.sunk | while | flops 92896256 | bytes 1076323456 | solution.py:84
  2130.5 12.9 pad.1466
  2572.6 12.9 pad.1466
  3014.7 12.9 pad.1466
  3456.7 12.9 pad.1466
  3898.8 12.9 pad.1466
  4340.8 12.9 pad.1466
  4782.9 12.9 pad.1466
  5345.2 18.8 multiply_reduce_fusion.10
  5414.3 16.5 fusion.27
  5430.9 30.8 reduce-scatter.21.cloned.1.call-done
  5463.2 99.7 %reduce-scatter.19.cloned.1.call-done = f32[96,96]{1,0:T(8,128)} async-done(((f32[3072,96]{1,0:T(8,128)}), f32[96,96]{1,0:T(8,128)}) %reduce-scatter.19.cloned.1.call-update) | async-done | bytes 36880
  5564.4 99.7 %reduce-scatter.15.cloned.1.call-done = f32[96,128]{1,0:T(8,128)} async-done(((f32[3072,128]{1,0:T(8,128)}), f32[96,128]{1,0:T(8,128)}) %reduce-scatter.15.cloned.1.call-update) | async-done | bytes 49168 | tf_op jit(solution)/shard_map/reduce_scatter | solution.py:188
  5665.5 210.9 %reduce-scatter.17.cloned.1.call-done = f32[96,1536]{1,0:T(8,128)} async-done(((f32[3072,1536]{1,0:T(8,128)}), f32[96,1536]{1,0:T(8,128)}) %reduce-scatter.17.cloned.1.call-update) | async-done | bytes 589840 | tf_op jit(solution)/shard_map/reduce_scatter | solution.py:191
  5878.2 267.2 %reduce-scatter.11.cloned.1.call-done = f32[1536,144]{0,1:T(8,128)} async-done(((f32[1536,4608]{0,1:T(8,128)}), f32[1536,144]{0,1:T(8,128)}) %reduce-scatter.11.cloned.1.call-update) | async-done | bytes 884752 | tf_op jit(solution)/shard_map/reduce_scatter | solution.py:186
  6147.4 353.0 %reduce-scatter.13.cloned.1.call-done = f32[1536,192]{0,1:T(8,128)} async-done(((f32[1536,6144]{0,1:T(8,128)}), f32[1536,192]{0,1:T(8,128)}) %reduce-scatter.13.cloned.1.call-update) | async-done | bytes 1179664 | tf_op jit(solution)/shard_map/reduce_scatter | solution.py:187
  6506.6 39.6 psum.7
  (3332 shorter events, 4966.3 us)
Async XLA Ops:
  7.2 139.3 %all-gather.5.cloned.1.call-start = ((), (), s32[]{:S(2)}) async-start(), calls=%async_computation.6 | async-start | bytes 14598144 | tf_op jit(solution)/shard_map/all_gather | solution.py:130
  9.3 242.9 %all-gather.7.cloned.1.call-start = ((), (), s32[]{:S(2)}) async-start(), calls=%async_computation.7 | async-start | bytes 19464192 | tf_op jit(solution)/shard_map/all_gather | solution.py:131
  11.6 324.3 %all-gather.9.cloned.1.call-start = ((), (), s32[]{:S(2)}) async-start(), calls=%async_computation.8 | async-start | bytes 9732096 | tf_op jit(solution)/shard_map/all_gather | solution.py:135
  12.5 5449.2 %reduce-scatter.21.cloned.1.call-start = ((), (), s32[]{:S(2)}) async-start(), calls=%async_computation.14 | async-start | bytes 1622016
  60.0 276.0 %copy-start.160 = (f32[256]{0:T(256)}, f32[256]{0:T(256)S(1)}, u32[]{:S(2)}) copy-start(f32[256]{0:T(256)S(1)} %and_convert_fusion) | copy-start | bytes 3076
  103.1 254.6 %copy-start.91 = (bf16[96,3072]{0,1:T(8,128)(2,1)}, bf16[96,3072]{0,1:T(8,128)(2,1)S(1)}, u32[]{:S(2)}) copy-start(bf16[96,3072]{0,1:T(8,128)(2,1)S(1)} %all_gather.26) | copy-start | bytes 1769476
  5365.9 197.0 %reduce-scatter.19.cloned.1.call-start = ((), (), s32[]{:S(2)}) async-start(), calls=%async_computation.13 | async-start | bytes 1622016
  5367.9 296.1 %reduce-scatter.15.cloned.1.call-start = ((), (), s32[]{:S(2)}) async-start(), calls=%async_computation.11 | async-start | bytes 1622016 | tf_op jit(solution)/shard_map/reduce_scatter | solution.py:188
  5371.8 504.5 %reduce-scatter.17.cloned.1.call-start = ((), (), s32[]{:S(2)}) async-start(), calls=%async_computation.12 | async-start | bytes 19464192 | tf_op jit(solution)/shard_map/reduce_scatter | solution.py:191
  5380.1 765.3 %reduce-scatter.11.cloned.1.call-start = ((), (), s32[]{:S(2)}) async-start(), calls=%async_computation.9 | async-start | bytes 29196288 | tf_op jit(solution)/shard_map/reduce_scatter | solution.py:186
  5413.6 1086.9 %reduce-scatter.13.cloned.1.call-start = ((), (), s32[]{:S(2)}) async-start(), calls=%async_computation.10 | async-start | bytes 38928384 | tf_op jit(solution)/shard_map/reduce_scatter | solution.py:187
  5430.7 1116.2 %copy-start.135 = (f32[23,96]{1,0:T(8,128)S(1)}, f32[23,96]{1,0:T(8,128)}, u32[]{:S(2)}) copy-start(f32[23,96]{1,0:T(8,128)} %param.54) | copy-start | bytes 26500
  5430.7 1116.2 %copy-start.145 = (f32[23,96]{1,0:T(8,128)S(1)}, f32[23,96]{1,0:T(8,128)}, u32[]{:S(2)}) copy-start(f32[23,96]{1,0:T(8,128)} %param.57) | copy-start | bytes 26500
  5430.7 1116.2 %copy-start.146 = (f32[23,96]{1,0:T(8,128)S(1)}, f32[23,96]{1,0:T(8,128)}, u32[]{:S(2)}) copy-start(f32[23,96]{1,0:T(8,128)} %param.56) | copy-start | bytes 26500
  5430.7 1116.3 %copy-start.147 = (f32[23,96]{1,0:T(8,128)S(1)}, f32[23,96]{1,0:T(8,128)}, u32[]{:S(2)}) copy-start(f32[23,96]{1,0:T(8,128)} %param.55) | copy-start | bytes 26500
  5430.7 1117.0 %copy-start.124 = (f32[96,96]{1,0:T(8,128)S(1)}, f32[96,96]{1,0:T(8,128)}, u32[]{:S(2)}) copy-start(f32[96,96]{1,0:T(8,128)} %param.50) | copy-start | bytes 110596
  5430.8 1116.9 %copy-start.136 = (f32[96,96]{1,0:T(8,128)S(1)}, f32[96,96]{1,0:T(8,128)}, u32[]{:S(2)}) copy-start(f32[96,96]{1,0:T(8,128)} %param.53) | copy-start | bytes 110596
  5430.8 1116.9 %copy-start.137 = (f32[96,96]{1,0:T(8,128)S(1)}, f32[96,96]{1,0:T(8,128)}, u32[]{:S(2)}) copy-start(f32[96,96]{1,0:T(8,128)} %param.52) | copy-start | bytes 110596
  5430.8 1116.9 %copy-start.138 = (f32[96,96]{1,0:T(8,128)S(1)}, f32[96,96]{1,0:T(8,128)}, u32[]{:S(2)}) copy-start(f32[96,96]{1,0:T(8,128)} %param.51) | copy-start | bytes 110596
  5430.8 1117.6 %copy-start.96 = (f32[96,1536]{1,0:T(8,128)S(1)}, f32[96,1536]{1,0:T(8,128)}, u32[]{:S(2)}) copy-start(f32[96,1536]{1,0:T(8,128)} %param.58) | copy-start | bytes 1769476
  5430.8 1117.6 %copy-start.113 = (f32[96,1536]{1,0:T(8,128)S(1)}, f32[96,1536]{1,0:T(8,128)}, u32[]{:S(2)}) copy-start(f32[96,1536]{1,0:T(8,128)} %param.61) | copy-start | bytes 1769476
  5430.8 1117.6 %copy-start.114 = (f32[96,1536]{1,0:T(8,128)S(1)}, f32[96,1536]{1,0:T(8,128)}, u32[]{:S(2)}) copy-start(f32[96,1536]{1,0:T(8,128)} %param.60) | copy-start | bytes 1769476
  5430.9 1117.6 %copy-start.115 = (f32[96,1536]{1,0:T(8,128)S(1)}, f32[96,1536]{1,0:T(8,128)}, u32[]{:S(2)}) copy-start(f32[96,1536]{1,0:T(8,128)} %param.59) | copy-start | bytes 1769476
  5876.3 672.1 %copy-start.97 = (f32[96,1536]{1,0:T(8,128)S(1)}, f32[96,1536]{1,0:T(8,128)}, u32[]{:S(2)}) copy-start(f32[96,1536]{1,0:T(8,128)} %reduce-scatter.17.cloned.1.call-done) | copy-start | bytes 1769476
  (880 other events, 9120.6 us)
Sparse Core Ops, SparseCore 0:
  11.6 112.1 all-gather.4
  127.2 124.9 all-gather.6
  255.7 80.2 all-gather.8
  5366.0 95.6 reduce-scatter.20
  5466.8 96.0 reduce-scatter.18
  5568.0 96.0 reduce-scatter.14
  5670.5 205.8 reduce-scatter.16
  5882.8 262.6 reduce-scatter.10
  6151.9 348.5 reduce-scatter.12
where the time goes:
time: 6620 us; the launch traced here: 6570 us
  local copies, waits for them, and re-layouts  3250 us (49%)
  other arithmetic  1750 us (26%)
  waiting for transfers between devices  1230 us (19%)
  blocking collectives  169 us (3%)
  matrix products  107 us (2%)
    pad x496, local copies, waits for them, and re-layouts, block(): lax.associative_scan(join, (decay, drive), axis=1)  2860 us
    mul x160, other arithmetic, join(): return (first[0] * second[0], second[0] * first[1] + second[1])  536 us
    reduce_scatter x1, waiting for transfers between devices, on_device(): lax.psum_scatter(grad_in, ('dp', 'fsdp'), scatter_dimension=1, tiled=True)  353 us
    add x128, other arithmetic, block(): lax.associative_scan(join, (decay, drive), axis=1)  318 us
    reduce_scatter x1, waiting for transfers between devices, on_device(): lax.psum_scatter(grad_ada, ('dp', 'fsdp'), scatter_dimension=1, tiled=True)  267 us
    concatenate x128, other arithmetic, block(): lax.associative_scan(join, (decay, drive), axis=1)  215 us
    reduce_scatter x1, waiting for transfers between devices, on_device(): lax.psum_scatter(grad_out, ('dp', 'fsdp'), scatter_dimension=0, tiled=True)  211 us
    add_any x40, other arithmetic, join(): return (first[0] * second[0], second[0] * first[1] + second[1])  182 us
  transfers between devices with their start and end apart: 9, of which 8 were waited for; matrix products, arithmetic and copies ran while one was open for 1% of the time, Pallas kernels for 0%

commit v1 on v0

v1 whole, which is shorter than its diff:
```python
import math

import jax
import jax.numpy as jnp
from jax import lax
from jax.experimental import pallas as pl
from jax.experimental.pallas import tpu as pltpu
from jax.sharding import PartitionSpec as P

D = 1536
E = 3072
N = 16
R = 96
CONV = 4
ITEM = 256
STEP = 10
SUB = 8
LANE = 128
ALL = ("dp", "fsdp")
LOG2E = math.log2(math.e)
LN2 = math.log(2.0)
F32 = jnp.float32
BF = jnp.bfloat16
VMEM_LIMIT = 40 * 1024 * 1024
SCAN_BLOCK = 64


def softplus(v):
    return jnp.maximum(v, 0.0) + jnp.log1p(jnp.exp(-jnp.abs(v)))


def scan_forward_body(u_ref, dtp_ref, bc_ref, rate_ref, row_ref, y_ref, states_ref, carry, parts):
    groups = u_ref.shape[0] // SUB
    chunks = u_ref.shape[1] // LANE

    @pl.when(pl.program_id(1) == 0)
    def _():
        carry[...] = jnp.zeros_like(carry)

    def group(g, _):
        base = pl.multiple_of(g * SUB, SUB)
        u8 = u_ref[pl.ds(base, SUB), :]
        step8 = softplus(dtp_ref[pl.ds(base, SUB), :] + row_ref[0:1, :])
        drive8 = step8 * u8
        bc = bc_ref[g]
        states = [carry[:, c * LANE : (c + 1) * LANE] for c in range(chunks)]
        for j in range(SUB):
            b = jnp.broadcast_to(bc[:N, j : j + 1], (N, LANE))
            cc = jnp.broadcast_to(bc[N:, j : j + 1], (N, LANE))
            at = pl.multiple_of((base + j) * N, N)
            for c in range(chunks):
                lanes = slice(c * LANE, (c + 1) * LANE)
                step = jnp.broadcast_to(step8[j : j + 1, lanes], (N, LANE))
                drive = jnp.broadcast_to(drive8[j : j + 1, lanes], (N, LANE))
                s = jnp.exp2(step * rate_ref[:, lanes]) * states[c] + b * drive
                states[c] = s
                states_ref[pl.ds(at, N), lanes] = s
                p = cc * s
                parts[c, j * SUB : (j + 1) * SUB, :] = p[:SUB] + p[SUB:]
        for c in range(chunks):
            lanes = slice(c * LANE, (c + 1) * LANE)
            carry[:, lanes] = states[c]
            total = row_ref[1:2, lanes] * u8[:, lanes]
            for n in range(SUB):
                total = total + parts[c, pl.ds(n, SUB, stride=SUB), :]
            y_ref[pl.ds(base, SUB), lanes] = total
        return 0

    lax.fori_loop(0, groups, group, 0)


def scan_forward(u, dtp, bc, rate, rows, item, block=SCAN_BLOCK):
    total, width = u.shape
    items = total // item
    steps = item // block
    chunks = width // LANE
    tok = pl.BlockSpec((block, width), lambda i, t: (i * steps + t, 0))
    whole = lambda r: pl.BlockSpec((r, width), lambda i, t: (0, 0))
    return pl.pallas_call(
        scan_forward_body,
        grid=(items, steps),
        in_specs=[tok, tok, pl.BlockSpec((block // SUB, 2 * N, SUB), lambda i, t: (i * steps + t, 0, 0)), whole(N), whole(2)],
        out_specs=[tok, pl.BlockSpec((block * N, width), lambda i, t: (i * steps + t, 0))],
        out_shape=[jax.ShapeDtypeStruct((total, width), F32), jax.ShapeDtypeStruct((total * N, width), F32)],
        scratch_shapes=[pltpu.VMEM((N, width), F32), pltpu.VMEM((chunks, SUB * SUB, LANE), F32)],
        compiler_params=pltpu.CompilerParams(vmem_limit_bytes=VMEM_LIMIT),
        cost_estimate=pl.CostEstimate(flops=8*total*N*width, bytes_accessed=4*total*width*(N+3), transcendentals=total*N*width),
        name="scan_forward",
    )(u, dtp, bc, rate, rows)


def scan_backward_body(u_ref, dtp_ref, dy_ref, bc_ref, states_ref, before_ref, rate_ref, row_ref,
                       du_ref, ddtp_ref, dbc_ref, drate_ref, drow_ref, carry, parts, parts2, sums):
    groups = u_ref.shape[0] // SUB
    chunks = u_ref.shape[1] // LANE
    first = pl.program_id(1) == pl.num_programs(1) - 1

    @pl.when(pl.program_id(1) == 0)
    def _():
        carry[...] = jnp.zeros_like(carry)

    @pl.when((pl.program_id(0) == 0) & (pl.program_id(1) == 0))
    def _():
        drate_ref[...] = jnp.zeros_like(drate_ref)
        drow_ref[...] = jnp.zeros_like(drow_ref)

    def group(k, _):
        g = groups - 1 - k
        base = pl.multiple_of(g * SUB, SUB)
        u8 = u_ref[pl.ds(base, SUB), :]
        pre8 = dtp_ref[pl.ds(base, SUB), :] + row_ref[0:1, :]
        step8 = softplus(pre8)
        drive8 = step8 * u8
        dy8 = dy_ref[pl.ds(base, SUB), :]
        bc = bc_ref[g]
        grads = [carry[:, c * LANE : (c + 1) * LANE] for c in range(chunks)]
        drate = [drate_ref[:, c * LANE : (c + 1) * LANE] for c in range(chunks)]
        for j in reversed(range(SUB)):
            b = jnp.broadcast_to(bc[:N, j : j + 1], (N, LANE))
            cc = jnp.broadcast_to(bc[N:, j : j + 1], (N, LANE))
            at = pl.multiple_of((base + j) * N, N)
            db = jnp.zeros((N, LANE), F32)
            dc = jnp.zeros((N, LANE), F32)
            for c in range(chunks):
                lanes = slice(c * LANE, (c + 1) * LANE)
                step = jnp.broadcast_to(step8[j : j + 1, lanes], (N, LANE))
                drive = jnp.broadcast_to(drive8[j : j + 1, lanes], (N, LANE))
                dy = jnp.broadcast_to(dy8[j : j + 1, lanes], (N, LANE))
                now = states_ref[pl.ds(at, N), lanes]
                if j > 0:
                    prev = states_ref[pl.ds(at - N, N), lanes]
                else:
                    prev = states_ref[pl.ds(pl.multiple_of(jnp.maximum(at - N, 0), N), N), lanes]
                    edge = jnp.where(first, 0.0, before_ref[:, lanes])
                    prev = jnp.where(g == 0, edge, prev)
                rate = rate_ref[:, lanes]
                grad = cc * dy + grads[c]
                dc = dc + now * dy
                db = db + grad * drive
                p = grad * b
                parts[c, j * SUB : (j + 1) * SUB, :] = p[:SUB] + p[SUB:]
                grad = grad * jnp.exp2(step * rate)
                grads[c] = grad
                q = grad * prev
                p = q * rate
                parts2[c, j * SUB : (j + 1) * SUB, :] = p[:SUB] + p[SUB:]
                drate[c] = drate[c] + q * step
            sums[pl.ds(at, N), :] = db
            sums[pl.ds(pl.multiple_of(groups * SUB * N + at, N), N), :] = dc
        for c in range(chunks):
            lanes = slice(c * LANE, (c + 1) * LANE)
            carry[:, lanes] = grads[c]
            drate_ref[:, lanes] = drate[c]
            x = parts[c, pl.ds(0, SUB, stride=SUB), :]
            r = parts2[c, pl.ds(0, SUB, stride=SUB), :]
            for n in range(1, SUB):
                x = x + parts[c, pl.ds(n, SUB, stride=SUB), :]
                r = r + parts2[c, pl.ds(n, SUB, stride=SUB), :]
            dy = dy8[:, lanes]
            u = u8[:, lanes]
            du_ref[pl.ds(base, SUB), lanes] = step8[:, lanes] * x + row_ref[1:2, lanes] * dy
            ddtp = (u * x + LN2 * r) * jax.nn.sigmoid(pre8[:, lanes])
            ddtp_ref[pl.ds(base, SUB), lanes] = ddtp
            drow_ref[:SUB, lanes] += ddtp
            drow_ref[SUB:, lanes] += dy * u
        return 0

    lax.fori_loop(0, groups, group, 0)
    dbc_ref[...] = lax.dot_general(jnp.ones((SUB, LANE), F32), sums[...], (((1,), (1,)), ((), ())),
                                   precision=lax.Precision.HIGHEST, preferred_element_type=F32)


def scan_backward(u, dtp, dy, bc, states, rate, rows, item, block=SCAN_BLOCK):
    total, width = u.shape
    items = total // item
    steps = item // block
    chunks = width // LANE
    at = lambda i, t: i * steps + steps - 1 - t
    tok = pl.BlockSpec((block, width), lambda i, t: (at(i, t), 0))
    whole = lambda r: pl.BlockSpec((r, width), lambda i, t: (0, 0))
    return pl.pallas_call(
        scan_backward_body,
        grid=(items, steps),
        in_specs=[tok, tok, tok, pl.BlockSpec((block // SUB, 2 * N, SUB), lambda i, t: (at(i, t), 0, 0)),
                  pl.BlockSpec((block * N, width), lambda i, t: (at(i, t), 0)),
                  pl.BlockSpec((N, width), lambda i, t: (jnp.maximum(at(i, t) * block - 1, 0), 0)),
                  whole(N), whole(2)],
        out_specs=[tok, tok, pl.BlockSpec((SUB, 2 * block * N), lambda i, t: (0, at(i, t))), whole(N), whole(2 * SUB)],
        out_shape=[jax.ShapeDtypeStruct((total, width), F32), jax.ShapeDtypeStruct((total, width), F32),
                   jax.ShapeDtypeStruct((SUB, 2 * total * N), F32), jax.ShapeDtypeStruct((N, width), F32), jax.ShapeDtypeStruct((2 * SUB, width), F32)],
        scratch_shapes=[pltpu.VMEM((N, width), F32), pltpu.VMEM((chunks, SUB * SUB, LANE), F32), pltpu.VMEM((chunks, SUB * SUB, LANE), F32),
                        pltpu.VMEM((2 * block * N, LANE), F32)],
        compiler_params=pltpu.CompilerParams(vmem_limit_bytes=VMEM_LIMIT),
        cost_estimate=pl.CostEstimate(flops=16*total*N*width, bytes_accessed=4*total*width*(N+5), transcendentals=total*N*width),
        name="scan_backward",
    )(u, dtp, dy, bc, states, states, rate, rows)


def product(left, right):
    return jnp.dot(left, right, preferred_element_type=F32)


def left_outer(left, right):
    return lax.dot_general(left, right, (((0,), (0,)), ((), ())), preferred_element_type=F32)


def right_inner(left, right):
    return lax.dot_general(left, right, (((1,), (1,)), ((), ())), preferred_element_type=F32)


def embed_time(steps):
    half = D // 2
    freqs = jnp.exp(-math.log(10000.0) * jnp.arange(half, dtype=F32) / half)
    angles = steps.astype(F32)[:, None] * freqs[None, :]
    return jax.nn.silu(jnp.concatenate([jnp.cos(angles), jnp.sin(angles)], axis=1))


def normalize(x):
    mean = jnp.mean(x, axis=2, keepdims=True)
    centered = x - mean
    var = jnp.mean(centered * centered, axis=2, keepdims=True)
    scale = lax.rsqrt(var + 1e-06)
    return centered * scale, scale


def group_bits(size):
    return [1 << k for k in reversed(range(size.bit_length() - 1))]


def swap(v, bit, size):
    return lax.ppermute(v, "fsdp", [(i, i ^ bit) for i in range(size)])


def group_gather(v, size):
    for bit in group_bits(size):
        v = jnp.concatenate([v, swap(v, bit, size)], axis=0)
    return v


def group_scatter(v, size):
    for bit in reversed(group_bits(size)):
        half = v.shape[0] // 2
        v = v[:half] + swap(v[half:].astype(BF), bit, size).astype(F32)
    return v


def group_sum(v, size):
    count = v.shape[0]
    for k, bit in enumerate(group_bits(size)):
        other = swap(v, bit, size)
        span = 1 << k
        other = jnp.flip(other.reshape((count // (2 * span), 2, span) + v.shape[1:]), 1).reshape(v.shape)
        v = v + other
    return v


def exchange(v):
    return lax.all_to_all(v, ALL, 0, 0, tiled=True)


def on_device(sizes, *args):
    (
        act, cotangent, item_counts, item_lengths, time_steps,
        ada_weight, ada_first, ada_second, ada_average,
        in_weight, in_first, in_second, in_average,
        x_weight, x_first, x_second, x_average,
        dt_weight, dt_first, dt_second, dt_average,
        chan_table, chan_first, chan_second, chan_average,
        out_weight, out_first, out_second, out_average,
    ) = args
    n_dp, n_fsdp = sizes
    devices = n_dp * n_fsdp
    count = item_lengths.shape[0]
    items = count * n_fsdp
    tokens = items * ITEM
    width = E // n_fsdp
    ada_cols = ada_weight.shape[1]
    f = lax.axis_index("fsdp")
    d = lax.axis_index("dp")
    offsets = [0]
    for bit in group_bits(n_fsdp):
        offsets = offsets + [o ^ bit for o in offsets]

    rows = jnp.concatenate(
        [out_weight.astype(BF), x_weight.astype(BF), dt_weight.astype(BF).T, chan_table.astype(BF).T], axis=1
    )
    used = rows.shape[1]
    rows = jnp.pad(rows, ((0, 0), (0, -used % LANE)))
    forth = []
    for b in range(devices):
        i, j = divmod(b, 2)
        k, g = divmod(i, n_fsdp)
        forth.append((b, (2 * k + j) * n_fsdp + g))
    in_full = lax.all_gather(in_weight.astype(BF).T, "dp", axis=0, tiled=True)
    rows_full = lax.all_gather(lax.ppermute(rows, ALL, forth), "dp", axis=0, tiled=True)
    out_full = rows_full[:, :D]
    x_full = rows_full[:, D : D + R + 2 * N]
    dt_full = rows_full[:, D + R + 2 * N : D + 2 * R + 2 * N]
    chan = rows_full[:, D + 2 * R + 2 * N : used].astype(F32).T

    live_items = jnp.arange(count, dtype=jnp.int32) < item_counts[0]
    live_rows = jnp.arange(ITEM, dtype=jnp.int32)[None, :] < item_lengths[:, None]
    live = live_items[:, None] & live_rows
    dfinal_own = jnp.where(live[..., None], cotangent.reshape(count, ITEM, D), jnp.zeros((), BF))
    x_all = group_gather(act.reshape(count, ITEM, D), n_fsdp)
    dfinal_all = group_gather(dfinal_own, n_fsdp)

    steps_all = exchange(jnp.broadcast_to(time_steps[None], (devices, count))).reshape(-1)
    cond_all = embed_time(steps_all).astype(BF)
    mod_cols = product(cond_all, ada_weight.astype(BF)).reshape(n_dp, 1, items, ada_cols)
    mod_cols = jnp.broadcast_to(mod_cols, (n_dp, n_fsdp, items, ada_cols)).reshape(devices, items, ada_cols)
    mod = jnp.swapaxes(exchange(mod_cols), 0, 1).reshape(n_fsdp, count, 3 * D)
    mod = jnp.take(mod, jnp.array(offsets, jnp.int32) ^ f, axis=0).reshape(items, 1, 3 * D)
    shift, scale, gate = mod[..., :D], mod[..., D : 2 * D], mod[..., 2 * D :]

    normed, _ = normalize(x_all.astype(F32))
    h_low = (normed * (1.0 + scale) + shift).astype(BF).reshape(tokens, D)
    do_low = (gate * dfinal_all.astype(F32)).astype(BF).reshape(tokens, D)

    xz = right_inner(h_low, in_full)
    xs = xz[:, :width].reshape(items, ITEM, width)
    z = xz[:, width:]
    xs_pad = jnp.pad(xs, ((0, 0), (CONV - 1, 0), (0, 0)))
    pre = chan[CONV]
    for k in range(CONV):
        pre = pre + xs_pad[:, k : k + ITEM, :] * chan[k]
    u = jax.nn.silu(pre).reshape(tokens, width)
    u_low = u.astype(BF)
    proj = group_sum(product(u_low, x_full).reshape(n_fsdp, count * ITEM, R + 2 * N), n_fsdp).reshape(tokens, R + 2 * N)
    rank_low = proj[:, :R].astype(BF)
    dtp = right_inner(rank_low, dt_full)
    a_neg = -jnp.exp(chan[CONV + 3 :])
    rate = a_neg * LOG2E
    pair = chan[CONV + 1 : CONV + 3]
    bc = jnp.swapaxes(proj[:, R:].reshape(tokens // SUB, SUB, 2 * N), 1, 2)
    y, states = scan_forward(u, dtp, bc, rate, pair, ITEM)

    dyg = right_inner(do_low, out_full)
    z_sig = jax.nn.sigmoid(z)
    z_act = z * z_sig
    mixed_low = (y * z_act).astype(BF)
    dy = dyg * z_act
    dz_low = (dyg * y * (z_sig + z_act * (1.0 - z_sig))).astype(BF)
    o_own = group_scatter(product(mixed_low, out_full).reshape(items, ITEM, D), n_fsdp)
    grad_out = left_outer(mixed_low, do_low).astype(BF)

    du_scan, ddtp, dbc, drate, drow = scan_backward(u, dtp, dy, bc, states, rate, pair, ITEM)
    ddtp_low = ddtp.astype(BF)
    dbc = jnp.swapaxes(dbc[0].reshape(-1, 2, SCAN_BLOCK, N), 1, 2).reshape(tokens, 2 * N)
    drank = product(ddtp_low, dt_full)
    dproj = group_sum(jnp.concatenate([drank, dbc], axis=1).reshape(n_fsdp, count * ITEM, R + 2 * N), n_fsdp)
    dproj_low = dproj.reshape(tokens, R + 2 * N).astype(BF)
    grad_dt = left_outer(ddtp_low, rank_low)
    grad_x = left_outer(u_low, dproj_low)
    du = (du_scan + right_inner(dproj_low, x_full)).reshape(items, ITEM, width)
    sig = jax.nn.sigmoid(pre)
    dpre = du * (sig + pre * sig * (1.0 - sig))
    dpre_pad = jnp.pad(dpre, ((0, 0), (0, CONV - 1), (0, 0)))
    dxs = dpre_pad[:, CONV - 1 :] * chan[0]
    for k in range(1, CONV):
        dxs = dxs + dpre_pad[:, CONV - 1 - k : CONV - 1 - k + ITEM] * chan[k]
    grad_taps = [jnp.sum(dpre * xs_pad[:, k : k + ITEM], axis=(0, 1)) for k in range(CONV)]
    grad_bias = jnp.sum(dpre, axis=(0, 1))
    dxz_low = jnp.concatenate([dxs.reshape(tokens, width).astype(BF), dz_low], axis=1)
    grad_in = left_outer(dxz_low, h_low).astype(BF)
    grad_chan = jnp.concatenate(
        [
            jnp.stack(grad_taps + [grad_bias, jnp.sum(drow[:SUB], axis=0), jnp.sum(drow[SUB:], axis=0)]),
            drate * a_neg,
        ],
        axis=0,
    )
    small = jnp.concatenate([grad_x, grad_dt, grad_chan.T], axis=1)
    small = jnp.pad(small, ((0, 0), (0, -small.shape[1] % LANE))).astype(BF)

    back = [(t, s) for s, t in forth]
    out_share = lax.ppermute(lax.psum_scatter(grad_out, "dp", scatter_dimension=0, tiled=True), ALL, back).astype(F32)
    in_share = lax.psum_scatter(grad_in, "dp", scatter_dimension=0, tiled=True).astype(F32).T
    small = lax.ppermute(lax.psum_scatter(small, "dp", scatter_dimension=0, tiled=True), ALL, back).astype(F32)
    x_share = small[:, : R + 2 * N]
    dt_share = small[:, R + 2 * N : 2 * R + 2 * N].T
    chan_share = small[:, 2 * R + 2 * N : 2 * R + 2 * N + chan_table.shape[0]].T

    dh = group_scatter(product(dxz_low, in_full).reshape(items, ITEM, D), n_fsdp)
    x = act.astype(F32).reshape(count, ITEM, D)
    normed, inverse = normalize(x)
    dfinal = dfinal_own.astype(F32)
    final = x + gate[:count] * o_own
    dmod = jnp.concatenate(
        [jnp.sum(dh, axis=1), jnp.sum(dh * normed, axis=1), jnp.sum(dfinal * o_own, axis=1)], axis=1
    ).astype(BF)
    dn = dh * (1.0 + scale[:count])
    act_grad = dfinal + inverse * (
        dn - jnp.mean(dn, axis=2, keepdims=True) - normed * jnp.mean(dn * normed, axis=2, keepdims=True)
    )
    dmod_all = exchange(jnp.swapaxes(dmod.reshape(count, devices, ada_cols), 0, 1)).reshape(devices * count, ada_cols)
    ada_share = left_outer(cond_all, dmod_all)

    shares = (ada_share, in_share, x_share, dt_share, chan_share, out_share)
    local = F32(0.0)
    for g in shares:
        local = local + jnp.sum(g * g)
    total = jnp.sum(exchange(jnp.broadcast_to(local, (devices, LANE)))[:, 0])
    grad_norm = jnp.sqrt(total)
    factor = jnp.minimum(1.0, 1.0 / (grad_norm + 1e-06))
    ema_keep = min(0.9999, (1.0 + STEP) / (10.0 + STEP))
    states = (
        (ada_weight, ada_first, ada_second, ada_average),
        (in_weight, in_first, in_second, in_average),
        (x_weight, x_first, x_second, x_average),
        (dt_weight, dt_first, dt_second, dt_average),
        (chan_table, chan_first, chan_second, chan_average),
        (out_weight, out_first, out_second, out_average),
    )
    settings = ((0.03, 0.1), (0.03, 0.1), (0.03, 0.1), (0.03, 0.1), (0.5, 0.0), (0.03, 0.1))
    results = []
    for (weight, first, second, average), g, (learn_rate, weight_decay) in zip(states, shares, settings):
        clipped = g * factor
        first = 0.9 * first + 0.1 * clipped
        second = 0.999 * second + 0.001 * clipped * clipped
        first_hat = first / (1.0 - 0.9**STEP)
        second_hat = second / (1.0 - 0.999**STEP)
        weight = weight - learn_rate * (
            first_hat / (jnp.sqrt(second_hat) + 1e-08) + weight_decay * weight
        )
        average = ema_keep * average + (1.0 - ema_keep) * weight
        results.extend([first, second, weight, average])
    return (final.reshape(count * ITEM, D), act_grad.reshape(count * ITEM, D), grad_norm, *results)


def solution(mesh):
    sizes = (mesh.shape["dp"], mesh.shape["fsdp"])
    first, second = P(ALL, None), P(None, ALL)
    weights = [second] * 8 + [first] * 4 + [second] * 8 + [first] * 4
    return jax.shard_map(
        lambda *args: on_device(sizes, *args),
        mesh=mesh,
        in_specs=(first, first, P(ALL), P(ALL), P(ALL), *weights),
        out_specs=(first, first, P(), *weights),
        check_vma=False,
    )
```

time: 6620 us -> 703 us (0.11)
  local copies, waits for them, and re-layouts: 3250 us -> 73.2 us
  other arithmetic: 1750 us -> 59.7 us
  waiting for transfers between devices: 1230 us -> 357 us
  blocking collectives: 169 us -> 0 us
  Pallas kernels: 0 us -> 88.4 us
    pad x496 -> x2, local copies, waits for them, and re-layouts: 2860 us -> 0.84 us  [the longest x1 0.81 us: on_device(): small = jnp.pad(small, ((0, 0), (0, -small.shape[1] % LANE))).astype(BF)]
    reduce_scatter x4 -> x3, waiting for transfers between devices: 931 us -> 177 us  [the longest x1 93.1 us: on_device(): lax.psum_scatter(grad_in, 'dp', scatter_dimension=0, tiled=True).astype(F32)]
    mul x201 -> x3, other arithmetic: 588 us -> 3.46 us  [the longest x1 2.82 us: on_device(): u = jax.nn.silu(pre).reshape(tokens, width)]
    add x161 -> x6, other arithmetic: 336 us -> 4.52 us  [the longest x3 3.44 us: group_sum(): v = v + other]
    reduce_sum x36 -> x9, other arithmetic: 308 us -> 14.1 us  [the longest x1 5.93 us: on_device(): grad_bias = jnp.sum(dpre, axis=(0, 1))]
    add_any x112 -> x0, other arithmetic: 216 us -> none  [the longest x40 182 us: join(): return (first[0] * second[0], second[0] * first[1] + second[1])]
    concatenate x128 -> x4, other arithmetic: 215 us -> 0.38 us  [the longest x2 0.29 us: group_gather(): v = jnp.concatenate([v, swap(v, bit, size)], axis=0)]
    while x1480 -> x0, local copies, waits for them, and re-layouts: 160 us -> none
  transfers between devices with their start and end apart: 9 -> 24, of which waited for: 8 -> 16; matrix products, arithmetic and copies ran while one was open for 1% -> 9% of each run, Pallas kernels for 0% -> 0%
where the time goes in v1:
time: 703 us; the launch traced here: 694 us
  waiting for transfers between devices  357 us (51%)
  Pallas kernels  88.4 us (13%)
  local copies, waits for them, and re-layouts  73.2 us (10%)
  other arithmetic  59.7 us (8%)
  matrix products  47.4 us (7%)
  starting transfers between devices  44.2 us (6%)
  between operations  23.2 us (3%)
    reduce_scatter x1, waiting for transfers between devices, on_device(): lax.psum_scatter(grad_in, 'dp', scatter_dimension=0, tiled=True).astype(F32)  93.1 us
    all_gather x1, waiting for transfers between devices, on_device(): in_full = lax.all_gather(in_weight.astype(BF).T, 'dp', axis=0, tiled=True)  80 us
    ppermute x12, waiting for transfers between devices, swap(): return lax.ppermute(v, 'fsdp', [(i, i ^ bit) for i in range(size)])  62.6 us
    pallas_call x1, Pallas kernels, scan_backward(): pl.pallas_call(scan_backward_body, grid=(items, steps), in_specs=[tok, to...  61.3 us
    reduce_scatter x1, waiting for transfers between devices, on_device(): lax.psum_scatter(grad_out, 'dp', scatter_dimension=0, tiled=True)  56.2 us
    unnamed x179, local copies, waits for them, and re-layouts  28.1 us
    reduce_scatter x1, waiting for transfers between devices, on_device(): lax.psum_scatter(small, 'dp', scatter_dimension=0, tiled=True)  27.7 us
    pallas_call x1, Pallas kernels, scan_forward(): pl.pallas_call(scan_forward_body, grid=(items, steps), in_specs=[tok, tok...  27 us
  transfers between devices with their start and end apart: 24, of which 16 were waited for; matrix products, arithmetic and copies ran while one was open for 9% of the time, Pallas kernels for 0%

profile of v1, /device:TPU:0, one launch (start us, length us, event | category | flops | bytes accessed | tf_op | source)
XLA Modules:
  0.0 693.5 jit_solution(6304408800065496520)
XLA Ops:
  15.0 12.4 %collective-permute-start.1 = (bf16[1,256,1536]{2,1,0:T(8,128)(2,1)S(1)}, bf16[1,256,1536]{2,1,0:T(8,128)(2,1)S(1)}, u32[]{:S(2)}, u32[]{:S(2)}) collective-permute-start(bf16[1,256,1536]{2,1,0:T(8,128)(2,1)S(1)} %bitcast.182), channel_id=1, source_target_pairs={{0,2},{1,3},{2,0},{3,1},{4,6},{5,7},{6,4},{7,5},{8,10},{9,11},{10,... | collective-permute-start | bytes 2359304 | tf_op jit(solution)/shard_map/ppermute | solution.py:231
  32.7 11.4 %all-to-all-done = s32[32,1,1]{2,1,0:T(1,128)S(1)} async-done(((s32[32,1,1]{2,1,0:T(1,128)}), s32[32,1,1]{2,1,0:T(1,128)S(1)}, u32[]{:S(2)}, u32[]{:S(2)}) %all-to-all-start) | async-done | bytes 160 | tf_op jit(solution)/shard_map/all_to_all | solution.py:258
  45.8 5.1 all-to-all-start.1
  51.0 8.1 %all-to-all-done.1 = f32[32,4,144]{2,1,0:T(4,128)S(1)} async-done(((f32[32,4,144]{2,1,0:T(4,128)}), f32[32,4,144]{2,1,0:T(4,128)S(1)}, u32[]{:S(2)}, u32[]{:S(2)}) %all-to-all-start.1) | async-done | bytes 73760 | tf_op jit(solution)/shard_map/all_to_all | solution.py:258
  67.7 14.4 %all-gather.3.cloned.1.call-done = bf16[768,1792]{1,0:T(8,128)(2,1)} async-done(((bf16[96,1792]{1,0:T(8,128)(2,1)}), bf16[768,1792]{1,0:T(8,128)(2,1)}) %all-gather.3.cloned.1.call-update) | async-done | bytes 2752528 | tf_op jit(solution)/shard_map/all_gather | solution.py:295
  83.3 80.0 %all-gather.5.cloned.1.call-done = bf16[1536,1536]{1,0:T(8,128)(2,1)} async-done(((bf16[192,1536]{1,0:T(8,128)(2,1)}), bf16[1536,1536]{1,0:T(8,128)(2,1)}) %all-gather.5.cloned.1.call-update) | async-done | bytes 4718608 | tf_op jit(solution)/shard_map/all_gather | solution.py:294
  163.3 7.0 %fusion.84 = f32[1024,1536]{1,0:T(8,128)S(1)} fusion(bf16[1024,1536]{1,0:T(8,128)(2,1)S(1)} %fusion, bf16[1536,1536]{1,0:T(8,128)(2,1)} %all-gather.5.cloned.1.call-done), kind=kOutput, calls=%fused_computation.197 | convolution fusion | flops 4831838208 | bytes 14155776 | tf_op jit(solution)/shard_map/dot_general | solution.py:208
  179.5 11.2 %collective-permute-done.3 = f32[4,256,128]{2,1,0:T(8,128)S(1)} collective-permute-done((f32[4,256,128]{2,1,0:T(8,128)S(1)}, f32[4,256,128]{2,1,0:T(8,128)S(1)}, u32[]{:S(2)}, u32[]{:S(2)}) %collective-permute-start.3) | collective-permute-done | bytes 524320 | tf_op jit(solution)/shard_map/ppermute | solution.py:231
  204.3 27.0 %scan_forward.1 = (f32[1024,768]{1,0:T(8,128)S(1)}, f32[16384,768]{1,0:T(8,128)}) custom-call(f32[1024,768]{1,0:T(8,128)S(1)} %bitcast.178, f32[1024,768]{1,0:T(8,128)S(1)} %fusion.50.dtp_ref, f32[128,32,8]{2,1,0:T(8,128)S(1)} %bitcast.180, f32[16,768]{1,0:T(8,128)S(1)} %fusion.60.rate_ref, f32[2,768]{1,0:T(2,128)S(1)} %slice.208.row_ref), custom_call_target="tpu_custom_call" | custom-call | flops 100663296 | bytes 59768832 | tf_op jit(solution)/shard_map/scan_forward/pallas_call | solution.py:79
  242.9 17.0 %collective-permute-done.6 = bf16[1,256,1536]{2,1,0:T(8,128)(2,1)S(1)} collective-permute-done((bf16[1,256,1536]{2,1,0:T(8,128)(2,1)S(1)}, bf16[1,256,1536]{2,1,0:T(8,128)(2,1)S(1)}, u32[]{:S(2)}, u32[]{:S(2)}) %collective-permute-start.6) | collective-permute-done | bytes 786464 | tf_op jit(solution)/shard_map/ppermute | solution.py:231
  263.7 17.5 %collective-permute-done.7 = bf16[1,256,1536]{2,1,0:T(8,128)(2,1)S(1)} collective-permute-done((bf16[1,256,1536]{2,1,0:T(8,128)(2,1)S(1)}, bf16[1,256,1536]{2,1,0:T(8,128)(2,1)S(1)}, u32[]{:S(2)}, u32[]{:S(2)}) %collective-permute-start.7) | collective-permute-done | bytes 786464 | tf_op jit(solution)/shard_map/ppermute | solution.py:231
  285.6 4.8 fusion.31
  290.4 61.3 %scan_backward.1 = (f32[1024,768]{1,0:T(8,128)S(1)}, f32[1024,768]{1,0:T(8,128)S(1)}, f32[8,32768]{1,0:T(8,128)S(1)}, f32[16,768]{1,0:T(8,128)S(1)}, f32[16,768]{1,0:T(8,128)S(1)}) custom-call(f32[1024,768]{1,0:T(8,128)S(1)} %bitcast.179, f32[1024,768]{1,0:T(8,128)} %copy-done, f32[1024,768]{1,0:T(8,128)} %get-tuple-element.282.dy_ref, ...), custom_call_target="tpu_custom_call" | custom-call | flops 201326592 | bytes 66060288 | tf_op jit(solution)/shard_map/scan_backward/pallas_call | solution.py:181
  374.9 6.1 collective-permute-done.9
  406.7 5.9 fusion.73
  414.5 6.6 convolution_convert_fusion.1
  423.8 7.1 %convolution_convert_fusion = bf16[1536,1536]{1,0:T(8,128)(2,1)} fusion(bf16[1024,1536]{1,0:T(8,128)(2,1)S(1)} %copy-done.27, bf16[1024,768]{1,0:T(8,128)(2,1)S(1)} %copy-done.75, bf16[1024,768]{1,0:T(8,128)(2,1)S(1)} %bitcast.202), kind=kOutput, calls=%fused_computation.1 | convolution fusion | flops 4840488960 | bytes 11010048 | tf_op jit(solution)/shard_map/dot_general | solution.py:204
  432.7 6.9 fusion.8
  447.7 27.7 %reduce-scatter.10.cloned.1.call-done = bf16[96,256]{1,0:T(8,128)(2,1)} async-done(((bf16[768,256]{1,0:T(8,128)(2,1)}), bf16[96,256]{1,0:T(8,128)(2,1)}) %reduce-scatter.10.cloned.1.call-update) | async-done | bytes 49168 | tf_op jit(solution)/shard_map/reduce_scatter | solution.py:379
  487.3 4.0 all-to-all-start.2
  491.3 56.2 %reduce-scatter.8.cloned.1.call-done = bf16[96,1536]{1,0:T(8,128)(2,1)} async-done(((bf16[768,1536]{1,0:T(8,128)(2,1)}), bf16[96,1536]{1,0:T(8,128)(2,1)}) %reduce-scatter.8.cloned.1.call-update) | async-done | bytes 294928 | tf_op jit(solution)/shard_map/reduce_scatter | solution.py:377
  552.3 93.1 %reduce-scatter.6.cloned.1.call-done = bf16[192,1536]{1,0:T(8,128)(2,1)} async-done(((bf16[1536,1536]{1,0:T(8,128)(2,1)}), bf16[192,1536]{1,0:T(8,128)(2,1)}) %reduce-scatter.6.cloned.1.call-update) | async-done | bytes 589840 | tf_op jit(solution)/shard_map/reduce_scatter | solution.py:378
  651.8 4.8 all-to-all-start.3
  674.9 4.5 multiply_add_fusion.2
  (340 shorter events, 170.2 us)
Async XLA Ops:
  7.2 74.8 %all-gather.3.cloned.1.call-start = ((), (), s32[]{:S(2)}) async-start(), calls=%async_computation.7 | async-start | bytes 3096576 | tf_op jit(solution)/shard_map/all_gather | solution.py:295
  12.6 0.7 collective-permute-start
  14.1 149.2 %all-gather.5.cloned.1.call-start = ((), (), s32[]{:S(2)}) async-start(), calls=%async_computation.8 | async-start | bytes 5308416 | tf_op jit(solution)/shard_map/all_gather | solution.py:294
  15.0 44.9 %collective-permute-start.1 = (bf16[1,256,1536]{2,1,0:T(8,128)(2,1)S(1)}, bf16[1,256,1536]{2,1,0:T(8,128)(2,1)S(1)}, u32[]{:S(2)}, u32[]{:S(2)}) collective-permute-start(bf16[1,256,1536]{2,1,0:T(8,128)(2,1)S(1)} %bitcast.182), channel_id=1, source_target_pairs={{0,2},{1,3},{2,0},{3,1},{4,6},{5,7},{6,4},{7,5},{8,10},{9,11},{10,... | collective-permute-start | bytes 2359304 | tf_op jit(solution)/shard_map/ppermute | solution.py:231
  28.7 15.4 %all-to-all-start = ((s32[32,1,1]{2,1,0:T(1,128)}), s32[32,1,1]{2,1,0:T(1,128)S(1)}, u32[]{:S(2)}, u32[]{:S(2)}) async-start(s32[32,1,1]{2,1,0:T(1,128)} %broadcast_in_dim.56), calls=%async_computation | async-start | bytes 32768 | tf_op jit(solution)/shard_map/all_to_all | solution.py:258
  45.8 13.4 %all-to-all-start.1 = ((f32[32,4,144]{2,1,0:T(4,128)}), f32[32,4,144]{2,1,0:T(4,128)S(1)}, u32[]{:S(2)}, u32[]{:S(2)}) async-start(f32[32,4,144]{2,1,0:T(4,128)} %bitcast.2), calls=%async_computation.1 | async-start | bytes 262144 | tf_op jit(solution)/shard_map/all_to_all | solution.py:258
  50.9 424.5 %reduce-scatter.10.cloned.1.call-start = ((), (), s32[]{:S(2)}) async-start(), calls=%async_computation.11 | async-start | bytes 442368 | tf_op jit(solution)/shard_map/reduce_scatter | solution.py:379
  60.1 3.7 collective-permute-start.2
  177.9 12.7 %collective-permute-start.3 = (f32[4,256,128]{2,1,0:T(8,128)S(1)}, f32[4,256,128]{2,1,0:T(8,128)S(1)}, u32[]{:S(2)}, u32[]{:S(2)}) collective-permute-start(f32[4,256,128]{2,1,0:T(8,128)S(1)} %fusion.47), channel_id=1, source_target_pairs={{0,2},{1,3},{2,0},{3,1},{4,6},{5,7},{6,4},{7,5},{8,10},{9,11},{10,... | collective-permute-start | bytes 1572872 | tf_op jit(solution)/shard_map/ppermute | solution.py:231
  190.8 2.9 collective-permute-start.4
  236.0 3.5 collective-permute-start.5
  240.0 19.9 %collective-permute-start.6 = (bf16[1,256,1536]{2,1,0:T(8,128)(2,1)S(1)}, bf16[1,256,1536]{2,1,0:T(8,128)(2,1)S(1)}, u32[]{:S(2)}, u32[]{:S(2)}) collective-permute-start(bf16[1,256,1536]{2,1,0:T(8,128)(2,1)S(1)} %slice.343), channel_id=1, source_target_pairs={{0,2},{1,3},{2,0},{3,1},{4,6},{5,7},{6,4},{7,5},{8,10},{9,11},{10,... | collective-permute-start | bytes 2359304 | tf_op jit(solution)/shard_map/ppermute | solution.py:231
  262.2 19.0 %collective-permute-start.7 = (bf16[1,256,1536]{2,1,0:T(8,128)(2,1)S(1)}, bf16[1,256,1536]{2,1,0:T(8,128)(2,1)S(1)}, u32[]{:S(2)}, u32[]{:S(2)}) collective-permute-start(bf16[1,256,1536]{2,1,0:T(8,128)(2,1)S(1)} %get-tuple-element.277), channel_id=1, source_target_pairs={{0,2},{1,3},{2,0},{3,1},{4,6},{5,7},{6,4},{7,5},{8,10},{9,11},{10,... | collective-permute-start | bytes 2359304 | tf_op jit(solution)/shard_map/ppermute | solution.py:231
  281.4 3.5 collective-permute-start.8
  366.7 14.3 %collective-permute-start.9 = (f32[4,256,128]{1,0,2:T(4,128)}, f32[4,256,128]{1,0,2:T(4,128)}, u32[]{:S(2)}, u32[]{:S(2)}) collective-permute-start(f32[4,256,128]{1,0,2:T(4,128)} %constant_dynamic-update-slice_fusion), channel_id=1, source_target_pairs={{0,2},{1,3},{2,0},{3,1},{4,6},{5,7},{6,4},{7,5},{8,10},{9,11},{10,... | collective-permute-start | bytes 1572872 | tf_op jit(solution)/shard_map/ppermute | solution.py:231
  391.4 5.1 collective-permute-start.10
  414.4 133.1 %reduce-scatter.8.cloned.1.call-start = ((), (), s32[]{:S(2)}) async-start(), calls=%async_computation.10 | async-start | bytes 2654208 | tf_op jit(solution)/shard_map/reduce_scatter | solution.py:377
  421.0 224.3 %reduce-scatter.6.cloned.1.call-start = ((), (), s32[]{:S(2)}) async-start(), calls=%async_computation.9 | async-start | bytes 5308416 | tf_op jit(solution)/shard_map/reduce_scatter | solution.py:378
  439.9 3.6 collective-permute-start.11
  445.8 38.2 %collective-permute-start.12 = (bf16[1,256,1536]{2,1,0:T(8,128)(2,1)S(1)}, bf16[1,256,1536]{2,1,0:T(8,128)(2,1)S(1)}, u32[]{:S(2)}, u32[]{:S(2)}) collective-permute-start(bf16[1,256,1536]{2,1,0:T(8,128)(2,1)S(1)} %slice.342), channel_id=1, source_target_pairs={{0,2},{1,3},{2,0},{3,1},{4,6},{5,7},{6,4},{7,5},{8,10},{9,11},{10,... | collective-permute-start | bytes 2359304 | tf_op jit(solution)/shard_map/ppermute | solution.py:231
  475.4 5.9 collective-permute-start.13
  487.3 62.4 %all-to-all-start.2 = ((bf16[32,1,144]{2,1,0:T(2,128)(2,1)}), bf16[32,1,144]{2,1,0:T(2,128)(2,1)S(1)}, u32[]{:S(2)}, u32[]{:S(2)}) async-start(bf16[32,1,144]{2,1,0:T(2,128)(2,1)} %convert_element_type.198), calls=%async_computation.2 | async-start | bytes 65536 | tf_op jit(solution)/shard_map/all_to_all | solution.py:258
  547.5 4.0 collective-permute-start.14
  651.8 12.0 %all-to-all-start.3 = ((f32[32,1,128]{2,1,0:T(1,128)}), f32[32,1,128]{2,1,0:T(1,128)}, u32[]{:S(2)}, u32[]{:S(2)}) async-start(f32[32,1,128]{2,1,0:T(1,128)} %broadcast_in_dim.63), calls=%async_computation.5 | async-start | bytes 32768 | tf_op jit(solution)/shard_map/all_to_all | solution.py:258
  (79 other events, 1585.2 us)
Sparse Core Ops, SparseCore 0:
  14.2 67.8 all-gather.2
  84.8 78.4 all-gather.4
  414.5 60.8 reduce-scatter.9
  478.7 68.6 reduce-scatter.7
  551.0 94.2 reduce-scatter.5

commit v2 on v1

v2 whole, which is shorter than its diff:
```python
import math

import jax
import jax.numpy as jnp
from jax import lax
from jax.experimental import pallas as pl
from jax.experimental.pallas import tpu as pltpu
from jax.sharding import PartitionSpec as P

D = 1536
E = 3072
N = 16
R = 96
CONV = 4
CH = 7 + N
ITEM = 256
STEP = 10
SUB = 8
LANE = 128
BIAS, STEP_BIAS, SKIP, RATE = CONV, CONV + 1, CONV + 2, CONV + 3
TABLE = 32
SMALL = 2 * LANE
ALL = ("dp", "fsdp")
LOG2E = math.log2(math.e)
LN2 = math.log(2.0)
F32 = jnp.float32
BF = jnp.bfloat16
VMEM_LIMIT = 60 * 1024 * 1024
SCAN_BLOCK = 64
PITCH = ITEM + SUB


def product(left, right):
    return jnp.dot(left, right, preferred_element_type=F32)


def left_outer(left, right):
    return lax.dot_general(left, right, (((0,), (0,)), ((), ())), preferred_element_type=F32)


def right_inner(left, right):
    return lax.dot_general(left, right, (((1,), (1,)), ((), ())), preferred_element_type=F32)


def softplus(v):
    return jnp.maximum(v, 0.0) + jnp.log1p(jnp.exp(-jnp.abs(v)))


def shape(rows, columns, dtype=F32):
    return jax.ShapeDtypeStruct((rows, columns), dtype)


def item_rows(v):
    return pl.BlockSpec((ITEM, v.shape[1]), lambda i: (i, 0))


def fixed(v):
    return pl.BlockSpec(v.shape, lambda i: (0, 0))


ANYWHERE = pl.BlockSpec(memory_space=pl.ANY)
PARAMS = pltpu.CompilerParams(vmem_limit_bytes=VMEM_LIMIT)


def cost(us):
    return pl.CostEstimate(flops=int(us * 1e9), bytes_accessed=int(us * 1e6), transcendentals=0)


def hold_body(v_ref, *refs):
    pass


def hold(v, *after):
    return pl.pallas_call(
        hold_body,
        in_specs=[ANYWHERE] * (1 + len(after)),
        out_specs=ANYWHERE,
        out_shape=jax.ShapeDtypeStruct(v.shape, v.dtype),
        input_output_aliases={0: 0},
        name="hold",
    )(v, *after)


def joined(blocks):
    return blocks if blocks[0].shape[0] % 16 == 0 else [jnp.concatenate(blocks, axis=0)]


def parted(blocks, count):
    if len(blocks) == count:
        return list(blocks)
    rows = blocks[0].shape[0] // count
    return [blocks[0][q * rows : (q + 1) * rows] for q in range(count)]


def delayed(v, k):
    if k == 0:
        return v
    row = lax.broadcasted_iota(jnp.int32, v.shape, 0)
    moved = pltpu.roll(v, k % v.shape[0], axis=0)
    return jnp.where(row >= k if k > 0 else row < v.shape[0] + k, moved, 0.0)


def convolved(xs, table):
    pre = table[BIAS : BIAS + 1, :]
    for k in range(CONV):
        pre = pre + delayed(xs, CONV - 1 - k) * table[k : k + 1, :]
    return pre


def mix_body(blocks_count, h_ref, *refs):
    blocks = refs[: blocks_count]
    xs_ref, u_ref, low_ref, proj_ref, stream_ref, x_ref, dt_ref, table_ref, tail = refs[-9:]

    @pl.when(pl.program_id(0) == 0)
    def _():
        at = 0
        for block in blocks:
            rows = slice(at, at + block.shape[0])
            stream_ref[rows, :] = block[:, :D]
            x_ref[rows, :] = block[:, D : D + LANE]
            tail[rows, :] = block[:, D + LANE :].astype(F32)
            at += block.shape[0]
        lane = lax.broadcasted_iota(jnp.int32, tail.shape, 1)
        dt_ref[...] = jnp.where(lane < R, tail[...], 0.0).astype(BF)
        table_ref[...] = tail[...].T[R:, :]

    xs = right_inner(h_ref[...], stream_ref[...])
    xs_ref[...] = xs
    pre = convolved(xs, table_ref)
    u = pre * jax.nn.sigmoid(pre)
    u_ref[...] = u
    low = u.astype(BF)
    low_ref[...] = low
    proj_ref[...] = product(low, x_ref[...])


def mix(h, blocks, after):
    tokens = h.shape[0]
    blocks = joined(blocks)
    width = sum(b.shape[0] for b in blocks)
    out_shape = [
        shape(tokens, width), shape(tokens, width), shape(tokens, width, BF), shape(tokens, LANE),
        shape(width, D, BF), shape(width, LANE, BF), shape(width, LANE, BF), shape(TABLE, width),
    ]
    return pl.pallas_call(
        lambda *refs: mix_body(len(blocks), *refs),
        grid=(tokens // ITEM,),
        in_specs=[item_rows(h)] + [fixed(b) for b in blocks] + [ANYWHERE] * len(after),
        out_specs=[item_rows(v) for v in out_shape[:4]] + [fixed(v) for v in out_shape[4:]],
        out_shape=out_shape,
        scratch_shapes=[pltpu.VMEM((width, LANE), F32)],
        compiler_params=PARAMS,
        cost_estimate=cost(6),
        name="mix",
    )(h, *blocks, *after)


def gates_body(count, h_ref, do_ref, y_ref, *refs):
    blocks, grads = refs[:count], refs[count + 4 : 2 * count + 4]
    dy_ref, dz_ref, o_ref, gate_ref = refs[count : count + 4]
    out_w, grad_gate, grad_out = refs[2 * count + 4 :]

    @pl.when(pl.program_id(0) == 0)
    def _():
        at = 0
        for block in blocks:
            rows = slice(at, at + block.shape[0])
            gate_ref[rows, :] = block[:, :D]
            out_w[rows, :] = block[:, D:]
            at += block.shape[0]
        grad_gate[...] = jnp.zeros_like(grad_gate)
        grad_out[...] = jnp.zeros_like(grad_out)

    h, do, y = h_ref[...], do_ref[...], y_ref[...]
    z = right_inner(h, gate_ref[...])
    dyg = right_inner(do, out_w[...])
    sig = jax.nn.sigmoid(z)
    act = z * sig
    dy_ref[...] = dyg * act
    mixed = (y * act).astype(BF)
    dz = (dyg * y * (sig + act * (1.0 - sig))).astype(BF)
    dz_ref[...] = dz
    o_ref[...] = product(mixed, out_w[...]).astype(BF)
    grad_gate[...] += left_outer(dz, h)
    grad_out[...] += left_outer(mixed, do)

    @pl.when(pl.program_id(0) == pl.num_programs(0) - 1)
    def _():
        at = 0
        for grad in grads:
            rows = slice(at, at + grad.shape[0])
            grad[:, :D] = grad_gate[rows, :].astype(BF)
            grad[:, D:] = grad_out[rows, :].astype(BF)
            at += grad.shape[0]


def gates(h, do, y, blocks):
    tokens, width = y.shape
    parts = len(blocks)
    blocks = joined(blocks)
    out_shape = [shape(tokens, width), shape(tokens, width, BF), shape(tokens, D, BF), shape(width, D, BF)]
    grads = [shape(*b.shape, BF) for b in blocks]
    once = lambda v: pl.BlockSpec(v.shape, lambda i: (0, 0), pipeline_mode=pl.Buffered(1))
    dy, dz, o, gate_full, *grads = pl.pallas_call(
        lambda *refs: gates_body(len(blocks), *refs),
        grid=(tokens // ITEM,),
        in_specs=[item_rows(h), item_rows(do), item_rows(y)] + [once(b) for b in blocks],
        out_specs=[item_rows(v) for v in out_shape[:3]] + [fixed(out_shape[3])] + [fixed(v) for v in grads],
        out_shape=out_shape + grads,
        scratch_shapes=[pltpu.VMEM((width, D), BF), pltpu.VMEM((width, D), F32), pltpu.VMEM((width, D), F32)],
        compiler_params=PARAMS,
        cost_estimate=cost(14),
        name="gates",
    )(h, do, y, *blocks)
    return dy, dz, o, gate_full, parted(grads, parts)


def mix_back_body(calls, count, h_ref, xs_ref, du_ref, ddtp_ref, low_ref, proj_ref, dproj_ref, x_ref, table_ref, *refs):
    drates, drows = refs[:calls], refs[calls : 2 * calls]
    dxs_ref, *grads = refs[-5 - count : -4]
    grad_stream, grad_x, grad_tail, rows = refs[-4:]

    @pl.when(pl.program_id(0) == 0)
    def _():
        grad_stream[...] = jnp.zeros_like(grad_stream)
        grad_x[...] = jnp.zeros_like(grad_x)
        grad_tail[...] = jnp.zeros_like(grad_tail)
        rows[...] = jnp.zeros_like(rows)

    dproj = dproj_ref[...].astype(BF)
    xs = xs_ref[...]
    pre = convolved(xs, table_ref)
    sig = jax.nn.sigmoid(pre)
    dpre = (du_ref[...] + right_inner(dproj, x_ref[...])) * (sig + pre * sig * (1.0 - sig))
    dxs = jnp.zeros_like(dpre)
    for k in range(CONV):
        back = CONV - 1 - k
        dxs = dxs + delayed(dpre, -back) * table_ref[k : k + 1, :]
        rows[R + k : R + k + 1, :] += jnp.sum(dpre * delayed(xs, back), axis=0, keepdims=True)
    rows[R + BIAS : R + BIAS + 1, :] += jnp.sum(dpre, axis=0, keepdims=True)
    low = dxs.astype(BF)
    dxs_ref[...] = low
    grad_stream[...] += left_outer(low, h_ref[...])
    grad_x[...] += left_outer(low_ref[...], dproj)
    lane = lax.broadcasted_iota(jnp.int32, dproj.shape, 1)
    rank = jnp.where(lane < R, proj_ref[...], 0.0).astype(BF)
    grad_tail[...] += left_outer(ddtp_ref[...], rank)

    @pl.when(pl.program_id(0) == pl.num_programs(0) - 1)
    def _():
        drow = sum(r[...] for r in drows)
        rows[R + STEP_BIAS : R + STEP_BIAS + 1, :] = jnp.sum(drow[:SUB], axis=0, keepdims=True)
        rows[R + SKIP : R + SKIP + 1, :] = jnp.sum(drow[SUB:], axis=0, keepdims=True)
        rows[R + RATE : R + CH, :] = sum(r[...] for r in drates) * -jnp.exp(table_ref[RATE:CH, :])
        grad_tail[...] += rows[...].T
        at = 0
        for grad in grads:
            part = slice(at, at + grad.shape[0])
            grad[:, :D] = grad_stream[part, :].astype(BF)
            grad[:, D : D + LANE] = grad_x[part, :].astype(BF)
            grad[:, D + LANE :] = grad_tail[part, :].astype(BF)
            at += grad.shape[0]


def mix_back(h, xs, du, ddtp, low, proj, dproj, x_full, table, drates, drows, parts, after):
    tokens, width = xs.shape
    block_rows = width // parts
    blocks = [shape(block_rows, D + SMALL, BF)] * parts if block_rows % 16 == 0 else [shape(width, D + SMALL, BF)]
    dxs_shape = shape(tokens, width, BF)
    calls = len(drates)
    dxs, *grads = pl.pallas_call(
        lambda *refs: mix_back_body(calls, len(blocks), *refs),
        grid=(tokens // ITEM,),
        in_specs=[item_rows(v) for v in (h, xs, du, ddtp, low, proj, dproj)]
        + [fixed(v) for v in (x_full, table, *drates, *drows)]
        + [ANYWHERE] * len(after),
        out_specs=[item_rows(dxs_shape)] + [fixed(v) for v in blocks],
        out_shape=[dxs_shape] + blocks,
        scratch_shapes=[
            pltpu.VMEM((width, D), F32), pltpu.VMEM((width, LANE), F32), pltpu.VMEM((width, LANE), F32),
            pltpu.VMEM((LANE, width), F32),
        ],
        compiler_params=PARAMS,
        cost_estimate=cost(8),
        name="mix_back",
    )(h, xs, du, ddtp, low, proj, dproj, x_full, table, *drates, *drows, *after)
    return dxs, parted(grads, parts)


def scan_prepare(proj_ref, dt_ref, table_ref, pre, rate, bc):
    pre[...] = right_inner(proj_ref[...].astype(BF), dt_ref[...]) + table_ref[STEP_BIAS : STEP_BIAS + 1, :]
    rate[...] = -jnp.exp(table_ref[RATE:CH, :]) * LOG2E
    turned = proj_ref[...].T
    for g in range(bc.shape[0]):
        bc[g, :, :SUB] = turned[R:, g * SUB : (g + 1) * SUB]


def scan_forward_body(u_ref, proj_ref, dt_ref, table_ref, *refs):
    y_ref, states_ref, pre, rate_ref, bc_ref, carry, parts = refs[-7:]
    groups = u_ref.shape[0] // SUB
    chunks = u_ref.shape[1] // LANE

    @pl.when(pl.program_id(1) == 0)
    def _():
        carry[...] = jnp.zeros_like(carry)

    scan_prepare(proj_ref, dt_ref, table_ref, pre, rate_ref, bc_ref)

    def group(g, _):
        base = pl.multiple_of(g * SUB, SUB)
        u8 = u_ref[pl.ds(base, SUB), :]
        step8 = softplus(pre[pl.ds(base, SUB), :])
        drive8 = step8 * u8
        bc = bc_ref[g]
        states = [carry[:, c * LANE : (c + 1) * LANE] for c in range(chunks)]
        for j in range(SUB):
            b = jnp.broadcast_to(bc[:N, j : j + 1], (N, LANE))
            cc = jnp.broadcast_to(bc[N:, j : j + 1], (N, LANE))
            at = pl.multiple_of((base + j) * N, N)
            for c in range(chunks):
                lanes = slice(c * LANE, (c + 1) * LANE)
                step = jnp.broadcast_to(step8[j : j + 1, lanes], (N, LANE))
                drive = jnp.broadcast_to(drive8[j : j + 1, lanes], (N, LANE))
                s = jnp.exp2(step * rate_ref[:, lanes]) * states[c] + b * drive
                states[c] = s
                states_ref[pl.ds(at, N), lanes] = s
                p = cc * s
                parts[c, j * SUB : (j + 1) * SUB, :] = p[:SUB] + p[SUB:]
        for c in range(chunks):
            lanes = slice(c * LANE, (c + 1) * LANE)
            carry[:, lanes] = states[c]
            total = table_ref[SKIP : SKIP + 1, lanes] * u8[:, lanes]
            for n in range(SUB):
                total = total + parts[c, pl.ds(n, SUB, stride=SUB), :]
            y_ref[pl.ds(base, SUB), lanes] = total
        return 0

    lax.fori_loop(0, groups, group, 0)


def scan_forward(begin, count, u, proj, dt, table, kept, after):
    total, width = u.shape
    block = SCAN_BLOCK
    steps = ITEM // block
    chunks = width // LANE
    at = lambda i, t: ((begin + i) * steps + t, 0)
    tok = pl.BlockSpec((block, width), at)
    whole = lambda v: pl.BlockSpec(v.shape, lambda i, t: (0, 0))
    extra = list(kept) + list(after)
    return pl.pallas_call(
        scan_forward_body,
        grid=(count, steps),
        in_specs=[tok, pl.BlockSpec((block, LANE), at), whole(dt), whole(table)] + [ANYWHERE] * len(extra),
        out_specs=[tok, pl.BlockSpec((block * N, width), at)],
        out_shape=[shape(total, width), shape(total * N, width)],
        scratch_shapes=[
            pltpu.VMEM((block, width), F32), pltpu.VMEM((N, width), F32), pltpu.VMEM((block // SUB, 2 * N, LANE), F32),
            pltpu.VMEM((N, width), F32), pltpu.VMEM((chunks, SUB * SUB, LANE), F32),
        ],
        input_output_aliases={4 + k: k for k in range(len(kept))},
        compiler_params=PARAMS,
        cost_estimate=cost(8 * count),
        name="scan_forward",
    )(u, proj, dt, table, *extra)


def scan_backward_body(u_ref, proj_ref, dy_ref, states_ref, before_ref, dt_ref, table_ref, *refs):
    du_ref, ddtp_ref, dproj_ref, drate_ref, drow_ref = refs[-15:-10]
    pre, rate_ref, bc_ref, ddtp, carry, parts, parts2, sums, stage, own = refs[-10:]
    block = u_ref.shape[0]
    groups = block // SUB
    chunks = u_ref.shape[1] // LANE
    back = pl.num_programs(1) - 1 - pl.program_id(1)
    first = back == 0

    @pl.when(pl.program_id(1) == 0)
    def _():
        carry[...] = jnp.zeros_like(carry)

    @pl.when((pl.program_id(0) == 0) & (pl.program_id(1) == 0))
    def _():
        drate_ref[...] = jnp.zeros_like(drate_ref)
        drow_ref[...] = jnp.zeros_like(drow_ref)

    scan_prepare(proj_ref, dt_ref, table_ref, pre, rate_ref, bc_ref)

    def group(k, _):
        g = groups - 1 - k
        base = pl.multiple_of(g * SUB, SUB)
        u8 = u_ref[pl.ds(base, SUB), :]
        pre8 = pre[pl.ds(base, SUB), :]
        step8 = softplus(pre8)
        drive8 = step8 * u8
        dy8 = dy_ref[pl.ds(base, SUB), :]
        bc = bc_ref[g]
        grads = [carry[:, c * LANE : (c + 1) * LANE] for c in range(chunks)]
        drate = [drate_ref[:, c * LANE : (c + 1) * LANE] for c in range(chunks)]
        for j in reversed(range(SUB)):
            b = jnp.broadcast_to(bc[:N, j : j + 1], (N, LANE))
            cc = jnp.broadcast_to(bc[N:, j : j + 1], (N, LANE))
            at = pl.multiple_of((base + j) * N, N)
            db = jnp.zeros((N, LANE), F32)
            dc = jnp.zeros((N, LANE), F32)
            for c in range(chunks):
                lanes = slice(c * LANE, (c + 1) * LANE)
                step = jnp.broadcast_to(step8[j : j + 1, lanes], (N, LANE))
                drive = jnp.broadcast_to(drive8[j : j + 1, lanes], (N, LANE))
                dy = jnp.broadcast_to(dy8[j : j + 1, lanes], (N, LANE))
                now = states_ref[pl.ds(at, N), lanes]
                if j > 0:
                    prev = states_ref[pl.ds(at - N, N), lanes]
                else:
                    prev = states_ref[pl.ds(pl.multiple_of(jnp.maximum(at - N, 0), N), N), lanes]
                    edge = jnp.where(first, 0.0, before_ref[:, lanes])
                    prev = jnp.where(g == 0, edge, prev)
                rate = rate_ref[:, lanes]
                grad = cc * dy + grads[c]
                dc = dc + now * dy
                db = db + grad * drive
                p = grad * b
                parts[c, j * SUB : (j + 1) * SUB, :] = p[:SUB] + p[SUB:]
                grad = grad * jnp.exp2(step * rate)
                grads[c] = grad
                q = grad * prev
                p = q * rate
                parts2[c, j * SUB : (j + 1) * SUB, :] = p[:SUB] + p[SUB:]
                drate[c] = drate[c] + q * step
            token = back * block + base + j
            sums[pl.ds(token, N, stride=PITCH), :] = db
            sums[pl.ds(N * PITCH + token, N, stride=PITCH), :] = dc
        for c in range(chunks):
            lanes = slice(c * LANE, (c + 1) * LANE)
            carry[:, lanes] = grads[c]
            drate_ref[:, lanes] = drate[c]
            x = parts[c, pl.ds(0, SUB, stride=SUB), :]
            r = parts2[c, pl.ds(0, SUB, stride=SUB), :]
            for n in range(1, SUB):
                x = x + parts[c, pl.ds(n, SUB, stride=SUB), :]
                r = r + parts2[c, pl.ds(n, SUB, stride=SUB), :]
            dy = dy8[:, lanes]
            u = u8[:, lanes]
            du_ref[pl.ds(base, SUB), lanes] = step8[:, lanes] * x + table_ref[SKIP : SKIP + 1, lanes] * dy
            d = (u * x + LN2 * r) * jax.nn.sigmoid(pre8[:, lanes])
            ddtp[pl.ds(base, SUB), lanes] = d
            drow_ref[:SUB, lanes] += d
            drow_ref[SUB:, lanes] += dy * u
        return 0

    lax.fori_loop(0, groups, group, 0)
    low = ddtp[...].astype(BF)
    ddtp_ref[...] = low
    own[pl.ds(pl.multiple_of(back * block, block), block), :] = product(low, dt_ref[...])

    @pl.when(first)
    def _():
        stage[...] = jnp.zeros_like(stage)
        ones = jnp.ones((SUB, LANE), BF)
        for n in range(2 * N):
            wide = sums[n * PITCH : n * PITCH + ITEM, :]
            high = wide.astype(BF)
            row = right_inner(ones, high) + right_inner(ones, (wide - high.astype(F32)).astype(BF))
            stage[R + n : R + n + 1, :] = row[:1]
        dproj_ref[...] = own[...] + stage[...].T


def scan_backward(begin, count, u, proj, dy, states, dt, table, kept, after):
    total, width = u.shape
    block = SCAN_BLOCK
    steps = ITEM // block
    chunks = width // LANE
    place = lambda i, t: (begin + i) * steps + steps - 1 - t
    at = lambda i, t: (place(i, t), 0)
    tok = pl.BlockSpec((block, width), at)
    whole = lambda v: pl.BlockSpec(v.shape, lambda i, t: (0, 0))
    extra = list(kept) + list(after)
    out_shape = [
        shape(total, width), shape(total, width, BF), shape(total, LANE), shape(N, width), shape(2 * SUB, width)
    ]
    return pl.pallas_call(
        scan_backward_body,
        grid=(count, steps),
        in_specs=[
            tok, pl.BlockSpec((block, LANE), at), tok,
            pl.BlockSpec((block * N, width), at),
            pl.BlockSpec((N, width), lambda i, t: (jnp.maximum(place(i, t) * block - 1, 0), 0)),
            whole(dt), whole(table),
        ]
        + [ANYWHERE] * len(extra),
        out_specs=[tok, tok, pl.BlockSpec((ITEM, LANE), lambda i, t: (begin + i, 0)), whole(out_shape[3]), whole(out_shape[4])],
        out_shape=out_shape,
        scratch_shapes=[
            pltpu.VMEM((block, width), F32), pltpu.VMEM((N, width), F32), pltpu.VMEM((block // SUB, 2 * N, LANE), F32),
            pltpu.VMEM((block, width), F32), pltpu.VMEM((N, width), F32),
            pltpu.VMEM((chunks, SUB * SUB, LANE), F32), pltpu.VMEM((chunks, SUB * SUB, LANE), F32),
            pltpu.VMEM((2 * N * PITCH, LANE), F32), pltpu.VMEM((LANE, ITEM), F32), pltpu.VMEM((ITEM, LANE), F32),
        ],
        input_output_aliases={7 + k: k for k in range(len(kept))},
        compiler_params=PARAMS,
        cost_estimate=cost(15 * count),
        name="scan_backward",
    )(u, proj, dy, states, states, dt, table, *extra)


def update_body(factor_ref, *refs):
    grads, states, outs = refs[:5], refs[5:29], refs[29:]
    factor = factor_ref[0, 0]
    ema_keep = min(0.9999, (1.0 + STEP) / (10.0 + STEP))

    def update(k, g):
        learn_rate, weight_decay = (0.5, 0.0) if k == 4 else (0.03, 0.1)
        weight, first, second, average = (states[4 * k + q][...] for q in range(4))
        clipped = g * factor
        first = 0.9 * first + 0.1 * clipped
        second = 0.999 * second + 0.001 * clipped * clipped
        first_hat = first / (1.0 - 0.9**STEP)
        second_hat = second / (1.0 - 0.999**STEP)
        weight = weight - learn_rate * (first_hat / (jnp.sqrt(second_hat) + 1e-08) + weight_decay * weight)
        average = ema_keep * average + (1.0 - ema_keep) * weight
        for q, v in enumerate((first, second, weight, average)):
            outs[4 * k + q][...] = v

    ada, wide, small, small_t, out = grads
    update(0, ada[...])
    update(1, wide[...])
    update(5, out[...])

    @pl.when(pl.program_id(0) == 0)
    def _():
        update(2, small[...])
        update(3, small_t[:R, :])
        update(4, small_t[R:CH + R, :])


def update_all(factor, ada, wide, small, small_t, out, states):
    part = 256
    right = lambda v: pl.BlockSpec((v.shape[0], part), lambda t: (0, t))
    kinds = [right, right, fixed, fixed, fixed, right]
    specs = [kind(v) for kind, group in zip(kinds, states) for v in group]
    flat = [v for group in states for v in group]
    return pl.pallas_call(
        update_body,
        grid=(D // part,),
        in_specs=[pl.BlockSpec(memory_space=pltpu.SMEM), right(ada), right(wide), fixed(small), fixed(small_t), right(out)]
        + specs,
        out_specs=specs,
        out_shape=[shape(*v.shape) for v in flat],
        compiler_params=PARAMS,
        cost_estimate=cost(11),
        name="update",
    )(factor.reshape(1, 1), ada, wide, small, small_t, out, *flat)


def embed_time(steps):
    half = D // 2
    freqs = jnp.exp(-math.log(10000.0) * jnp.arange(half, dtype=F32) / half)
    angles = steps.astype(F32)[:, None] * freqs[None, :]
    return jax.nn.silu(jnp.concatenate([jnp.cos(angles), jnp.sin(angles)], axis=1))


def normalize(x):
    mean = jnp.mean(x, axis=2, keepdims=True)
    centered = x - mean
    var = jnp.mean(centered * centered, axis=2, keepdims=True)
    scale = lax.rsqrt(var + 1e-06)
    return centered * scale, scale


def group_bits(size):
    return [1 << k for k in reversed(range(size.bit_length() - 1))]


def swap(v, bit, size):
    return lax.ppermute(v, "fsdp", [(i, i ^ bit) for i in range(size)])


def group_gather(v, size):
    for bit in group_bits(size):
        v = jnp.concatenate([v, swap(v, bit, size)], axis=0)
    return v


def group_scatter_steps(v, size, gate):
    for bit in reversed(group_bits(size)):
        half = v.shape[0] // 2
        away = v[half:].astype(BF)
        if gate:
            away = hold(away, *gate)
        v = v[:half].astype(F32) + swap(away, bit, size).astype(F32)
        yield v


def group_sum(v, size):
    bits = group_bits(size)
    half = v.shape[0] // 2
    total = v[:half] + swap(v[half:], bits[-1], size)
    for k, bit in enumerate(bits[:-1]):
        other = swap(total, bit, size)
        rows = other.shape[0] // (size // 2)
        total = total + jnp.concatenate(
            [other[(p ^ (1 << k)) * rows : ((p ^ (1 << k)) + 1) * rows] for p in range(size // 2)], axis=0
        )
    return jnp.concatenate([total, swap(total, bits[-1], size)], axis=0)


def ring_order(size):
    if size == 8:
        return [0, 2, 4, 6, 7, 5, 3, 1]
    return list(range(size))


def ring_move(v, way, size):
    order = ring_order(size)
    return lax.ppermute(v, "dp", [(order[p], order[(p + way) % size]) for p in range(size)])


def ring_gather_steps(v, size, gate):
    behind = ahead = v
    for _ in range(size // 2 - 1):
        if gate:
            behind, ahead = hold(behind, *gate), hold(ahead, *gate)
        behind, ahead = ring_move(behind, 1, size), ring_move(ahead, -1, size)
        yield [behind, ahead]
    cut = v.shape[0] // 2
    if gate:
        behind, ahead = hold(behind, *gate), hold(ahead, *gate)
    yield [jnp.concatenate([ring_move(behind[:cut], 1, size), ring_move(ahead[cut:], -1, size)], axis=0)]


def ring_scatter_steps(blocks, size, gate):
    cut = blocks[0].shape[0] // 2
    add = lambda a, b: (a.astype(F32) + b.astype(F32)).astype(BF)
    up, down = ring_move(blocks[-1][:cut], 1, size), ring_move(blocks[-1][cut:], -1, size)
    yield [up, down]
    for s in range(size // 2 - 1, 0, -1):
        ahead, behind = blocks[2 * s], blocks[2 * s - 1]
        if s == size // 2 - 1:
            ahead = jnp.concatenate([add(ahead[:cut], up), ahead[cut:]], axis=0)
            behind = jnp.concatenate([behind[:cut], add(behind[cut:], down)], axis=0)
        else:
            ahead, behind = add(ahead, up), add(behind, down)
        if gate:
            ahead, behind = hold(ahead, *gate), hold(behind, *gate)
        up, down = ring_move(ahead, 1, size), ring_move(behind, -1, size)
        yield [up, down]
    yield blocks[0].astype(F32) + up.astype(F32) + down.astype(F32)


def exchange(v):
    return lax.all_to_all(v, ALL, 0, 0, tiled=True)


def on_device(sizes, *args):
    (
        act, cotangent, item_counts, item_lengths, time_steps,
        ada_weight, ada_first, ada_second, ada_average,
        in_weight, in_first, in_second, in_average,
        x_weight, x_first, x_second, x_average,
        dt_weight, dt_first, dt_second, dt_average,
        chan_table, chan_first, chan_second, chan_average,
        out_weight, out_first, out_second, out_average,
    ) = args
    n_dp, n_fsdp = sizes
    devices = n_dp * n_fsdp
    count = item_lengths.shape[0]
    items = count * n_fsdp
    tokens = items * ITEM
    ada_cols = ada_weight.shape[1]
    f = lax.axis_index("fsdp")
    half = n_dp // 2
    low_half = lax.axis_index("dp") < half
    offsets = [0]
    for bit in group_bits(n_fsdp):
        offsets = offsets + [o ^ bit for o in offsets]

    forth = []
    for b in range(devices):
        i, j = divmod(b, 2)
        k, g = divmod(i, n_fsdp)
        forth.append((b, (k + half * j) * n_fsdp + g))
    back = [(t, s) for s, t in forth]
    across = [(q, (q + half) % n_dp) for q in range(n_dp)]
    wide = in_weight.astype(BF).T
    rows = wide.shape[0] // 2
    leaving = jnp.where(low_half, wide[rows:], wide[:rows])
    swapped = lax.ppermute(leaving, "dp", across)
    small = jnp.concatenate([x_weight.astype(BF), dt_weight.astype(BF).T, chan_table.astype(BF).T], axis=1)
    small = jnp.pad(small, ((0, 0), (0, SMALL - small.shape[1])))
    small = lax.ppermute(hold(small, leaving), ALL, forth)
    stream_own = jnp.concatenate([jnp.where(low_half, wide[:rows], swapped), small], axis=1)
    gate_own = jnp.where(low_half, swapped, wide[rows:])

    live_items = jnp.arange(count, dtype=jnp.int32) < item_counts[0]
    live_rows = jnp.arange(ITEM, dtype=jnp.int32)[None, :] < item_lengths[:, None]
    live = live_items[:, None] & live_rows
    dfinal_own = jnp.where(live[..., None], cotangent.reshape(count, ITEM, D), jnp.zeros((), BF))
    x_all = group_gather(act.reshape(count, ITEM, D), n_fsdp)
    dfinal_all = group_gather(hold(dfinal_own, x_all), n_fsdp)

    steps_all = exchange(hold(jnp.broadcast_to(time_steps[None], (devices, count)), leaving)).reshape(-1)
    cond_all = embed_time(steps_all).astype(BF)
    mod_cols = product(cond_all, ada_weight.astype(BF)).reshape(n_dp, 1, items, ada_cols)
    mod_cols = jnp.broadcast_to(mod_cols, (n_dp, n_fsdp, items, ada_cols)).reshape(devices, items, ada_cols)
    mod = jnp.swapaxes(exchange(hold(mod_cols, stream_own)), 0, 1).reshape(n_fsdp, count, 3 * D)
    mod = jnp.take(mod, jnp.array(offsets, jnp.int32) ^ f, axis=0).reshape(items, 1, 3 * D)
    shift, scale, gate = mod[..., :D], mod[..., D : 2 * D], mod[..., 2 * D :]

    normed, _ = normalize(x_all.astype(F32))
    h_low = (normed * (1.0 + scale) + shift).astype(BF).reshape(tokens, D)
    do_low = (gate * dfinal_all.astype(F32)).astype(BF).reshape(tokens, D)

    stream, gate_ring = [stream_own], []
    steps = ring_gather_steps(stream_own, n_dp, gate_ring)
    for s in range(half):
        stream += next(steps)
        if s == half - 3:
            gate_ring[:] = [x_all]
        if s == half - 2:
            gate_ring[:] = [h_low]
    out_own = lax.ppermute(hold(out_weight.astype(BF), stream[half - 1]), ALL, forth)
    rest_own = hold(jnp.concatenate([gate_own, out_own], axis=1), stream[-1])
    rest_steps = list(ring_gather_steps(rest_own, n_dp, []))
    rest = [rest_own] + sum(rest_steps, [])

    xs, u, u_low, proj, stream_full, x_full, dt_full, table = mix(h_low, stream, [rest_own])
    proj = group_sum(proj, n_fsdp)
    calls = 2
    part = items // calls
    kept = []
    for i in range(calls):
        kept = scan_forward(i * part, part, u, proj, dt_full, table, kept, rest_steps[half // 2 - 1 + i])
    y, states = kept

    dy, dz_low, o_part, gate_full, early = gates(h_low, do_low, y, rest)
    gate_early = []
    early_steps = ring_scatter_steps(early, n_dp, gate_early)
    o_steps = group_scatter_steps(o_part.reshape(items, ITEM, D), n_fsdp, gate_early)
    came = next(early_steps)
    o_own = next(o_steps)
    kept, drates, drows = [], [], []
    after = list(early)
    for i in range(calls):
        *kept, drate, drow = scan_backward(i * part, part, u, proj, dy, states, dt_full, table, kept, after)
        drates.append(drate)
        drows.append(drow)
        after = list(came)
        gate_early[:] = [drate]
        came = next(early_steps)
        o_own = next(o_steps, o_own)
    for o_own in o_steps:
        pass
    for early_sum in early_steps:
        pass
    du_scan, ddtp_low, dproj = kept

    dproj = group_sum(dproj, n_fsdp)
    dxs_low, late = mix_back(h_low, xs, du_scan, ddtp_low, u_low, proj, dproj, x_full, table, drates, drows, n_dp, [o_own])
    dh = (product(dxs_low, stream_full) + product(dz_low, gate_full)).reshape(items, ITEM, D)
    dh_steps = group_scatter_steps(dh, n_fsdp, [])
    gate_late = []
    late_steps = ring_scatter_steps(late, n_dp, gate_late)
    next(late_steps)
    dh = next(dh_steps)
    next(late_steps)
    gate_late[:] = [dh]
    for dh in dh_steps:
        pass
    for late_sum in late_steps:
        pass

    small = lax.ppermute(late_sum[:, D:].astype(BF), ALL, back).astype(F32)
    small_t = small[:, LANE:].T
    out_share = lax.ppermute(early_sum[:, D:].astype(BF), ALL, back).astype(F32)
    gate_sum = early_sum[:, :D].astype(BF)
    late_sum = hold(late_sum[:, :D].astype(BF), dh)
    gate_moved = lax.ppermute(gate_sum, "dp", [(q, q + half) for q in range(half)])
    late_moved = lax.ppermute(late_sum, "dp", [(q + half, q) for q in range(half)])
    in_share = jnp.concatenate(
        [jnp.where(low_half, late_sum, gate_moved), jnp.where(low_half, late_moved, gate_sum)], axis=0
    )
    in_share = in_share.astype(F32)

    x = act.astype(F32).reshape(count, ITEM, D)
    normed, inverse = normalize(x)
    dfinal = dfinal_own.astype(F32)
    final = x + gate[:count] * o_own
    dmod = jnp.concatenate(
        [jnp.sum(dh, axis=1), jnp.sum(dh * normed, axis=1), jnp.sum(dfinal * o_own, axis=1)], axis=1
    ).astype(BF)
    dn = dh * (1.0 + scale[:count])
    act_grad = dfinal + inverse * (
        dn - jnp.mean(dn, axis=2, keepdims=True) - normed * jnp.mean(dn * normed, axis=2, keepdims=True)
    )
    dmod_all = exchange(jnp.swapaxes(dmod.reshape(count, devices, ada_cols), 0, 1)).reshape(devices * count, ada_cols)
    ada_share = left_outer(dmod_all, cond_all)

    shares = (ada_share, in_share, small, out_share)
    local = F32(0.0)
    for g in shares:
        local = local + jnp.sum(g * g)
    total = jnp.sum(exchange(jnp.broadcast_to(local, (devices, LANE)))[:, 0])
    grad_norm = jnp.sqrt(total)
    factor = jnp.minimum(1.0, 1.0 / (grad_norm + 1e-06))
    results = update_all(
        factor, ada_share, in_share, small[:, :LANE], small_t, out_share,
        (
            (ada_weight.T, ada_first.T, ada_second.T, ada_average.T),
            (in_weight.T, in_first.T, in_second.T, in_average.T),
            (x_weight, x_first, x_second, x_average),
            (dt_weight, dt_first, dt_second, dt_average),
            (chan_table, chan_first, chan_second, chan_average),
            (out_weight, out_first, out_second, out_average),
        ),
    )
    results = [v.T for v in results[:8]] + list(results[8:])
    return (final.reshape(count * ITEM, D), act_grad.reshape(count * ITEM, D), grad_norm, *results)


def solution(mesh):
    sizes = (mesh.shape["dp"], mesh.shape["fsdp"])
    first, second = P(ALL, None), P(None, ALL)
    weights = [second] * 8 + [first] * 4 + [second] * 8 + [first] * 4
    return jax.shard_map(
        lambda *args: on_device(sizes, *args),
        mesh=mesh,
        in_specs=(first, first, P(ALL), P(ALL), P(ALL), *weights),
        out_specs=(first, first, P(), *weights),
        check_vma=False,
    )
```

time: 703 us -> 499 us (0.71)
  waiting for transfers between devices: 357 us -> 112 us
  Pallas kernels: 88.4 us -> 155 us
  starting transfers between devices: 44.2 us -> 90 us
  matrix products: 47.4 us -> 11 us
  local copies, waits for them, and re-layouts: 73.2 us -> 40.3 us
  between operations: 23.2 us -> 8.5 us
  other arithmetic: 59.7 us -> 71.8 us
    reduce_scatter x3 -> x0, waiting for transfers between devices: 177 us -> none  [the longest x1 93.1 us: on_device(): lax.psum_scatter(grad_in, 'dp', scatter_dimension=0, tiled=True).astype(F32)]
    all_gather x2 -> x0, waiting for transfers between devices: 94.3 us -> none  [the longest x1 80 us: on_device(): in_full = lax.all_gather(in_weight.astype(BF).T, 'dp', axis=0, tiled=True)]
    pallas_call x2 -> x30, Pallas kernels: 88.4 us -> 155 us  [the longest x2 63.9 us: scan_backward(): pl.pallas_call(scan_backward_body, grid=(count, steps), in_specs=[tok, pl...]
    ppermute x3 -> x39, waiting for transfers between devices: 0.01 us -> 65 us  [the longest x32 60.9 us: ring_move(): lax.ppermute(v, 'dp', [(order[p], order[(p + way) % size]) for p in range...]
    ppermute x3 -> x39, starting transfers between devices: 4.35 us -> 51.2 us  [the longest x32 33.7 us: ring_move(): lax.ppermute(v, 'dp', [(order[p], order[(p + way) % size]) for p in range...]
    ppermute x12 -> x14, waiting for transfers between devices: 62.6 us -> 33.1 us  [swap(): return lax.ppermute(v, 'fsdp', [(i, i ^ bit) for i in range(size)])]
    dot_general x4 -> x0, matrix products: 15.7 us -> none  [right_inner(): lax.dot_general(left, right, (((1,), (1,)), ((), ())), preferred_element_...]
    dot_general x5 -> x1, matrix products: 18 us -> 2.78 us  [left_outer(): lax.dot_general(left, right, (((0,), (0,)), ((), ())), preferred_element_...]
  transfers between devices with their start and end apart: 24 -> 57, of which waited for: 16 -> 22; matrix products, arithmetic and copies ran while one was open for 9% -> 21% of each run, Pallas kernels for 0% -> 23%
where the time goes in v2:
time: 499 us; the launch traced here: 489 us
  Pallas kernels  155 us (31%)
  waiting for transfers between devices  112 us (22%)
  starting transfers between devices  90 us (18%)
  other arithmetic  71.8 us (14%)
  local copies, waits for them, and re-layouts  40.3 us (8%)
  matrix products  11 us (2%)
  between operations  8.5 us (2%)
    pallas_call x2, Pallas kernels, scan_backward(): pl.pallas_call(scan_backward_body, grid=(count, steps), in_specs=[tok, pl...  63.9 us
    ppermute x32, waiting for transfers between devices, ring_move(): lax.ppermute(v, 'dp', [(order[p], order[(p + way) % size]) for p in range...  60.9 us
    pallas_call x2, Pallas kernels, scan_forward(): pl.pallas_call(scan_forward_body, grid=(count, steps), in_specs=[tok, pl....  33.9 us
    ppermute x32, starting transfers between devices, ring_move(): lax.ppermute(v, 'dp', [(order[p], order[(p + way) % size]) for p in range...  33.7 us
    ppermute x14, waiting for transfers between devices, swap(): return lax.ppermute(v, 'fsdp', [(i, i ^ bit) for i in range(size)])  33.1 us
    all_to_all x4, starting transfers between devices, exchange(): return lax.all_to_all(v, ALL, 0, 0, tiled=True)  30.9 us
    pallas_call x1, Pallas kernels, gates(): pl.pallas_call(lambda *refs: gates_body(len(blocks), *refs), grid=(tokens...  22 us
    pallas_call x1, Pallas kernels, mix_back(): pl.pallas_call(lambda *refs: mix_back_body(calls, len(blocks), *refs), gr...  14.4 us
  transfers between devices with their start and end apart: 57, of which 22 were waited for; matrix products, arithmetic and copies ran while one was open for 21% of the time, Pallas kernels for 23%

profile of v2, /device:TPU:0, one launch (start us, length us, event | category | flops | bytes accessed | tf_op | source)
XLA Modules:
  0.0 489.4 jit_solution(3916355035766861025)
XLA Ops:
  35.7 5.4 %all-to-all-done.1 = f32[32,4,144]{2,1,0:T(4,128)S(1)} async-done(((f32[32,4,144]{2,1,0:T(4,128)}), f32[32,4,144]{2,1,0:T(4,128)S(1)}, u32[]{:S(2)}, u32[]{:S(2)}) %all-to-all-start.1) | async-done | bytes 73760 | tf_op jit(solution)/shard_map/all_to_all | solution.py:649
  47.6 7.3 %collective-permute-done.8.refs_0_.refs_4_ = bf16[96,1792]{1,0:T(8,128)(2,1)S(1)} collective-permute-done((bf16[96,1792]{1,0:T(8,128)(2,1)S(1)}, bf16[96,1792]{1,0:T(8,128)(2,1)S(1)}, u32[]{:S(2)}, u32[]{:S(2)}) %collective-permute-start.8) | collective-permute-done | bytes 344096 | tf_op jit(solution)/shard_map/ppermute | solution.py:613
  84.5 5.0 %collective-permute-done.13 = bf16[48,1792]{1,0:T(8,128)(2,1)S(1)} collective-permute-done((bf16[48,1792]{1,0:T(8,128)(2,1)S(1)}, bf16[48,1792]{1,0:T(8,128)(2,1)S(1)}, u32[]{:S(2)}, u32[]{:S(2)}) %collective-permute-start.13) | collective-permute-done | bytes 172064 | tf_op jit(solution)/shard_map/ppermute | solution.py:613
  90.3 9.9 %mix.1 = (f32[1024,768]{1,0:T(8,128)}, f32[1024,768]{1,0:T(8,128)}, bf16[1024,768]{1,0:T(8,128)(2,1)}, f32[1024,128]{1,0:T(8,128)}, bf16[768,1536]{1,0:T(8,128)(...) custom-call(bf16[1024,1536]{1,0:T(8,128)(2,1)} %fusion.refs_0_, ...), custom_call_target="tpu_custom_call" | custom-call | flops 6000000000 | bytes 6000000 | tf_op jit(solution)/shard_map/mix/pallas_call | solution.py:145
  108.2 19.7 %collective-permute-done.16 = f32[512,128]{1,0:T(8,128)S(1)} collective-permute-done((f32[512,128]{1,0:T(8,128)S(1)}, f32[512,128]{1,0:T(8,128)S(1)}, u32[]{:S(2)}, u32[]{:S(2)}) %collective-permute-start.16) | collective-permute-done | bytes 262176 | tf_op jit(solution)/shard_map/ppermute | solution.py:573
  132.8 10.3 %collective-permute-done.19.refs_0_.refs_6_ = bf16[96,3072]{1,0:T(8,128)(2,1)} collective-permute-done((bf16[96,3072]{1,0:T(8,128)(2,1)S(1)}, bf16[96,3072]{1,0:T(8,128)(2,1)}, u32[]{:S(2)}, u32[]{:S(2)}) %collective-permute-start.19) | collective-permute-done | bytes 589856 | tf_op jit(solution)/shard_map/ppermute | solution.py:613
  145.1 17.0 %scan_forward.2 = (f32[1024,768]{1,0:T(8,128)}, f32[16384,768]{1,0:T(8,128)}) custom-call(f32[1024,768]{1,0:T(8,128)} %get-tuple-element.94.u_ref, f32[1024,128]{1,0:T(8,128)} %pad_maximum_fusion.7.proj_ref.refs_5_, bf16[768,128]{1,0:T(8,128)(2,1)} %get-tuple-element.96.dt_ref, f32[32,768]{1,0:T(8,128)} %get-tuple-element.97.table_ref.refs_8_, ...), custom_call_target="tpu_custom_call" | custom-call | flops 16000000000 | bytes 16000000 | tf_op jit(solution)/shard_map/scan_forward/pallas_call | solution.py:350
  164.5 16.9 %scan_forward.3 = (f32[1024,768]{1,0:T(8,128)}, f32[16384,768]{1,0:T(8,128)}) custom-call(f32[1024,768]{1,0:T(8,128)} %get-tuple-element.94.u_ref, f32[1024,128]{1,0:T(8,128)} %pad_maximum_fusion.7.proj_ref.refs_5_, bf16[768,128]{1,0:T(8,128)(2,1)} %get-tuple-element.96.dt_ref, ...), custom_call_target="tpu_custom_call", output_to_operand_aliasing={{0}: (4, {}), {1}: (5, {})} | custom-call | flops 16000000000 | bytes 16000000 | tf_op jit(solution)/shard_map/scan_forward/pallas_call | solution.py:350
  185.5 22.0 %gates.1 = (f32[1024,768]{1,0:T(8,128)}, bf16[1024,768]{1,0:T(8,128)(2,1)}, bf16[1024,1536]{1,0:T(8,128)(2,1)}, bf16[768,1536]{1,0:T(8,128)(2,1)}, bf16[96,3072]...) custom-call(bf16[1024,1536]{1,0:T(8,128)(2,1)} %fusion.refs_0_, ...), custom_call_target="tpu_custom_call" | custom-call | flops 14000000000 | bytes 14000000 | tf_op jit(solution)/shard_map/gates/pallas_call | solution.py:204
  215.5 31.9 %scan_backward.2 = (f32[1024,768]{1,0:T(8,128)}, bf16[1024,768]{1,0:T(8,128)(2,1)}, f32[1024,128]{1,0:T(8,128)}, f32[16,768]{1,0:T(8,128)}, f32[16,768]{1,0:T(8,128)}) custom-call(f32[1024,768]{1,0:T(8,128)} %get-tuple-element.94.u_ref, f32[1024,128]{1,0:T(8,128)} %pad_maximum_fusion.7.proj_ref.refs_5_, f32[1024,768]{1,0:T(8,128)} %get-tuple-element.102.dy_ref, ...), custom_call_target="tpu_custom_call" | custom-call | flops 30000001024 | bytes 30000000 | tf_op jit(solution)/shard_map/scan_backward/pallas_call | solution.py:479
  248.3 32.0 %scan_backward.3 = (f32[1024,768]{1,0:T(8,128)}, bf16[1024,768]{1,0:T(8,128)(2,1)}, f32[1024,128]{1,0:T(8,128)}, f32[16,768]{1,0:T(8,128)}, f32[16,768]{1,0:T(8,128)}) custom-call(f32[1024,768]{1,0:T(8,128)} %get-tuple-element.94.u_ref, f32[1024,128]{1,0:T(8,128)} %pad_maximum_fusion.7.proj_ref.refs_5_, ...), custom_call_target="tpu_custom_call", output_to_operand_aliasing={{0}: (7, {}), {1}: (8, {}), {2}: (9, {})} | custom-call | flops 30000001024 | bytes 30000000 | tf_op jit(solution)/shard_map/scan_backward/pallas_call | solution.py:479
  288.9 5.9 %collective-permute-done.31 = f32[512,128]{1,0:T(8,128)S(1)} collective-permute-done((f32[512,128]{1,0:T(8,128)S(1)}, f32[512,128]{1,0:T(8,128)S(1)}, u32[]{:S(2)}, u32[]{:S(2)}) %collective-permute-start.31) | collective-permute-done | bytes 262176 | tf_op jit(solution)/shard_map/ppermute | solution.py:573
  294.9 5.1 %collective-permute-done.46 = bf16[96,3072]{1,0:T(8,128)(2,1)} collective-permute-done((bf16[96,3072]{1,0:T(8,128)(2,1)}, bf16[96,3072]{1,0:T(8,128)(2,1)}, u32[]{:S(2)}, u32[]{:S(2)}) %collective-permute-start.46) | collective-permute-done | bytes 589856 | tf_op jit(solution)/shard_map/ppermute | solution.py:613
  312.6 4.2 collective-permute-done.47
  320.5 7.4 %collective-permute-done.27 = bf16[1,256,1536]{2,1,0:T(8,128)(2,1)} collective-permute-done((bf16[1,256,1536]{2,1,0:T(8,128)(2,1)}, bf16[1,256,1536]{2,1,0:T(8,128)(2,1)}, u32[]{:S(2)}, u32[]{:S(2)}) %collective-permute-start.27) | collective-permute-done | bytes 786464 | tf_op jit(solution)/shard_map/ppermute | solution.py:573
  330.7 14.4 %mix_back.1 = (bf16[1024,768]{1,0:T(8,128)(2,1)}, bf16[96,1792]{1,0:T(8,128)(2,1)}, bf16[96,1792]{1,0:T(8,128)(2,1)}, bf16[96,1792]{1,0:T(8,128)(2,1)}, bf16[96,...) custom-call(bf16[1024,1536]{1,0:T(8,128)(2,1)} %fusion.refs_0_, ...), custom_call_target="tpu_custom_call" | custom-call | flops 8000000000 | bytes 8000000 | tf_op jit(solution)/shard_map/mix_back/pallas_call | solution.py:271
  347.5 4.1 fusion.37
  374.5 5.4 %collective-permute-done.41 = bf16[96,1792]{1,0:T(8,128)(2,1)S(1)} collective-permute-done((bf16[96,1792]{1,0:T(8,128)(2,1)}, bf16[96,1792]{1,0:T(8,128)(2,1)S(1)}, u32[]{:S(2)}, u32[]{:S(2)}) %collective-permute-start.41) | collective-permute-done | bytes 344096 | tf_op jit(solution)/shard_map/ppermute | solution.py:613
  394.8 5.8 %collective-permute-done.38 = bf16[96,1792]{0,1:T(8,128)(2,1)} collective-permute-done((bf16[96,1792]{0,1:T(8,128)(2,1)}, bf16[96,1792]{0,1:T(8,128)(2,1)}, u32[]{:S(2)}, u32[]{:S(2)}) %collective-permute-start.38) | collective-permute-done | bytes 344096 | tf_op jit(solution)/shard_map/ppermute | solution.py:613
  404.7 4.8 collective-permute-done.45
  423.3 7.2 %all-to-all-start.2 = ((bf16[32,1,144]{2,1,0:T(2,128)(2,1)}), bf16[32,1,144]{2,1,0:T(2,128)(2,1)}, u32[]{:S(2)}, u32[]{:S(2)}) async-start(bf16[32,1,144]{2,1,0:T(2,128)(2,1)} %convert_element_type.314), calls=%async_computation.2 | async-start | bytes 65536 | tf_op jit(solution)/shard_map/all_to_all | solution.py:649
  452.1 15.9 %all-to-all-start.3 = ((f32[32,1,128]{2,1,0:T(1,128)}), f32[32,1,128]{2,1,0:T(1,128)S(1)}, u32[]{:S(2)}, u32[]{:S(2)}) async-start(f32[32,1,128]{2,1,0:T(1,128)} %broadcast_in_dim.63), calls=%async_computation.3 | async-start | bytes 32768 | tf_op jit(solution)/shard_map/all_to_all | solution.py:649
  470.0 5.1 %all-to-all-done.3 = f32[32,1,128]{2,1,0:T(1,128)S(1)} async-done(((f32[32,1,128]{2,1,0:T(1,128)}), f32[32,1,128]{2,1,0:T(1,128)S(1)}, u32[]{:S(2)}, u32[]{:S(2)}) %all-to-all-start.3) | async-done | bytes 16416 | tf_op jit(solution)/shard_map/all_to_all | solution.py:649
  476.4 11.5 %update.1 = (f32[144,1536]{1,0:T(8,128)}, f32[144,1536]{1,0:T(8,128)}, f32[144,1536]{1,0:T(8,128)}, f32[144,1536]{1,0:T(8,128)}, f32[192,1536]{1,0:T(8,128)}, /*...) custom-call(f32[1,1]{1,0:T(1,128)} %bitcast.29.factor_ref, ...), custom_call_target="tpu_custom_call" | custom-call | flops 11000000512 | bytes 11000000 | tf_op jit(solution)/shard_map/update/pallas_call | solution.py:540
  (374 shorter events, 206.9 us)
Async XLA Ops:
  2.2 22.5 %collective-permute-start = (bf16[96,1536]{1,0:T(8,128)(2,1)S(1)}, bf16[96,1536]{1,0:T(8,128)(2,1)}, u32[]{:S(2)}, u32[]{:S(2)}) collective-permute-start(bf16[96,1536]{1,0:T(8,128)(2,1)S(1)} %broadcast_select_fusion.4.refs_0_), channel_id=1, source_target_pairs={{0,16},{4,20},{8,24},{12,28},{16,0},{20,4},{24,8},{28,12},{1,17},{... | collective-permute-start | bytes 884744 | tf_op jit(solution)/shard_map/ppermute | solution.py:685
  14.5 27.4 %collective-permute-start.2 = (bf16[1,256,1536]{2,1,0:T(8,128)(2,1)S(1)}, bf16[1,256,1536]{2,1,0:T(8,128)(2,1)S(1)}, u32[]{:S(2)}, u32[]{:S(2)}) collective-permute-start(bf16[1,256,1536]{2,1,0:T(8,128)(2,1)S(1)} %bitcast.114), channel_id=1, source_target_pairs={{0,2},{1,3},{2,0},{3,1},{4,6},{5,7},{6,4},{7,5},{8,10},{9,11},{10,... | collective-permute-start | bytes 2359304 | tf_op jit(solution)/shard_map/ppermute | solution.py:573
  43.2 18.7 %collective-permute-start.3 = (bf16[2,256,1536]{2,1,0:T(8,128)(2,1)}, bf16[2,256,1536]{2,1,0:T(8,128)(2,1)}, u32[]{:S(2)}, u32[]{:S(2)}) collective-permute-start(bf16[2,256,1536]{2,1,0:T(8,128)(2,1)} %pad_maximum_fusion.1), channel_id=1, source_target_pairs={{0,1},{1,0},{2,3},{3,2},{4,5},{5,4},{6,7},{7,6},{8,9},{9,8},{10,11... | collective-permute-start | bytes 4718600 | tf_op jit(solution)/shard_map/ppermute | solution.py:573
  55.6 23.5 %collective-permute-start.14 = (bf16[96,1536]{1,0:T(8,128)(2,1)}, bf16[96,1536]{1,0:T(8,128)(2,1)}, u32[]{:S(2)}, u32[]{:S(2)}) collective-permute-start(bf16[96,1536]{1,0:T(8,128)(2,1)} %hold.30), channel_id=1, source_target_pairs={{0,0},{1,16},{2,1},{3,17},{4,2},{5,18},{6,3},{7,19},{8,4},{9,20},{... | collective-permute-start | bytes 884744 | tf_op jit(solution)/shard_map/ppermute | solution.py:719
  102.1 28.1 %collective-permute-start.4 = (bf16[1,256,1536]{2,1,0:T(8,128)(2,1)}, bf16[1,256,1536]{2,1,0:T(8,128)(2,1)S(1)}, u32[]{:S(2)}, u32[]{:S(2)}) collective-permute-start(bf16[1,256,1536]{2,1,0:T(8,128)(2,1)} %hold.25), channel_id=1, source_target_pairs={{0,2},{1,3},{2,0},{3,1},{4,6},{5,7},{6,4},{7,5},{8,10},{9,11},{10,... | collective-permute-start | bytes 2359304 | tf_op jit(solution)/shard_map/ppermute | solution.py:573
  103.1 24.9 %collective-permute-start.18 = (bf16[96,3072]{1,0:T(8,128)(2,1)S(1)}, bf16[96,3072]{1,0:T(8,128)(2,1)S(1)}, u32[]{:S(2)}, u32[]{:S(2)}) collective-permute-start(bf16[96,3072]{1,0:T(8,128)(2,1)S(1)} %copy-done.13), channel_id=1, source_target_pairs={{0,8},{8,16},{16,24},{24,28},{28,20},{20,12},{12,4},{4,0},{1,9},{9... | collective-permute-start | bytes 1769480 | tf_op jit(solution)/shard_map/ppermute | solution.py:613
  104.3 24.9 %collective-permute-start.20 = (bf16[96,3072]{1,0:T(8,128)(2,1)S(1)}, bf16[96,3072]{1,0:T(8,128)(2,1)S(1)}, u32[]{:S(2)}, u32[]{:S(2)}) collective-permute-start(bf16[96,3072]{1,0:T(8,128)(2,1)S(1)} %copy-done.13), channel_id=1, source_target_pairs={{0,4},{8,0},{16,8},{24,16},{28,24},{20,28},{12,20},{4,12},{1,5},{9... | collective-permute-start | bytes 1769480 | tf_op jit(solution)/shard_map/ppermute | solution.py:613
  106.1 21.8 %collective-permute-start.16 = (f32[512,128]{1,0:T(8,128)S(1)}, f32[512,128]{1,0:T(8,128)S(1)}, u32[]{:S(2)}, u32[]{:S(2)}) collective-permute-start(f32[512,128]{1,0:T(8,128)S(1)} %slice_add_fusion.3), channel_id=1, source_target_pairs={{0,2},{1,3},{2,0},{3,1},{4,6},{5,7},{6,4},{7,5},{8,10},{9,11},{10,... | collective-permute-start | bytes 786440 | tf_op jit(solution)/shard_map/ppermute | solution.py:573
  131.5 49.9 %collective-permute-start.5 = (bf16[2,256,1536]{2,1,0:T(8,128)(2,1)}, bf16[2,256,1536]{2,1,0:T(8,128)(2,1)}, u32[]{:S(2)}, u32[]{:S(2)}) collective-permute-start(bf16[2,256,1536]{2,1,0:T(8,128)(2,1)} %pad_maximum_fusion.2), channel_id=1, source_target_pairs={{0,1},{1,0},{2,3},{3,2},{4,5},{5,4},{6,7},{7,6},{8,9},{9,8},{10,11... | collective-permute-start | bytes 4718600 | tf_op jit(solution)/shard_map/ppermute | solution.py:573
  143.1 20.4 %collective-permute-start.22 = (bf16[96,3072]{1,0:T(8,128)(2,1)}, bf16[96,3072]{1,0:T(8,128)(2,1)S(1)}, u32[]{:S(2)}, u32[]{:S(2)}) collective-permute-start(bf16[96,3072]{1,0:T(8,128)(2,1)} %collective-permute-done.19.refs_0_.refs_6_), channel_id=1, source_target_pairs={{0,8},{8,16},{16,24},{24,28},{28,20},{20,12},{12,4},{4,0},{1,9},{9... | collective-permute-start | bytes 1769480 | tf_op jit(solution)/shard_map/ppermute | solution.py:613
  144.3 17.9 %collective-permute-start.23 = (bf16[96,3072]{1,0:T(8,128)(2,1)S(1)}, bf16[96,3072]{1,0:T(8,128)(2,1)S(1)}, u32[]{:S(2)}, u32[]{:S(2)}) collective-permute-start(bf16[96,3072]{1,0:T(8,128)(2,1)S(1)} %collective-permute-done.21.refs_1_.refs_7_), channel_id=1, source_target_pairs={{0,4},{8,0},{16,8},{24,16},{28,24},{20,28},{12,20},{4,12},{1,5},{9... | collective-permute-start | bytes 1769480 | tf_op jit(solution)/shard_map/ppermute | solution.py:613
  162.2 22.4 %collective-permute-start.25 = (bf16[48,3072]{1,0:T(8,128)(2,1)S(1)}, bf16[48,3072]{1,0:T(8,128)(2,1)S(1)}, u32[]{:S(2)}, u32[]{:S(2)}) collective-permute-start(bf16[48,3072]{1,0:T(8,128)(2,1)S(1)} %slice.218), channel_id=1, source_target_pairs={{0,4},{8,0},{16,8},{24,16},{28,24},{20,28},{12,20},{4,12},{1,5},{9... | collective-permute-start | bytes 884744 | tf_op jit(solution)/shard_map/ppermute | solution.py:613
  163.5 21.1 %collective-permute-start.24 = (bf16[48,3072]{1,0:T(8,128)(2,1)S(1)}, bf16[48,3072]{1,0:T(8,128)(2,1)S(1)}, u32[]{:S(2)}, u32[]{:S(2)}) collective-permute-start(bf16[48,3072]{1,0:T(8,128)(2,1)S(1)} %slice.217), channel_id=1, source_target_pairs={{0,8},{8,16},{16,24},{24,28},{28,20},{20,12},{12,4},{4,0},{1,9},{9... | collective-permute-start | bytes 884744 | tf_op jit(solution)/shard_map/ppermute | solution.py:613
  209.4 38.0 %collective-permute-start.28 = (bf16[48,3072]{1,0:T(8,128)(2,1)}, bf16[48,3072]{1,0:T(8,128)(2,1)S(1)}, u32[]{:S(2)}, u32[]{:S(2)}) collective-permute-start(bf16[48,3072]{1,0:T(8,128)(2,1)} %get-tuple-element.184), channel_id=1, source_target_pairs={{0,8},{8,16},{16,24},{24,28},{28,20},{20,12},{12,4},{4,0},{1,9},{9... | collective-permute-start | bytes 884744 | tf_op jit(solution)/shard_map/ppermute | solution.py:613
  210.5 36.9 %collective-permute-start.29 = (bf16[48,3072]{1,0:T(8,128)(2,1)}, bf16[48,3072]{1,0:T(8,128)(2,1)S(1)}, u32[]{:S(2)}, u32[]{:S(2)}) collective-permute-start(bf16[48,3072]{1,0:T(8,128)(2,1)} %get-tuple-element.183), channel_id=1, source_target_pairs={{0,4},{8,0},{16,8},{24,16},{28,24},{20,28},{12,20},{4,12},{1,5},{9... | collective-permute-start | bytes 884744 | tf_op jit(solution)/shard_map/ppermute | solution.py:613
  214.8 91.3 %collective-permute-start.26 = (bf16[2,256,1536]{2,1,0:T(8,128)(2,1)S(1)}, bf16[2,256,1536]{2,1,0:T(8,128)(2,1)}, u32[]{:S(2)}, u32[]{:S(2)}) collective-permute-start(bf16[2,256,1536]{2,1,0:T(8,128)(2,1)S(1)} %bitcast.121), channel_id=1, source_target_pairs={{0,1},{1,0},{2,3},{3,2},{4,5},{5,4},{6,7},{7,6},{8,9},{9,8},{10,11... | collective-permute-start | bytes 4718600 | tf_op jit(solution)/shard_map/ppermute | solution.py:573
  294.9 16.0 %collective-permute-start.32 = (f32[512,128]{1,0:T(8,128)S(1)}, f32[512,128]{1,0:T(8,128)}, u32[]{:S(2)}, u32[]{:S(2)}) collective-permute-start(f32[512,128]{1,0:T(8,128)S(1)} %maximum_add_fusion.1), channel_id=1, source_target_pairs={{0,1},{1,0},{2,3},{3,2},{4,5},{5,4},{6,7},{7,6},{8,9},{9,8},{10,11... | collective-permute-start | bytes 786440 | tf_op jit(solution)/shard_map/ppermute | solution.py:573
  305.3 82.3 %collective-permute-start.44 = (bf16[96,3072]{1,0:T(8,128)(2,1)}, bf16[96,3072]{1,0:T(8,128)(2,1)}, u32[]{:S(2)}, u32[]{:S(2)}) collective-permute-start(bf16[96,3072]{1,0:T(8,128)(2,1)} %hold.39), channel_id=1, source_target_pairs={{0,8},{8,16},{16,24},{24,28},{28,20},{20,12},{12,4},{4,0},{1,9},{9... | collective-permute-start | bytes 1769480 | tf_op jit(solution)/shard_map/ppermute | solution.py:613
  309.4 18.4 %collective-permute-start.27 = (bf16[1,256,1536]{2,1,0:T(8,128)(2,1)}, bf16[1,256,1536]{2,1,0:T(8,128)(2,1)}, u32[]{:S(2)}, u32[]{:S(2)}) collective-permute-start(bf16[1,256,1536]{2,1,0:T(8,128)(2,1)} %hold.32), channel_id=1, source_target_pairs={{0,2},{1,3},{2,0},{3,1},{4,6},{5,7},{6,4},{7,5},{8,10},{9,11},{10,... | collective-permute-start | bytes 2359304 | tf_op jit(solution)/shard_map/ppermute | solution.py:573
  319.0 85.7 %collective-permute-start.48 = (bf16[96,3072]{1,0:T(8,128)(2,1)}, bf16[96,3072]{1,0:T(8,128)(2,1)}, u32[]{:S(2)}, u32[]{:S(2)}) collective-permute-start(bf16[96,3072]{1,0:T(8,128)(2,1)} %hold.43), channel_id=1, source_target_pairs={{0,4},{8,0},{16,8},{24,16},{28,24},{20,28},{12,20},{4,12},{1,5},{9... | collective-permute-start | bytes 1769480 | tf_op jit(solution)/shard_map/ppermute | solution.py:613
  390.0 19.5 %collective-permute-start.45 = (bf16[96,3072]{1,0:T(8,128)(2,1)}, bf16[96,3072]{1,0:T(8,128)(2,1)}, u32[]{:S(2)}, u32[]{:S(2)}) collective-permute-start(bf16[96,3072]{1,0:T(8,128)(2,1)} %hold.40), channel_id=1, source_target_pairs={{0,8},{8,16},{16,24},{24,28},{28,20},{20,12},{12,4},{4,0},{1,9},{9... | collective-permute-start | bytes 1769480 | tf_op jit(solution)/shard_map/ppermute | solution.py:613
  393.7 22.5 %collective-permute-start.34 = (bf16[1,256,1536]{2,1,0:T(8,128)(2,1)}, bf16[1,256,1536]{2,1,0:T(8,128)(2,1)}, u32[]{:S(2)}, u32[]{:S(2)}) collective-permute-start(bf16[1,256,1536]{2,1,0:T(8,128)(2,1)} %slice.263), channel_id=1, source_target_pairs={{0,2},{1,3},{2,0},{3,1},{4,6},{5,7},{6,4},{7,5},{8,10},{9,11},{10,... | collective-permute-start | bytes 2359304 | tf_op jit(solution)/shard_map/ppermute | solution.py:573
  423.3 19.4 %all-to-all-start.2 = ((bf16[32,1,144]{2,1,0:T(2,128)(2,1)}), bf16[32,1,144]{2,1,0:T(2,128)(2,1)}, u32[]{:S(2)}, u32[]{:S(2)}) async-start(bf16[32,1,144]{2,1,0:T(2,128)(2,1)} %convert_element_type.314), calls=%async_computation.2 | async-start | bytes 65536 | tf_op jit(solution)/shard_map/all_to_all | solution.py:649
  452.1 23.0 %all-to-all-start.3 = ((f32[32,1,128]{2,1,0:T(1,128)}), f32[32,1,128]{2,1,0:T(1,128)S(1)}, u32[]{:S(2)}, u32[]{:S(2)}) async-start(f32[32,1,128]{2,1,0:T(1,128)} %broadcast_in_dim.63), calls=%async_computation.3 | async-start | bytes 32768 | tf_op jit(solution)/shard_map/all_to_all | solution.py:649
  (98 other events, 1152.2 us)

commit v3 on v2

--- a/solution.py
+++ b/solution.py
@@ -4,6 +4,7 @@
 import jax.numpy as jnp
 from jax import lax
 from jax.experimental import pallas as pl
+from jax.experimental.layout import Layout, with_layout_constraint
 from jax.experimental.pallas import tpu as pltpu
 from jax.sharding import PartitionSpec as P
 
@@ -54,8 +55,18 @@
     return pl.BlockSpec((ITEM, v.shape[1]), lambda i: (i, 0))
 
 
+def halves(tokens):
+    last = tokens // ITEM // 2 - 1
+    near = pl.BlockSpec((ITEM, D), lambda i: (jnp.minimum(i, last), 0))
+    return near, pl.BlockSpec((ITEM, D), lambda i: (jnp.maximum(i - last - 1, 0), 0))
+
+
 def fixed(v):
     return pl.BlockSpec(v.shape, lambda i: (0, 0))
+
+
+def once(v):
+    return pl.BlockSpec(v.shape, lambda i: (0, 0), pipeline_mode=pl.Buffered(1))
 
 
 ANYWHERE = pl.BlockSpec(memory_space=pl.ANY)
@@ -81,15 +92,71 @@
     )(v, *after)
 
 
+def ring_sizes(rows, size):
+    return [rows] * (size - 1) + [rows // 2] * 2
+
+
 def joined(blocks):
-    return blocks if blocks[0].shape[0] % 16 == 0 else [jnp.concatenate(blocks, axis=0)]
-
-
-def parted(blocks, count):
-    if len(blocks) == count:
+    return blocks if all(b.shape[0] % 16 == 0 for b in blocks) else [jnp.concatenate(blocks, axis=0)]
+
+
+def parted(blocks, sizes):
+    if len(blocks) == len(sizes):
         return list(blocks)
-    rows = blocks[0].shape[0] // count
-    return [blocks[0][q * rows : (q + 1) * rows] for q in range(count)]
+    ends = [sum(sizes[: k + 1]) for k in range(len(sizes))]
+    return [blocks[0][end - size : end] for end, size in zip(ends, sizes)]
+
+
+def pick(refs, item, held):
+    for p, ref in enumerate(refs):
+        @pl.when(item == p)
+        def _(ref=ref):
+            held[...] = ref[...]
+
+
+def fold_body(near_ref, came_ref, *refs):
+    keep_ref, away_ref = refs[-2:]
+    half = keep_ref.shape[0]
+    keep_ref[...] = near_ref[:half, :].astype(F32) + came_ref[:half, :].astype(F32)
+    away_ref[...] = (near_ref[half:, :].astype(F32) + came_ref[half:, :].astype(F32)).astype(BF)
+
+
+def fold(near, came, after):
+    half = near.shape[0] // 2
+    whole = pl.BlockSpec(memory_space=pltpu.VMEM)
+    return pl.pallas_call(
+        fold_body,
+        in_specs=[whole, whole] + [ANYWHERE] * len(after),
+        out_specs=[whole, whole],
+        out_shape=[shape(half, near.shape[1]), shape(half, near.shape[1], BF)],
+        compiler_params=PARAMS,
+        cost_estimate=cost(2),
+        name="fold",
+    )(near, came, *after)
+
+
+def ring_add_body(ahead_ref, behind_ref, up_ref, down_ref, *refs):
+    up, down = up_ref.shape[0], down_ref.shape[0]
+    rows = ahead_ref.shape[0]
+    to_ahead, to_behind = refs[-2:]
+    to_ahead[:up, :] = (ahead_ref[:up, :].astype(F32) + up_ref[...].astype(F32)).astype(BF)
+    to_behind[rows - down :, :] = (behind_ref[rows - down :, :].astype(F32) + down_ref[...].astype(F32)).astype(BF)
+    if up < rows:
+        to_ahead[up:, :] = ahead_ref[up:, :]
+        to_behind[: rows - down, :] = behind_ref[: rows - down, :]
+
+
+def ring_add(ahead, behind, up, down, after):
+    whole = pl.BlockSpec(memory_space=pltpu.VMEM)
+    return pl.pallas_call(
+        ring_add_body,
+        in_specs=[whole] * 4 + [ANYWHERE] * len(after),
+        out_specs=[whole, whole],
+        out_shape=[shape(*ahead.shape, BF)] * 2,
+        compiler_params=PARAMS,
+        cost_estimate=cost(2),
+        name="ring_add",
+    )(ahead, behind, up, down, *after)
 
 
 def delayed(v, k):
@@ -107,9 +174,9 @@
     return pre
 
 
-def mix_body(blocks_count, h_ref, *refs):
-    blocks = refs[: blocks_count]
-    xs_ref, u_ref, low_ref, proj_ref, stream_ref, x_ref, dt_ref, table_ref, tail = refs[-9:]
+def mix_body(items, count, mod_ref, *refs):
+    pieces, blocks = refs[:items], refs[items : items + count]
+    h_ref, xs_ref, u_ref, low_ref, proj_ref, stream_ref, x_ref, dt_ref, table_ref, tail, held = refs[-11:]
 
     @pl.when(pl.program_id(0) == 0)
     def _():
@@ -124,7 +191,14 @@
         dt_ref[...] = jnp.where(lane < R, tail[...], 0.0).astype(BF)
         table_ref[...] = tail[...].T[R:, :]
 
-    xs = right_inner(h_ref[...], stream_ref[...])
+    pick(pieces, pl.program_id(0), held)
+    x = held[...].astype(F32)
+    centered = x - jnp.mean(x, axis=1, keepdims=True)
+    normed = centered * lax.rsqrt(jnp.mean(centered * centered, axis=1, keepdims=True) + 1e-06)
+    mod = mod_ref[pl.ds(pl.program_id(0), 1), :]
+    h = (normed * (1.0 + mod[:, D : 2 * D]) + mod[:, :D]).astype(BF)
+    h_ref[...] = h
+    xs = right_inner(h, stream_ref[...])
     xs_ref[...] = xs
     pre = convolved(xs, table_ref)
     u = pre * jax.nn.sigmoid(pre)
@@ -134,31 +208,33 @@
     proj_ref[...] = product(low, x_ref[...])
 
 
-def mix(h, blocks, after):
-    tokens = h.shape[0]
+def mix(pieces, mod, blocks, after):
+    items = len(pieces)
+    tokens = items * ITEM
     blocks = joined(blocks)
     width = sum(b.shape[0] for b in blocks)
     out_shape = [
-        shape(tokens, width), shape(tokens, width), shape(tokens, width, BF), shape(tokens, LANE),
+        shape(tokens, D, BF), shape(tokens, width), shape(tokens, width), shape(tokens, width, BF), shape(tokens, LANE),
         shape(width, D, BF), shape(width, LANE, BF), shape(width, LANE, BF), shape(TABLE, width),
     ]
     return pl.pallas_call(
-        lambda *refs: mix_body(len(blocks), *refs),
-        grid=(tokens // ITEM,),
-        in_specs=[item_rows(h)] + [fixed(b) for b in blocks] + [ANYWHERE] * len(after),
-        out_specs=[item_rows(v) for v in out_shape[:4]] + [fixed(v) for v in out_shape[4:]],
+        lambda *refs: mix_body(items, len(blocks), *refs),
+        grid=(items,),
+        in_specs=[fixed(mod)] + [once(v) for v in (*pieces, *blocks)] + [ANYWHERE] * len(after),
+        out_specs=[item_rows(v) for v in out_shape[:5]] + [fixed(v) for v in out_shape[5:]],
         out_shape=out_shape,
-        scratch_shapes=[pltpu.VMEM((width, LANE), F32)],
+        scratch_shapes=[pltpu.VMEM((width, LANE), F32), pltpu.VMEM((ITEM, D), BF)],
         compiler_params=PARAMS,
-        cost_estimate=cost(6),
+        cost_estimate=cost(11),
         name="mix",
-    )(h, *blocks, *after)
-
-
-def gates_body(count, h_ref, do_ref, y_ref, *refs):
-    blocks, grads = refs[:count], refs[count + 4 : 2 * count + 4]
-    dy_ref, dz_ref, o_ref, gate_ref = refs[count : count + 4]
-    out_w, grad_gate, grad_out = refs[2 * count + 4 :]
+    )(mod, *pieces, *blocks, *after)
+
+
+def gates_body(items, count, h_ref, mod_ref, y_ref, *refs):
+    pieces, blocks = refs[:items], refs[items : items + count]
+    dy_ref, dz_ref, near_ref, far_ref, gate_ref, *grads = refs[items + count : -4]
+    out_w, grad_gate, grad_out, held = refs[-4:]
+    item = pl.program_id(0)
 
     @pl.when(pl.program_id(0) == 0)
     def _():
@@ -171,7 +247,9 @@
         grad_gate[...] = jnp.zeros_like(grad_gate)
         grad_out[...] = jnp.zeros_like(grad_out)
 
-    h, do, y = h_ref[...], do_ref[...], y_ref[...]
+    pick(pieces, item, held)
+    h, y = h_ref[...], y_ref[...]
+    do = (mod_ref[pl.ds(item, 1), 2 * D :] * held[...].astype(F32)).astype(BF)
     z = right_inner(h, gate_ref[...])
     dyg = right_inner(do, out_w[...])
     sig = jax.nn.sigmoid(z)
@@ -180,7 +258,17 @@
     mixed = (y * act).astype(BF)
     dz = (dyg * y * (sig + act * (1.0 - sig))).astype(BF)
     dz_ref[...] = dz
-    o_ref[...] = product(mixed, out_w[...]).astype(BF)
+    o = product(mixed, out_w[...]).astype(BF)
+    in_near = item < pl.num_programs(0) // 2
+
+    @pl.when(in_near)
+    def _():
+        near_ref[...] = o
+
+    @pl.when(jnp.logical_not(in_near))
+    def _():
+        far_ref[...] = o
+
     grad_gate[...] += left_outer(dz, h)
     grad_out[...] += left_outer(mixed, do)
 
@@ -194,30 +282,39 @@
             at += grad.shape[0]
 
 
-def gates(h, do, y, blocks):
+def gates(h, pieces, mod, y, blocks):
     tokens, width = y.shape
-    parts = len(blocks)
+    sizes = [b.shape[0] for b in blocks]
+    items = len(pieces)
     blocks = joined(blocks)
-    out_shape = [shape(tokens, width), shape(tokens, width, BF), shape(tokens, D, BF), shape(width, D, BF)]
+    out_shape = [
+        shape(tokens, width), shape(tokens, width, BF), shape(tokens // 2, D, BF), shape(tokens // 2, D, BF), shape(width, D, BF)
+    ]
+    near, far = halves(tokens)
     grads = [shape(*b.shape, BF) for b in blocks]
-    once = lambda v: pl.BlockSpec(v.shape, lambda i: (0, 0), pipeline_mode=pl.Buffered(1))
-    dy, dz, o, gate_full, *grads = pl.pallas_call(
-        lambda *refs: gates_body(len(blocks), *refs),
+    dy, dz, o_near, o_far, gate_full, *grads = pl.pallas_call(
+        lambda *refs: gates_body(items, len(blocks), *refs),
         grid=(tokens // ITEM,),
-        in_specs=[item_rows(h), item_rows(do), item_rows(y)] + [once(b) for b in blocks],
-        out_specs=[item_rows(v) for v in out_shape[:3]] + [fixed(out_shape[3])] + [fixed(v) for v in grads],
+        in_specs=[item_rows(h), fixed(mod), item_rows(y)] + [once(b) for b in (*pieces, *blocks)],
+        out_specs=[item_rows(v) for v in out_shape[:2]] + [near, far, fixed(out_shape[4])] + [fixed(v) for v in grads],
         out_shape=out_shape + grads,
-        scratch_shapes=[pltpu.VMEM((width, D), BF), pltpu.VMEM((width, D), F32), pltpu.VMEM((width, D), F32)],
+        scratch_shapes=[
+            pltpu.VMEM((width, D), BF), pltpu.VMEM((width, D), F32), pltpu.VMEM((width, D), F32), pltpu.VMEM((ITEM, D), BF)
+        ],
         compiler_params=PARAMS,
-        cost_estimate=cost(14),
+        cost_estimate=cost(24),
         name="gates",
-    )(h, do, y, *blocks)
-    return dy, dz, o, gate_full, parted(grads, parts)
-
-
-def mix_back_body(calls, count, h_ref, xs_ref, du_ref, ddtp_ref, low_ref, proj_ref, dproj_ref, x_ref, table_ref, *refs):
+    )(h, mod, y, *pieces, *blocks)
+    return dy, dz, o_near, o_far, gate_full, parted(grads, sizes)
+
+
+def mix_back_body(
+    calls, count, h_ref, xs_ref, du_ref, ddtp_ref, low_ref, proj_ref, dproj_ref, dz_ref,
+    x_ref, table_ref, stream_ref, gate_ref, *refs
+):
     drates, drows = refs[:calls], refs[calls : 2 * calls]
-    dxs_ref, *grads = refs[-5 - count : -4]
+    near_ref, far_ref, *grads = refs[-6 - count : -4]
+    item = pl.program_id(0)
     grad_stream, grad_x, grad_tail, rows = refs[-4:]
 
     @pl.when(pl.program_id(0) == 0)
@@ -239,7 +336,17 @@
         rows[R + k : R + k + 1, :] += jnp.sum(dpre * delayed(xs, back), axis=0, keepdims=True)
     rows[R + BIAS : R + BIAS + 1, :] += jnp.sum(dpre, axis=0, keepdims=True)
     low = dxs.astype(BF)
-    dxs_ref[...] = low
+    dh = product(low, stream_ref[...]) + product(dz_ref[...], gate_ref[...])
+    in_near = item < pl.num_programs(0) // 2
+
+    @pl.when(in_near)
+    def _():
+        near_ref[...] = dh
+
+    @pl.when(jnp.logical_not(in_near))
+    def _():
+        far_ref[...] = dh.astype(BF)
+
     grad_stream[...] += left_outer(low, h_ref[...])
     grad_x[...] += left_outer(low_ref[...], dproj)
     lane = lax.broadcasted_iota(jnp.int32, dproj.shape, 1)
@@ -262,29 +369,29 @@
             at += grad.shape[0]
 
 
-def mix_back(h, xs, du, ddtp, low, proj, dproj, x_full, table, drates, drows, parts, after):
+def mix_back(h, xs, du, ddtp, low, proj, dproj, dz, x_full, table, stream, gate, drates, drows, sizes, after):
     tokens, width = xs.shape
-    block_rows = width // parts
-    blocks = [shape(block_rows, D + SMALL, BF)] * parts if block_rows % 16 == 0 else [shape(width, D + SMALL, BF)]
-    dxs_shape = shape(tokens, width, BF)
+    aligned = all(size % 16 == 0 for size in sizes)
+    blocks = [shape(size, D + SMALL, BF) for size in (sizes if aligned else [width])]
+    near, far = halves(tokens)
     calls = len(drates)
-    dxs, *grads = pl.pallas_call(
+    dh_near, dh_far, *grads = pl.pallas_call(
         lambda *refs: mix_back_body(calls, len(blocks), *refs),
         grid=(tokens // ITEM,),
-        in_specs=[item_rows(v) for v in (h, xs, du, ddtp, low, proj, dproj)]
-        + [fixed(v) for v in (x_full, table, *drates, *drows)]
+        in_specs=[item_rows(v) for v in (h, xs, du, ddtp, low, proj, dproj, dz)]
+        + [once(v) for v in (x_full, table, stream, gate, *drates, *drows)]
         + [ANYWHERE] * len(after),
-        out_specs=[item_rows(dxs_shape)] + [fixed(v) for v in blocks],
-        out_shape=[dxs_shape] + blocks,
+        out_specs=[near, far] + [fixed(v) for v in blocks],
+        out_shape=[shape(tokens // 2, D), shape(tokens // 2, D, BF)] + blocks,
         scratch_shapes=[
             pltpu.VMEM((width, D), F32), pltpu.VMEM((width, LANE), F32), pltpu.VMEM((width, LANE), F32),
             pltpu.VMEM((LANE, width), F32),
         ],
         compiler_params=PARAMS,
-        cost_estimate=cost(8),
+        cost_estimate=cost(19),
         name="mix_back",
-    )(h, xs, du, ddtp, low, proj, dproj, x_full, table, *drates, *drows, *after)
-    return dxs, parted(grads, parts)
+    )(h, xs, du, ddtp, low, proj, dproj, dz, x_full, table, stream, gate, *drates, *drows, *after)
+    return dh_near, dh_far, parted(grads, sizes)
 
 
 def scan_prepare(proj_ref, dt_ref, table_ref, pre, rate, bc):
@@ -521,8 +628,8 @@
 
     ada, wide, small, small_t, out = grads
     update(0, ada[...])
-    update(1, wide[...])
-    update(5, out[...])
+    update(1, wide[...].astype(F32))
+    update(5, out[...].astype(F32))
 
     @pl.when(pl.program_id(0) == 0)
     def _():
@@ -569,37 +676,37 @@
     return [1 << k for k in reversed(range(size.bit_length() - 1))]
 
 
+def moved(v, axes, pairs):
+    return lax.ppermute(with_layout_constraint(v, Layout(tuple(range(v.ndim)))), axes, pairs)
+
+
 def swap(v, bit, size):
-    return lax.ppermute(v, "fsdp", [(i, i ^ bit) for i in range(size)])
+    return moved(v, "fsdp", [(i, i ^ bit) for i in range(size)])
+
+
+def tick(v, size):
+    return swap(v[:16, :LANE], 1, size)
 
 
 def group_gather(v, size):
+    blocks = [v]
     for bit in group_bits(size):
-        v = jnp.concatenate([v, swap(v, bit, size)], axis=0)
-    return v
-
-
-def group_scatter_steps(v, size, gate):
-    for bit in reversed(group_bits(size)):
-        half = v.shape[0] // 2
-        away = v[half:].astype(BF)
-        if gate:
-            away = hold(away, *gate)
-        v = v[:half].astype(F32) + swap(away, bit, size).astype(F32)
-        yield v
+        blocks += [swap(b, bit, size) for b in blocks]
+    return blocks
 
 
 def group_sum(v, size):
     bits = group_bits(size)
     half = v.shape[0] // 2
-    total = v[:half] + swap(v[half:], bits[-1], size)
+    other = swap(v[half:], bits[-1], size)
+    total = v[:half] + other
     for k, bit in enumerate(bits[:-1]):
         other = swap(total, bit, size)
         rows = other.shape[0] // (size // 2)
         total = total + jnp.concatenate(
             [other[(p ^ (1 << k)) * rows : ((p ^ (1 << k)) + 1) * rows] for p in range(size // 2)], axis=0
         )
-    return jnp.concatenate([total, swap(total, bits[-1], size)], axis=0)
+    return jnp.concatenate([total, swap(total, bits[-1], size)], axis=0), other
 
 
 def ring_order(size):
@@ -610,39 +717,47 @@
 
 def ring_move(v, way, size):
     order = ring_order(size)
-    return lax.ppermute(v, "dp", [(order[p], order[(p + way) % size]) for p in range(size)])
-
-
-def ring_gather_steps(v, size, gate):
+    return moved(v, "dp", [(order[p], order[(p + way) % size]) for p in range(size)])
+
+
+def ring_gather_steps(v, size, split):
     behind = ahead = v
     for _ in range(size // 2 - 1):
-        if gate:
-            behind, ahead = hold(behind, *gate), hold(ahead, *gate)
         behind, ahead = ring_move(behind, 1, size), ring_move(ahead, -1, size)
         yield [behind, ahead]
     cut = v.shape[0] // 2
-    if gate:
-        behind, ahead = hold(behind, *gate), hold(ahead, *gate)
-    yield [jnp.concatenate([ring_move(behind[:cut], 1, size), ring_move(ahead[cut:], -1, size)], axis=0)]
-
-
-def ring_scatter_steps(blocks, size, gate):
-    cut = blocks[0].shape[0] // 2
+    if split:
+        yield [ring_move(behind[:cut], 1, size), ring_move(ahead[cut:], -1, size)]
+    else:
+        yield [ring_move(behind, 1, size)]
+
+
+def ring_partial(blocks, step, came, after):
+    size = len(blocks) - 1
+    if step == 0:
+        return blocks[-2:]
+    away = size // 2 - step
+    ahead, behind = blocks[2 * away], blocks[2 * away - 1]
+    if all(v.shape[0] % 16 == 0 for v in came):
+        return ring_add(ahead, behind, *came, after)
     add = lambda a, b: (a.astype(F32) + b.astype(F32)).astype(BF)
-    up, down = ring_move(blocks[-1][:cut], 1, size), ring_move(blocks[-1][cut:], -1, size)
-    yield [up, down]
-    for s in range(size // 2 - 1, 0, -1):
-        ahead, behind = blocks[2 * s], blocks[2 * s - 1]
-        if s == size // 2 - 1:
-            ahead = jnp.concatenate([add(ahead[:cut], up), ahead[cut:]], axis=0)
-            behind = jnp.concatenate([behind[:cut], add(behind[cut:], down)], axis=0)
-        else:
-            ahead, behind = add(ahead, up), add(behind, down)
-        if gate:
-            ahead, behind = hold(ahead, *gate), hold(behind, *gate)
-        up, down = ring_move(ahead, 1, size), ring_move(behind, -1, size)
-        yield [up, down]
-    yield blocks[0].astype(F32) + up.astype(F32) + down.astype(F32)
+    up, down = came
+    if step == 1:
+        cut = up.shape[0]
+        return [
+            jnp.concatenate([add(ahead[:cut], up), ahead[cut:]], axis=0),
+            jnp.concatenate([behind[:-cut], add(behind[-cut:], down)], axis=0),
+        ]
+    return [add(ahead, up), add(behind, down)]
+
+
+def ring_send(partial):
+    size = lax.axis_size("dp")
+    return [ring_move(partial[0], 1, size), ring_move(partial[1], -1, size)]
+
+
+def ring_last(blocks, came):
+    return blocks[0].astype(F32) + came[0].astype(F32) + came[1].astype(F32)
 
 
 def exchange(v):
@@ -682,10 +797,10 @@
     wide = in_weight.astype(BF).T
     rows = wide.shape[0] // 2
     leaving = jnp.where(low_half, wide[rows:], wide[:rows])
-    swapped = lax.ppermute(leaving, "dp", across)
+    swapped = moved(leaving, "dp", across)
     small = jnp.concatenate([x_weight.astype(BF), dt_weight.astype(BF).T, chan_table.astype(BF).T], axis=1)
     small = jnp.pad(small, ((0, 0), (0, SMALL - small.shape[1])))
-    small = lax.ppermute(hold(small, leaving), ALL, forth)
+    small = moved(hold(small, leaving), ALL, forth)
     stream_own = jnp.concatenate([jnp.where(low_half, wide[:rows], swapped), small], axis=1)
     gate_own = jnp.where(low_half, swapped, wide[rows:])
 
@@ -693,36 +808,27 @@
     live_rows = jnp.arange(ITEM, dtype=jnp.int32)[None, :] < item_lengths[:, None]
     live = live_items[:, None] & live_rows
     dfinal_own = jnp.where(live[..., None], cotangent.reshape(count, ITEM, D), jnp.zeros((), BF))
-    x_all = group_gather(act.reshape(count, ITEM, D), n_fsdp)
-    dfinal_all = group_gather(hold(dfinal_own, x_all), n_fsdp)
+    x_all = group_gather(act.reshape(count * ITEM, D), n_fsdp)
 
     steps_all = exchange(hold(jnp.broadcast_to(time_steps[None], (devices, count)), leaving)).reshape(-1)
     cond_all = embed_time(steps_all).astype(BF)
     mod_cols = product(cond_all, ada_weight.astype(BF)).reshape(n_dp, 1, items, ada_cols)
     mod_cols = jnp.broadcast_to(mod_cols, (n_dp, n_fsdp, items, ada_cols)).reshape(devices, items, ada_cols)
-    mod = jnp.swapaxes(exchange(hold(mod_cols, stream_own)), 0, 1).reshape(n_fsdp, count, 3 * D)
-    mod = jnp.take(mod, jnp.array(offsets, jnp.int32) ^ f, axis=0).reshape(items, 1, 3 * D)
-    shift, scale, gate = mod[..., :D], mod[..., D : 2 * D], mod[..., 2 * D :]
-
-    normed, _ = normalize(x_all.astype(F32))
-    h_low = (normed * (1.0 + scale) + shift).astype(BF).reshape(tokens, D)
-    do_low = (gate * dfinal_all.astype(F32)).astype(BF).reshape(tokens, D)
-
-    stream, gate_ring = [stream_own], []
-    steps = ring_gather_steps(stream_own, n_dp, gate_ring)
-    for s in range(half):
-        stream += next(steps)
-        if s == half - 3:
-            gate_ring[:] = [x_all]
-        if s == half - 2:
-            gate_ring[:] = [h_low]
-    out_own = lax.ppermute(hold(out_weight.astype(BF), stream[half - 1]), ALL, forth)
-    rest_own = hold(jnp.concatenate([gate_own, out_own], axis=1), stream[-1])
-    rest_steps = list(ring_gather_steps(rest_own, n_dp, []))
+    mod = exchange(hold(mod_cols, tick(stream_own, n_fsdp)))
+    dfinal_all = group_gather(hold(dfinal_own.reshape(count * ITEM, D), mod), n_fsdp)
+    mod = jnp.swapaxes(mod, 0, 1).reshape(n_fsdp, count, 3 * D)
+    mod = jnp.take(mod, jnp.array(offsets, jnp.int32) ^ f, axis=0).reshape(items, 3 * D)
+
+    stream = [stream_own]
+    for came in ring_gather_steps(stream_own, n_dp, False):
+        stream += came
+    out_own = moved(hold(out_weight.astype(BF), stream[half - 1]), ALL, forth)
+    rest_own = hold(jnp.concatenate([gate_own, out_own], axis=1), tick(stream[-2], n_fsdp))
+    rest_steps = list(ring_gather_steps(rest_own, n_dp, True))
     rest = [rest_own] + sum(rest_steps, [])
 
-    xs, u, u_low, proj, stream_full, x_full, dt_full, table = mix(h_low, stream, [rest_own])
-    proj = group_sum(proj, n_fsdp)
+    h_low, xs, u, u_low, proj, stream_full, x_full, dt_full, table = mix(x_all, mod, stream, [rest_own, *dfinal_all])
+    proj, _ = group_sum(hold(proj, *rest_steps[0]), n_fsdp)
     calls = 2
     part = items // calls
     kept = []
@@ -730,73 +836,77 @@
         kept = scan_forward(i * part, part, u, proj, dt_full, table, kept, rest_steps[half // 2 - 1 + i])
     y, states = kept
 
-    dy, dz_low, o_part, gate_full, early = gates(h_low, do_low, y, rest)
-    gate_early = []
-    early_steps = ring_scatter_steps(early, n_dp, gate_early)
-    o_steps = group_scatter_steps(o_part.reshape(items, ITEM, D), n_fsdp, gate_early)
-    came = next(early_steps)
-    o_own = next(o_steps)
-    kept, drates, drows = [], [], []
-    after = list(early)
+    dy, dz_low, o_own, o_far, gate_full, early = gates(h_low, dfinal_all, mod, y, rest)
+    bits = group_bits(n_fsdp)[::-1]
+    kept, drates, drows, came, o_came = [], [], [], None, None
     for i in range(calls):
-        *kept, drate, drow = scan_backward(i * part, part, u, proj, dy, states, dt_full, table, kept, after)
+        partial = ring_partial(early, i, came, drates[-1:])
+        came = ring_send(partial)
+        *kept, drate, drow = scan_backward(
+            i * part, part, u, proj, dy, states, dt_full, table, kept, [*partial, *([] if i else [o_far])]
+        )
         drates.append(drate)
         drows.append(drow)
-        after = list(came)
-        gate_early[:] = [drate]
-        came = next(early_steps)
-        o_own = next(o_steps, o_own)
-    for o_own in o_steps:
-        pass
-    for early_sum in early_steps:
-        pass
+        if i == 0:
+            o_came = swap(o_far, bits[0], n_fsdp)
+    beside = came
+    partial = ring_partial(early, calls, came, drates[-1:])
+    came = ring_send(partial)
     du_scan, ddtp_low, dproj = kept
 
-    dproj = group_sum(dproj, n_fsdp)
-    dxs_low, late = mix_back(h_low, xs, du_scan, ddtp_low, u_low, proj, dproj, x_full, table, drates, drows, n_dp, [o_own])
-    dh = (product(dxs_low, stream_full) + product(dz_low, gate_full)).reshape(items, ITEM, D)
-    dh_steps = group_scatter_steps(dh, n_fsdp, [])
-    gate_late = []
-    late_steps = ring_scatter_steps(late, n_dp, gate_late)
-    next(late_steps)
-    dh = next(dh_steps)
-    next(late_steps)
-    gate_late[:] = [dh]
-    for dh in dh_steps:
-        pass
-    for late_sum in late_steps:
-        pass
-
-    small = lax.ppermute(late_sum[:, D:].astype(BF), ALL, back).astype(F32)
+    dproj, other = group_sum(hold(dproj, *beside), n_fsdp)
+    for bit in bits[1:]:
+        o_own, o_far = fold(o_own, o_came, [other])
+        o_came = swap(o_far, bit, n_fsdp)
+    o_own = o_own.astype(F32) + o_came.astype(F32)
+    dh, dh_far, late = mix_back(
+        h_low, xs, du_scan, ddtp_low, u_low, proj, dproj, dz_low, x_full, table, stream_full, gate_full,
+        drates, drows, ring_sizes(rows, n_dp), [o_far, *partial]
+    )
+    dh_far, *late[-2:] = [hold(v, *came, o_came) for v in (dh_far, *late[-2:])]
+    for i in range(calls + 1, half):
+        came = ring_send(ring_partial(early, i, came, late[-1:]))
+    early_sum = ring_last(early, came)
+    last_early, came, dh_came = came, None, None
+    for i in range(half):
+        if 0 < i < len(bits):
+            dh, dh_far = fold(dh, dh_came, [])
+        after = [dh_far] if i == 1 else last_early if i == 2 else [dh_came] if i == half - 1 else []
+        came = ring_send(ring_partial(late, i, came, after))
+        if i < len(bits):
+            dh_came = swap(dh_far, bits[i], n_fsdp)
+    dh = dh + dh_came.astype(F32)
+    late_sum = ring_last(late, came)
+    squares = jnp.sum(early_sum * early_sum) + jnp.sum(late_sum * late_sum)
+    small = moved(late_sum[:, D:].astype(BF), ALL, back).astype(F32)
     small_t = small[:, LANE:].T
-    out_share = lax.ppermute(early_sum[:, D:].astype(BF), ALL, back).astype(F32)
+    late_sum = late_sum[:, :D].astype(BF)
     gate_sum = early_sum[:, :D].astype(BF)
-    late_sum = hold(late_sum[:, :D].astype(BF), dh)
-    gate_moved = lax.ppermute(gate_sum, "dp", [(q, q + half) for q in range(half)])
-    late_moved = lax.ppermute(late_sum, "dp", [(q + half, q) for q in range(half)])
+    gate_moved = moved(hold(gate_sum, late_sum), "dp", [(q, q + half) for q in range(half)])
+    out_share = moved(hold(early_sum[:, D:].astype(BF), late_sum), ALL, back)
+    late_moved = moved(late_sum, "dp", [(q + half, q) for q in range(half)])
     in_share = jnp.concatenate(
         [jnp.where(low_half, late_sum, gate_moved), jnp.where(low_half, late_moved, gate_sum)], axis=0
     )
-    in_share = in_share.astype(F32)
+    dh, o_own = dh.reshape(count, ITEM, D), o_own.reshape(count, ITEM, D)
 
     x = act.astype(F32).reshape(count, ITEM, D)
     normed, inverse = normalize(x)
     dfinal = dfinal_own.astype(F32)
-    final = x + gate[:count] * o_own
+    scale, gate = mod[:count, None, D : 2 * D], mod[:count, None, 2 * D :]
+    final = x + gate * o_own
     dmod = jnp.concatenate(
         [jnp.sum(dh, axis=1), jnp.sum(dh * normed, axis=1), jnp.sum(dfinal * o_own, axis=1)], axis=1
     ).astype(BF)
-    dn = dh * (1.0 + scale[:count])
+    dn = dh * (1.0 + scale)
     act_grad = dfinal + inverse * (
         dn - jnp.mean(dn, axis=2, keepdims=True) - normed * jnp.mean(dn * normed, axis=2, keepdims=True)
     )
+    dmod = hold(dmod, late_sum)
     dmod_all = exchange(jnp.swapaxes(dmod.reshape(count, devices, ada_cols), 0, 1)).reshape(devices * count, ada_cols)
     ada_share = left_outer(dmod_all, cond_all)
 
-    shares = (ada_share, in_share, small, out_share)
-    local = F32(0.0)
-    for g in shares:
-        local = local + jnp.sum(g * g)
+    local = squares + jnp.sum(ada_share * ada_share)
     total = jnp.sum(exchange(jnp.broadcast_to(local, (devices, LANE)))[:, 0])
     grad_norm = jnp.sqrt(total)
     factor = jnp.minimum(1.0, 1.0 / (grad_norm + 1e-06))

time: 499 us -> 413 us (0.83)
  the two profiles are of different devices: /device:TPU:0 before, /device:TPU:2 now
where the time goes in v3:
time: 413 us; the launch traced here: 412 us
  Pallas kernels  188 us (46%)
  waiting for transfers between devices  93.6 us (23%)
  starting transfers between devices  79.2 us (19%)
  other arithmetic  24.1 us (6%)
  local copies, waits for them, and re-layouts  17.8 us (4%)
  between operations  7.36 us (2%)
    ppermute x56, waiting for transfers between devices, moved(): lax.ppermute(with_layout_constraint(v, Layout(tuple(range(v.ndim)))), axe...  79.6 us
    pallas_call x2, Pallas kernels, scan_backward(): pl.pallas_call(scan_backward_body, grid=(count, steps), in_specs=[tok, pl...  63.8 us
    ppermute x56, starting transfers between devices, moved(): lax.ppermute(with_layout_constraint(v, Layout(tuple(range(v.ndim)))), axe...  61.1 us
    pallas_call x2, Pallas kernels, scan_forward(): pl.pallas_call(scan_forward_body, grid=(count, steps), in_specs=[tok, pl....  33.8 us
    pallas_call x1, Pallas kernels, gates(): pl.pallas_call(lambda *refs: gates_body(items, len(blocks), *refs), grid=...  24.1 us
    pallas_call x1, Pallas kernels, mix_back(): pl.pallas_call(lambda *refs: mix_back_body(calls, len(blocks), *refs), gr...  20.7 us
    all_to_all x4, starting transfers between devices, exchange(): return lax.all_to_all(v, ALL, 0, 0, tiled=True)  18.1 us
    pallas_call x6, Pallas kernels, ring_add(): pl.pallas_call(ring_add_body, in_specs=[whole] * 4 + [ANYWHERE] * len(aft...  14.7 us
  transfers between devices with their start and end apart: 60, of which 23 were waited for; matrix products, arithmetic and copies ran while one was open for 7% of the time, Pallas kernels for 36%

profile of v3, /device:TPU:2, one launch (start us, length us, event | category | flops | bytes accessed | tf_op | source)
XLA Modules:
  0.0 411.6 jit_solution(18239130469512072618)
XLA Ops:
  10.5 5.0 %all-to-all-start = ((s32[32,1,1]{2,1,0:T(1,128)}), s32[32,1,1]{2,1,0:T(1,128)S(1)}, u32[]{:S(2)}, u32[]{:S(2)}) async-start(s32[32,1,1]{2,1,0:T(1,128)} %bitcast.43), calls=%async_computation | async-start | bytes 32768 | tf_op jit(solution)/shard_map/all_to_all | solution.py:764
  26.8 4.3 %all-to-all-start.1 = ((f32[32,4,144]{2,1,0:T(4,128)}), f32[32,4,144]{2,1,0:T(4,128)S(1)}, u32[]{:S(2)}, u32[]{:S(2)}) async-start(f32[32,4,144]{2,1,0:T(4,128)} %hold.15), calls=%async_computation.1 | async-start | bytes 262144 | tf_op jit(solution)/shard_map/all_to_all | solution.py:764
  32.1 7.7 %all-to-all-done.1.refs_0_ = f32[32,4,144]{2,1,0:T(4,128)S(1)} async-done(((f32[32,4,144]{2,1,0:T(4,128)}), f32[32,4,144]{2,1,0:T(4,128)S(1)}, u32[]{:S(2)}, u32[]{:S(2)}) %all-to-all-start.1) | async-done | bytes 73760 | tf_op jit(solution)/shard_map/all_to_all | solution.py:764
  43.3 8.3 %collective-permute-done.9.refs_9_ = bf16[96,1792]{1,0:T(8,128)(2,1)} collective-permute-done((bf16[96,1792]{1,0:T(8,128)(2,1)}, bf16[96,1792]{1,0:T(8,128)(2,1)}, u32[]{:S(2)}, u32[]{:S(2)}) %collective-permute-start.9) | collective-permute-done | bytes 344096 | tf_op jit(solution)/shard_map/ppermute | solution.py:680
  70.1 7.4 %collective-permute-done.12.refs_12_ = bf16[96,1792]{1,0:T(8,128)(2,1)S(1)} collective-permute-done((bf16[96,1792]{1,0:T(8,128)(2,1)}, bf16[96,1792]{1,0:T(8,128)(2,1)S(1)}, u32[]{:S(2)}, u32[]{:S(2)}) %collective-permute-start.12) | collective-permute-done | bytes 344096 | tf_op jit(solution)/shard_map/ppermute | solution.py:680
  78.3 11.9 %mix.1 = (bf16[1024,1536]{1,0:T(8,128)(2,1)}, f32[1024,768]{1,0:T(8,128)}, f32[1024,768]{1,0:T(8,128)}, bf16[1024,768]{1,0:T(8,128)(2,1)}, f32[1024,128]{1,0:T(8...) custom-call(f32[4,4608]{1,0:T(4,128)} %broadcast_select_fusion.6.ref, ...), custom_call_target="tpu_custom_call" | custom-call | flops 11000000512 | bytes 11000000 | tf_op jit(solution)/shard_map/mix/pallas_call | solution.py:220
  98.9 4.5 %collective-permute-done.21 = f32[512,128]{1,0:T(8,128)S(1)} collective-permute-done((f32[512,128]{1,0:T(8,128)S(1)}, f32[512,128]{1,0:T(8,128)S(1)}, u32[]{:S(2)}, u32[]{:S(2)}) %collective-permute-start.21) | collective-permute-done | bytes 262176 | tf_op jit(solution)/shard_map/ppermute | solution.py:680
  103.5 8.6 %collective-permute-done.23.refs_0_.refs_10_ = bf16[96,3072]{1,0:T(8,128)(2,1)S(1)} collective-permute-done((bf16[96,3072]{1,0:T(8,128)(2,1)}, bf16[96,3072]{1,0:T(8,128)(2,1)S(1)}, u32[]{:S(2)}, u32[]{:S(2)}) %collective-permute-start.23) | collective-permute-done | bytes 589856 | tf_op jit(solution)/shard_map/ppermute | solution.py:680
  115.5 17.0 %scan_forward.2 = (f32[1024,768]{1,0:T(8,128)}, f32[16384,768]{1,0:T(8,128)}) custom-call(f32[1024,768]{1,0:T(8,128)} %get-tuple-element.116.u_ref, f32[1024,128]{1,0:T(8,128)} %pad_maximum_fusion.2.proj_ref.refs_5_, bf16[768,128]{1,0:T(8,128)(2,1)} %get-tuple-element.118.dt_ref, f32[32,768]{1,0:T(8,128)} %get-tuple-element.119.table_ref.refs_9_, ...), custom_call_target="tpu_custom_call" | custom-call | flops 16000000000 | bytes 16000000 | tf_op jit(solution)/shard_map/scan_forward/pallas_call | solution.py:457
  135.4 16.9 %scan_forward.3 = (f32[1024,768]{1,0:T(8,128)}, f32[16384,768]{1,0:T(8,128)}) custom-call(f32[1024,768]{1,0:T(8,128)} %get-tuple-element.116.u_ref, f32[1024,128]{1,0:T(8,128)} %pad_maximum_fusion.2.proj_ref.refs_5_, bf16[768,128]{1,0:T(8,128)(2,1)} %get-tuple-element.118.dt_ref, ...), custom_call_target="tpu_custom_call", output_to_operand_aliasing={{0}: (4, {}), {1}: (5, {})} | custom-call | flops 16000000000 | bytes 16000000 | tf_op jit(solution)/shard_map/scan_forward/pallas_call | solution.py:457
  153.1 24.1 %gates.1 = (f32[1024,768]{1,0:T(8,128)}, bf16[1024,768]{1,0:T(8,128)(2,1)}, bf16[512,1536]{1,0:T(8,128)(2,1)}, bf16[512,1536]{1,0:T(8,128)(2,1)}, bf16[768,1536]...) custom-call(bf16[1024,1536]{1,0:T(8,128)(2,1)} %get-tuple-element.11, ...), custom_call_target="tpu_custom_call" | custom-call | flops 24000000000 | bytes 24000000 | tf_op jit(solution)/shard_map/gates/pallas_call | solution.py:295
  179.3 31.9 %scan_backward.2 = (f32[1024,768]{1,0:T(8,128)}, bf16[1024,768]{1,0:T(8,128)(2,1)}, f32[1024,128]{1,0:T(8,128)}, f32[16,768]{1,0:T(8,128)}, f32[16,768]{1,0:T(8,128)}) custom-call(f32[1024,768]{1,0:T(8,128)} %get-tuple-element.116.u_ref, f32[1024,128]{1,0:T(8,128)} %pad_maximum_fusion.2.proj_ref.refs_5_, f32[1024,768]{1,0:T(8,128)} %get-tuple-element.125.dy_ref, ...), custom_call_target="tpu_custom_call" | custom-call | flops 30000001024 | bytes 30000000 | tf_op jit(solution)/shard_map/scan_backward/pallas_call | solution.py:586
  216.6 31.9 %scan_backward.3 = (f32[1024,768]{1,0:T(8,128)}, bf16[1024,768]{1,0:T(8,128)(2,1)}, f32[1024,128]{1,0:T(8,128)}, f32[16,768]{1,0:T(8,128)}, f32[16,768]{1,0:T(8,128)}) custom-call(f32[1024,768]{1,0:T(8,128)} %get-tuple-element.116.u_ref, f32[1024,128]{1,0:T(8,128)} %pad_maximum_fusion.2.proj_ref.refs_5_, ...), custom_call_target="tpu_custom_call", output_to_operand_aliasing={{0}: (7, {}), {1}: (8, {}), {2}: (9, {})} | custom-call | flops 30000001024 | bytes 30000000 | tf_op jit(solution)/shard_map/scan_backward/pallas_call | solution.py:586
  253.4 8.0 %collective-permute-done.35.refs_0_ = f32[512,128]{1,0:T(8,128)S(1)} collective-permute-done((f32[512,128]{1,0:T(8,128)S(1)}, f32[512,128]{1,0:T(8,128)S(1)}, u32[]{:S(2)}, u32[]{:S(2)}) %collective-permute-start.35) | collective-permute-done | bytes 262176 | tf_op jit(solution)/shard_map/ppermute | solution.py:680
  271.0 20.7 %mix_back.1 = (f32[512,1536]{1,0:T(8,128)}, bf16[512,1536]{1,0:T(8,128)(2,1)}, bf16[96,1792]{1,0:T(8,128)(2,1)}, bf16[96,1792]{1,0:T(8,128)(2,1)}, bf16[96,1792]...) custom-call(bf16[1024,1536]{1,0:T(8,128)(2,1)} %get-tuple-element.11, ...), custom_call_target="tpu_custom_call" | custom-call | flops 19000000512 | bytes 19000000 | tf_op jit(solution)/shard_map/mix_back/pallas_call | solution.py:378
  299.8 3.9 fold.3
  310.5 3.6 collective-permute-done.42.refs_0_
  316.1 4.6 %collective-permute-done.46.up_ref = bf16[96,1792]{1,0:T(8,128)(2,1)S(1)} collective-permute-done((bf16[96,1792]{1,0:T(8,128)(2,1)}, bf16[96,1792]{1,0:T(8,128)(2,1)S(1)}, u32[]{:S(2)}, u32[]{:S(2)}) %collective-permute-start.46) | collective-permute-done | bytes 344096 | tf_op jit(solution)/shard_map/ppermute | solution.py:680
  327.7 5.8 %collective-permute-done.48.up_ref = bf16[96,1792]{1,0:T(8,128)(2,1)S(1)} collective-permute-done((bf16[96,1792]{1,0:T(8,128)(2,1)}, bf16[96,1792]{1,0:T(8,128)(2,1)S(1)}, u32[]{:S(2)}, u32[]{:S(2)}) %collective-permute-start.48) | collective-permute-done | bytes 344096 | tf_op jit(solution)/shard_map/ppermute | solution.py:680
  342.2 4.2 %fusion.10 = (bf16[1536]{0:T(1024)(128)(2,1)S(1)}, f32[256,1536]{1,0:T(8,128)}, f32[256,1536]{1,0:T(8,128)}) fusion(f32[256,1536]{1,0:T(8,128)} %get-tuple-element.138, bf16[256,1536]{1,0:T(8,128)(2,1)S(1)} %copy-done.3, f32[1536]{0:T(1024)S(1)} %get-tuple-element.208, bf16[256,1536]{1,0:T(8,128)(2,1)S(1)} %copy-done.1, f32[256]{0:T(256)S(1)} %get-tuple-element.231, ...), kind=kLoop, calls=%fused_computation.16 | loop fusion | flops 7469568 | bytes 9456896 | tf_op jit(solution)/shard_map/reduce_sum | solution.py:899
  351.0 6.2 %all-to-all-start.2 = ((bf16[32,1,144]{2,1,0:T(2,128)(2,1)}), bf16[32,1,144]{2,1,0:T(2,128)(2,1)S(1)}, u32[]{:S(2)}, u32[]{:S(2)}) async-start(bf16[32,1,144]{2,1,0:T(2,128)(2,1)} %transpose_reshape.4), calls=%async_computation.2 | async-start | bytes 65536 | tf_op jit(solution)/shard_map/all_to_all | solution.py:764
  372.8 4.3 %collective-permute-start.52 = (bf16[96,1536]{1,0:T(8,128)(2,1)}, bf16[96,1536]{1,0:T(8,128)(2,1)S(1)}, u32[]{:S(2)}, u32[]{:S(2)}) collective-permute-start(bf16[96,1536]{1,0:T(8,128)(2,1)} %hold.26), channel_id=1, source_target_pairs={{0,16},{4,20},{8,24},{12,28},{1,17},{5,21},{9,25},{13,29},{2,18},{... | collective-permute-start | bytes 884744 | tf_op jit(solution)/shard_map/ppermute | solution.py:680
  385.0 13.6 %collective-permute-done.55.refs_4_ = bf16[96,1536]{1,0:T(8,128)(2,1)S(1)} collective-permute-done((bf16[96,1536]{1,0:T(8,128)(2,1)}, bf16[96,1536]{1,0:T(8,128)(2,1)S(1)}, u32[]{:S(2)}, u32[]{:S(2)}) %collective-permute-start.55) | collective-permute-done | bytes 294944 | tf_op jit(solution)/shard_map/ppermute | solution.py:680
  399.3 11.2 %update.1 = (f32[144,1536]{1,0:T(8,128)}, f32[144,1536]{1,0:T(8,128)}, f32[144,1536]{1,0:T(8,128)}, f32[144,1536]{1,0:T(8,128)}, f32[192,1536]{1,0:T(8,128)}, /*...) custom-call(f32[1,1]{1,0:T(1,128)} %bitcast.10.factor_ref, ...), custom_call_target="tpu_custom_call" | custom-call | flops 11000000512 | bytes 11000000 | tf_op jit(solution)/shard_map/update/pallas_call | solution.py:647
  (311 shorter events, 138.8 us)
Async XLA Ops:
  2.3 20.9 %collective-permute-start = (bf16[96,1536]{1,0:T(8,128)(2,1)S(1)}, bf16[96,1536]{1,0:T(8,128)(2,1)S(1)}, u32[]{:S(2)}, u32[]{:S(2)}) collective-permute-start(bf16[96,1536]{1,0:T(8,128)(2,1)S(1)} %broadcast_select_fusion.5.refs_0_), channel_id=1, source_target_pairs={{0,16},{4,20},{8,24},{12,28},{16,0},{20,4},{24,8},{28,12},{1,17},{... | collective-permute-start | bytes 884744 | tf_op jit(solution)/shard_map/ppermute | solution.py:680
  5.9 17.4 %collective-permute-start.5 = (bf16[96,256]{1,0:T(8,128)(2,1)}, bf16[96,256]{1,0:T(8,128)(2,1)S(1)}, u32[]{:S(2)}, u32[]{:S(2)}) collective-permute-start(bf16[96,256]{1,0:T(8,128)(2,1)} %hold.16), channel_id=1, source_target_pairs={{0,0},{1,16},{2,1},{3,17},{4,2},{5,18},{6,3},{7,19},{8,4},{9,20},{... | collective-permute-start | bytes 147464 | tf_op jit(solution)/shard_map/ppermute | solution.py:680
  15.5 46.3 %collective-permute-start.2 = (bf16[256,1536]{1,0:T(8,128)(2,1)S(1)}, bf16[256,1536]{1,0:T(8,128)(2,1)}, u32[]{:S(2)}, u32[]{:S(2)}) collective-permute-start(bf16[256,1536]{1,0:T(8,128)(2,1)S(1)} %copy-done), channel_id=1, source_target_pairs={{0,2},{1,3},{2,0},{3,1},{4,6},{5,7},{6,4},{7,5},{8,10},{9,11},{10,... | collective-permute-start | bytes 2359304 | tf_op jit(solution)/shard_map/ppermute | solution.py:680
  24.0 18.1 %collective-permute-start.6 = (bf16[96,1792]{1,0:T(8,128)(2,1)}, bf16[96,1792]{1,0:T(8,128)(2,1)}, u32[]{:S(2)}, u32[]{:S(2)}) collective-permute-start(bf16[96,1792]{1,0:T(8,128)(2,1)} %pad_maximum_fusion.4.refs_5_), channel_id=1, source_target_pairs={{0,8},{8,16},{16,24},{24,28},{28,20},{20,12},{12,4},{4,0},{1,9},{9... | collective-permute-start | bytes 1032200 | tf_op jit(solution)/shard_map/ppermute | solution.py:680
  40.5 21.9 %collective-permute-start.15 = (bf16[256,1536]{1,0:T(8,128)(2,1)}, bf16[256,1536]{1,0:T(8,128)(2,1)}, u32[]{:S(2)}, u32[]{:S(2)}) collective-permute-start(bf16[256,1536]{1,0:T(8,128)(2,1)} %hold.19.refs_14_.refs_3_), channel_id=1, source_target_pairs={{0,2},{1,3},{2,0},{3,1},{4,6},{5,7},{6,4},{7,5},{8,10},{9,11},{10,... | collective-permute-start | bytes 2359304 | tf_op jit(solution)/shard_map/ppermute | solution.py:680
  67.4 22.8 %collective-permute-start.18 = (bf16[96,3072]{1,0:T(8,128)(2,1)}, bf16[96,3072]{1,0:T(8,128)(2,1)S(1)}, u32[]{:S(2)}, u32[]{:S(2)}) collective-permute-start(bf16[96,3072]{1,0:T(8,128)(2,1)} %hold.18.refs_13_.refs_7_), channel_id=1, source_target_pairs={{0,8},{8,16},{16,24},{24,28},{28,20},{20,12},{12,4},{4,0},{1,9},{9... | collective-permute-start | bytes 1769480 | tf_op jit(solution)/shard_map/ppermute | solution.py:680
  70.1 20.1 %collective-permute-start.19 = (bf16[96,3072]{1,0:T(8,128)(2,1)}, bf16[96,3072]{1,0:T(8,128)(2,1)S(1)}, u32[]{:S(2)}, u32[]{:S(2)}) collective-permute-start(bf16[96,3072]{1,0:T(8,128)(2,1)} %hold.18.refs_13_.refs_7_), channel_id=1, source_target_pairs={{0,4},{8,0},{16,8},{24,16},{28,24},{20,28},{12,20},{4,12},{1,5},{9... | collective-permute-start | bytes 1769480 | tf_op jit(solution)/shard_map/ppermute | solution.py:680
  112.1 20.4 %collective-permute-start.25 = (bf16[96,3072]{1,0:T(8,128)(2,1)S(1)}, bf16[96,3072]{1,0:T(8,128)(2,1)S(1)}, u32[]{:S(2)}, u32[]{:S(2)}) collective-permute-start(bf16[96,3072]{1,0:T(8,128)(2,1)S(1)} %collective-permute-done.23.refs_0_.refs_10_), channel_id=1, source_target_pairs={{0,8},{8,16},{16,24},{24,28},{28,20},{20,12},{12,4},{4,0},{1,9},{9... | collective-permute-start | bytes 1769480 | tf_op jit(solution)/shard_map/ppermute | solution.py:680
  114.5 20.1 %collective-permute-start.26 = (bf16[96,3072]{1,0:T(8,128)(2,1)S(1)}, bf16[96,3072]{1,0:T(8,128)(2,1)S(1)}, u32[]{:S(2)}, u32[]{:S(2)}) collective-permute-start(bf16[96,3072]{1,0:T(8,128)(2,1)S(1)} %collective-permute-done.24.refs_1_.refs_11_), channel_id=1, source_target_pairs={{0,4},{8,0},{16,8},{24,16},{28,24},{20,28},{12,20},{4,12},{1,5},{9... | collective-permute-start | bytes 1769480 | tf_op jit(solution)/shard_map/ppermute | solution.py:680
  132.5 19.8 %collective-permute-start.27 = (bf16[48,3072]{1,0:T(8,128)(2,1)S(1)}, bf16[48,3072]{1,0:T(8,128)(2,1)S(1)}, u32[]{:S(2)}, u32[]{:S(2)}) collective-permute-start(bf16[48,3072]{1,0:T(8,128)(2,1)S(1)} %slice.109), channel_id=1, source_target_pairs={{0,8},{8,16},{16,24},{24,28},{28,20},{20,12},{12,4},{4,0},{1,9},{9... | collective-permute-start | bytes 884744 | tf_op jit(solution)/shard_map/ppermute | solution.py:680
  134.6 17.7 %collective-permute-start.28 = (bf16[48,3072]{1,0:T(8,128)(2,1)S(1)}, bf16[48,3072]{1,0:T(8,128)(2,1)S(1)}, u32[]{:S(2)}, u32[]{:S(2)}) collective-permute-start(bf16[48,3072]{1,0:T(8,128)(2,1)S(1)} %slice.110), channel_id=1, source_target_pairs={{0,4},{8,0},{16,8},{24,16},{28,24},{20,28},{12,20},{4,12},{1,5},{9... | collective-permute-start | bytes 884744 | tf_op jit(solution)/shard_map/ppermute | solution.py:680
  177.2 34.0 %collective-permute-start.30 = (bf16[48,3072]{1,0:T(8,128)(2,1)}, bf16[48,3072]{1,0:T(8,128)(2,1)S(1)}, u32[]{:S(2)}, u32[]{:S(2)}) collective-permute-start(bf16[48,3072]{1,0:T(8,128)(2,1)} %get-tuple-element.127.refs_0_), channel_id=1, source_target_pairs={{0,8},{8,16},{16,24},{24,28},{28,20},{20,12},{12,4},{4,0},{1,9},{9... | collective-permute-start | bytes 884744 | tf_op jit(solution)/shard_map/ppermute | solution.py:680
  179.2 32.0 %collective-permute-start.31 = (bf16[48,3072]{1,0:T(8,128)(2,1)}, bf16[48,3072]{1,0:T(8,128)(2,1)S(1)}, u32[]{:S(2)}, u32[]{:S(2)}) collective-permute-start(bf16[48,3072]{1,0:T(8,128)(2,1)} %get-tuple-element.128.refs_1_), channel_id=1, source_target_pairs={{0,4},{8,0},{16,8},{24,16},{28,24},{20,28},{12,20},{4,12},{1,5},{9... | collective-permute-start | bytes 884744 | tf_op jit(solution)/shard_map/ppermute | solution.py:680
  179.3 87.1 %collective-permute-start.29 = (bf16[512,1536]{1,0:T(8,128)(2,1)}, bf16[512,1536]{1,0:T(8,128)(2,1)}, u32[]{:S(2)}, u32[]{:S(2)}) collective-permute-start(bf16[512,1536]{1,0:T(8,128)(2,1)} %get-tuple-element.124.refs_2_), channel_id=1, source_target_pairs={{0,1},{1,0},{2,3},{3,2},{4,5},{5,4},{6,7},{7,6},{8,9},{9,8},{10,11... | collective-permute-start | bytes 4718600 | tf_op jit(solution)/shard_map/ppermute | solution.py:680
  214.5 33.9 %collective-permute-start.32 = (bf16[96,3072]{1,0:T(8,128)(2,1)}, bf16[96,3072]{1,0:T(8,128)(2,1)S(1)}, u32[]{:S(2)}, u32[]{:S(2)}) collective-permute-start(bf16[96,3072]{1,0:T(8,128)(2,1)} %get-tuple-element.135.refs_3_), channel_id=1, source_target_pairs={{0,8},{8,16},{16,24},{24,28},{28,20},{20,12},{12,4},{4,0},{1,9},{9... | collective-permute-start | bytes 1769480 | tf_op jit(solution)/shard_map/ppermute | solution.py:680
  216.4 32.0 %collective-permute-start.33 = (bf16[96,3072]{1,0:T(8,128)(2,1)}, bf16[96,3072]{1,0:T(8,128)(2,1)S(1)}, u32[]{:S(2)}, u32[]{:S(2)}) collective-permute-start(bf16[96,3072]{1,0:T(8,128)(2,1)} %get-tuple-element.136.refs_4_), channel_id=1, source_target_pairs={{0,4},{8,0},{16,8},{24,16},{28,24},{20,28},{12,20},{4,12},{1,5},{9... | collective-permute-start | bytes 1769480 | tf_op jit(solution)/shard_map/ppermute | solution.py:680
  264.3 27.4 %collective-permute-start.38 = (bf16[96,3072]{1,0:T(8,128)(2,1)}, bf16[96,3072]{1,0:T(8,128)(2,1)S(1)}, u32[]{:S(2)}, u32[]{:S(2)}) collective-permute-start(bf16[96,3072]{1,0:T(8,128)(2,1)} %get-tuple-element.153.refs_17_), channel_id=1, source_target_pairs={{0,8},{8,16},{16,24},{24,28},{28,20},{20,12},{12,4},{4,0},{1,9},{9... | collective-permute-start | bytes 1769480 | tf_op jit(solution)/shard_map/ppermute | solution.py:680
  266.2 25.5 %collective-permute-start.39 = (bf16[96,3072]{1,0:T(8,128)(2,1)}, bf16[96,3072]{1,0:T(8,128)(2,1)S(1)}, u32[]{:S(2)}, u32[]{:S(2)}) collective-permute-start(bf16[96,3072]{1,0:T(8,128)(2,1)} %get-tuple-element.154.refs_18_), channel_id=1, source_target_pairs={{0,4},{8,0},{16,8},{24,16},{28,24},{20,28},{12,20},{4,12},{1,5},{9... | collective-permute-start | bytes 1769480 | tf_op jit(solution)/shard_map/ppermute | solution.py:680
  269.8 21.9 %collective-permute-start.36 = (bf16[256,1536]{1,0:T(8,128)(2,1)}, bf16[256,1536]{1,0:T(8,128)(2,1)S(1)}, u32[]{:S(2)}, u32[]{:S(2)}) collective-permute-start(bf16[256,1536]{1,0:T(8,128)(2,1)} %get-tuple-element.139.refs_16_), channel_id=1, source_target_pairs={{0,2},{1,3},{2,0},{3,1},{4,6},{5,7},{6,4},{7,5},{8,10},{9,11},{10,... | collective-permute-start | bytes 2359304 | tf_op jit(solution)/shard_map/ppermute | solution.py:680
  297.7 16.4 %collective-permute-start.42 = (bf16[96,3072]{1,0:T(8,128)(2,1)}, bf16[96,3072]{1,0:T(8,128)(2,1)S(1)}, u32[]{:S(2)}, u32[]{:S(2)}) collective-permute-start(bf16[96,3072]{1,0:T(8,128)(2,1)} %get-tuple-element.163), channel_id=1, source_target_pairs={{0,8},{8,16},{16,24},{24,28},{28,20},{20,12},{12,4},{4,0},{1,9},{9... | collective-permute-start | bytes 1769480 | tf_op jit(solution)/shard_map/ppermute | solution.py:680
  299.6 16.4 %collective-permute-start.43 = (bf16[96,3072]{1,0:T(8,128)(2,1)}, bf16[96,3072]{1,0:T(8,128)(2,1)S(1)}, u32[]{:S(2)}, u32[]{:S(2)}) collective-permute-start(bf16[96,3072]{1,0:T(8,128)(2,1)} %get-tuple-element.164), channel_id=1, source_target_pairs={{0,4},{8,0},{16,8},{24,16},{28,24},{20,28},{12,20},{4,12},{1,5},{9... | collective-permute-start | bytes 1769480 | tf_op jit(solution)/shard_map/ppermute | solution.py:680
  308.8 25.8 %collective-permute-start.41 = (bf16[256,1536]{1,0:T(8,128)(2,1)S(1)}, bf16[256,1536]{1,0:T(8,128)(2,1)S(1)}, u32[]{:S(2)}, u32[]{:S(2)}) collective-permute-start(bf16[256,1536]{1,0:T(8,128)(2,1)S(1)} %copy-done.44), channel_id=1, source_target_pairs={{0,2},{1,3},{2,0},{3,1},{4,6},{5,7},{6,4},{7,5},{8,10},{9,11},{10,... | collective-permute-start | bytes 2359304 | tf_op jit(solution)/shard_map/ppermute | solution.py:680
  348.0 24.0 %collective-permute-start.53 = (bf16[96,1536]{1,0:T(8,128)(2,1)S(1)}, bf16[96,1536]{1,0:T(8,128)(2,1)S(1)}, u32[]{:S(2)}, u32[]{:S(2)}) collective-permute-start(bf16[96,1536]{1,0:T(8,128)(2,1)S(1)} %slice.116.refs_0_), channel_id=1, source_target_pairs={{16,0},{20,4},{24,8},{28,12},{17,1},{21,5},{25,9},{29,13},{18,2},{... | collective-permute-start | bytes 884744 | tf_op jit(solution)/shard_map/ppermute | solution.py:680
  379.9 18.7 %collective-permute-start.55 = (bf16[96,1536]{1,0:T(8,128)(2,1)}, bf16[96,1536]{1,0:T(8,128)(2,1)S(1)}, u32[]{:S(2)}, u32[]{:S(2)}) collective-permute-start(bf16[96,1536]{1,0:T(8,128)(2,1)} %hold.27), channel_id=1, source_target_pairs={{0,0},{16,1},{1,2},{17,3},{2,4},{18,5},{3,6},{19,7},{4,8},{20,9},{... | collective-permute-start | bytes 884744 | tf_op jit(solution)/shard_map/ppermute | solution.py:680
  (94 other events, 656.3 us)

commit v4 on v3

--- a/solution.py
+++ b/solution.py
@@ -231,9 +231,10 @@
 
 
 def gates_body(items, count, h_ref, mod_ref, y_ref, *refs):
+    here = pl.ds(pl.multiple_of(pl.program_id(0) * ITEM, ITEM), ITEM)
     pieces, blocks = refs[:items], refs[items : items + count]
     dy_ref, dz_ref, near_ref, far_ref, gate_ref, *grads = refs[items + count : -4]
-    out_w, grad_gate, grad_out, held = refs[-4:]
+    out_w, all_dz, all_mixed, all_do = refs[-4:]
     item = pl.program_id(0)
 
     @pl.when(pl.program_id(0) == 0)
@@ -244,12 +245,11 @@
             gate_ref[rows, :] = block[:, :D]
             out_w[rows, :] = block[:, D:]
             at += block.shape[0]
-        grad_gate[...] = jnp.zeros_like(grad_gate)
-        grad_out[...] = jnp.zeros_like(grad_out)
-
-    pick(pieces, item, held)
-    h, y = h_ref[...], y_ref[...]
-    do = (mod_ref[pl.ds(item, 1), 2 * D :] * held[...].astype(F32)).astype(BF)
+
+    pick(pieces, item, all_do.at[here])
+    h, y = h_ref[here, :], y_ref[...]
+    do = (mod_ref[pl.ds(item, 1), 2 * D :] * all_do[here, :].astype(F32)).astype(BF)
+    all_do[here, :] = do
     z = right_inner(h, gate_ref[...])
     dyg = right_inner(do, out_w[...])
     sig = jax.nn.sigmoid(z)
@@ -258,6 +258,8 @@
     mixed = (y * act).astype(BF)
     dz = (dyg * y * (sig + act * (1.0 - sig))).astype(BF)
     dz_ref[...] = dz
+    all_dz[here, :] = dz
+    all_mixed[here, :] = mixed
     o = product(mixed, out_w[...]).astype(BF)
     in_near = item < pl.num_programs(0) // 2
 
@@ -269,17 +271,14 @@
     def _():
         far_ref[...] = o
 
-    grad_gate[...] += left_outer(dz, h)
-    grad_out[...] += left_outer(mixed, do)
-
     @pl.when(pl.program_id(0) == pl.num_programs(0) - 1)
     def _():
-        at = 0
-        for grad in grads:
-            rows = slice(at, at + grad.shape[0])
-            grad[:, :D] = grad_gate[rows, :].astype(BF)
-            grad[:, D:] = grad_out[rows, :].astype(BF)
-            at += grad.shape[0]
+        for lanes, left, right in ((slice(D), all_dz, h_ref), (slice(D, 2 * D), all_mixed, all_do)):
+            total = left_outer(left[...], right[...]).astype(BF)
+            at = 0
+            for grad in grads:
+                grad[:, lanes] = total[at : at + grad.shape[0], :]
+                at += grad.shape[0]
 
 
 def gates(h, pieces, mod, y, blocks):
@@ -295,11 +294,12 @@
     dy, dz, o_near, o_far, gate_full, *grads = pl.pallas_call(
         lambda *refs: gates_body(items, len(blocks), *refs),
         grid=(tokens // ITEM,),
-        in_specs=[item_rows(h), fixed(mod), item_rows(y)] + [once(b) for b in (*pieces, *blocks)],
+        in_specs=[once(h), fixed(mod), item_rows(y)] + [once(b) for b in (*pieces, *blocks)],
         out_specs=[item_rows(v) for v in out_shape[:2]] + [near, far, fixed(out_shape[4])] + [fixed(v) for v in grads],
         out_shape=out_shape + grads,
         scratch_shapes=[
-            pltpu.VMEM((width, D), BF), pltpu.VMEM((width, D), F32), pltpu.VMEM((width, D), F32), pltpu.VMEM((ITEM, D), BF)
+            pltpu.VMEM((width, D), BF), pltpu.VMEM((tokens, width), BF), pltpu.VMEM((tokens, width), BF),
+            pltpu.VMEM((tokens, D), BF),
         ],
         compiler_params=PARAMS,
         cost_estimate=cost(24),
@@ -394,8 +394,10 @@
     return dh_near, dh_far, parted(grads, sizes)
 
 
-def scan_prepare(proj_ref, dt_ref, table_ref, pre, rate, bc):
+def scan_prepare(u_ref, proj_ref, dt_ref, table_ref, pre, step, drive, rate, bc):
     pre[...] = right_inner(proj_ref[...].astype(BF), dt_ref[...]) + table_ref[STEP_BIAS : STEP_BIAS + 1, :]
+    step[...] = softplus(pre[...])
+    drive[...] = step[...] * u_ref[...]
     rate[...] = -jnp.exp(table_ref[RATE:CH, :]) * LOG2E
     turned = proj_ref[...].T
     for g in range(bc.shape[0]):
@@ -403,7 +405,7 @@
 
 
 def scan_forward_body(u_ref, proj_ref, dt_ref, table_ref, *refs):
-    y_ref, states_ref, pre, rate_ref, bc_ref, carry, parts = refs[-7:]
+    y_ref, states_ref, pre, step_ref, drive_ref, rate_ref, bc_ref, carry, parts = refs[-9:]
     groups = u_ref.shape[0] // SUB
     chunks = u_ref.shape[1] // LANE
 
@@ -411,13 +413,12 @@
     def _():
         carry[...] = jnp.zeros_like(carry)
 
-    scan_prepare(proj_ref, dt_ref, table_ref, pre, rate_ref, bc_ref)
+    scan_prepare(u_ref, proj_ref, dt_ref, table_ref, pre, step_ref, drive_ref, rate_ref, bc_ref)
 
     def group(g, _):
         base = pl.multiple_of(g * SUB, SUB)
-        u8 = u_ref[pl.ds(base, SUB), :]
-        step8 = softplus(pre[pl.ds(base, SUB), :])
-        drive8 = step8 * u8
+        step8 = step_ref[pl.ds(base, SUB), :]
+        drive8 = drive_ref[pl.ds(base, SUB), :]
         bc = bc_ref[g]
         states = [carry[:, c * LANE : (c + 1) * LANE] for c in range(chunks)]
         for j in range(SUB):
@@ -432,17 +433,19 @@
                 states[c] = s
                 states_ref[pl.ds(at, N), lanes] = s
                 p = cc * s
-                parts[c, j * SUB : (j + 1) * SUB, :] = p[:SUB] + p[SUB:]
+                parts[c, pl.ds(pl.multiple_of((base + j) * SUB, SUB), SUB), :] = p[:SUB] + p[SUB:]
         for c in range(chunks):
             lanes = slice(c * LANE, (c + 1) * LANE)
             carry[:, lanes] = states[c]
-            total = table_ref[SKIP : SKIP + 1, lanes] * u8[:, lanes]
-            for n in range(SUB):
-                total = total + parts[c, pl.ds(n, SUB, stride=SUB), :]
-            y_ref[pl.ds(base, SUB), lanes] = total
         return 0
 
     lax.fori_loop(0, groups, group, 0)
+    for c in range(chunks):
+        lanes = slice(c * LANE, (c + 1) * LANE)
+        total = table_ref[SKIP : SKIP + 1, lanes] * u_ref[:, lanes]
+        for n in range(SUB):
+            total = total + parts[c, pl.ds(n, groups * SUB, stride=SUB), :]
+        y_ref[:, lanes] = total
 
 
 def scan_forward(begin, count, u, proj, dt, table, kept, after):
@@ -461,8 +464,9 @@
         out_specs=[tok, pl.BlockSpec((block * N, width), at)],
         out_shape=[shape(total, width), shape(total * N, width)],
         scratch_shapes=[
-            pltpu.VMEM((block, width), F32), pltpu.VMEM((N, width), F32), pltpu.VMEM((block // SUB, 2 * N, LANE), F32),
-            pltpu.VMEM((N, width), F32), pltpu.VMEM((chunks, SUB * SUB, LANE), F32),
+            *[pltpu.VMEM((block, width), F32)] * 3, pltpu.VMEM((N, width), F32),
+            pltpu.VMEM((block // SUB, 2 * N, LANE), F32),
+            pltpu.VMEM((N, width), F32), pltpu.VMEM((chunks, block * SUB, LANE), F32),
         ],
         input_output_aliases={4 + k: k for k in range(len(kept))},
         compiler_params=PARAMS,
@@ -472,8 +476,8 @@
 
 
 def scan_backward_body(u_ref, proj_ref, dy_ref, states_ref, before_ref, dt_ref, table_ref, *refs):
-    du_ref, ddtp_ref, dproj_ref, drate_ref, drow_ref = refs[-15:-10]
-    pre, rate_ref, bc_ref, ddtp, carry, parts, parts2, sums, stage, own = refs[-10:]
+    du_ref, ddtp_ref, dproj_ref, drate_ref, drow_ref = refs[-16:-11]
+    pre, step_ref, drive_ref, rate_ref, bc_ref, carry, parts, parts2, sums, stage, own = refs[-11:]
     block = u_ref.shape[0]
     groups = block // SUB
     chunks = u_ref.shape[1] // LANE
@@ -489,15 +493,13 @@
         drate_ref[...] = jnp.zeros_like(drate_ref)
         drow_ref[...] = jnp.zeros_like(drow_ref)
 
-    scan_prepare(proj_ref, dt_ref, table_ref, pre, rate_ref, bc_ref)
+    scan_prepare(u_ref, proj_ref, dt_ref, table_ref, pre, step_ref, drive_ref, rate_ref, bc_ref)
 
     def group(k, _):
         g = groups - 1 - k
         base = pl.multiple_of(g * SUB, SUB)
-        u8 = u_ref[pl.ds(base, SUB), :]
-        pre8 = pre[pl.ds(base, SUB), :]
-        step8 = softplus(pre8)
-        drive8 = step8 * u8
+        step8 = step_ref[pl.ds(base, SUB), :]
+        drive8 = drive_ref[pl.ds(base, SUB), :]
         dy8 = dy_ref[pl.ds(base, SUB), :]
         bc = bc_ref[g]
         grads = [carry[:, c * LANE : (c + 1) * LANE] for c in range(chunks)]
@@ -525,12 +527,12 @@
                 dc = dc + now * dy
                 db = db + grad * drive
                 p = grad * b
-                parts[c, j * SUB : (j + 1) * SUB, :] = p[:SUB] + p[SUB:]
+                parts[c, pl.ds(pl.multiple_of((base + j) * SUB, SUB), SUB), :] = p[:SUB] + p[SUB:]
                 grad = grad * jnp.exp2(step * rate)
                 grads[c] = grad
                 q = grad * prev
                 p = q * rate
-                parts2[c, j * SUB : (j + 1) * SUB, :] = p[:SUB] + p[SUB:]
+                parts2[c, pl.ds(pl.multiple_of((base + j) * SUB, SUB), SUB), :] = p[:SUB] + p[SUB:]
                 drate[c] = drate[c] + q * step
             token = back * block + base + j
             sums[pl.ds(token, N, stride=PITCH), :] = db
@@ -539,23 +541,23 @@
             lanes = slice(c * LANE, (c + 1) * LANE)
             carry[:, lanes] = grads[c]
             drate_ref[:, lanes] = drate[c]
-            x = parts[c, pl.ds(0, SUB, stride=SUB), :]
-            r = parts2[c, pl.ds(0, SUB, stride=SUB), :]
-            for n in range(1, SUB):
-                x = x + parts[c, pl.ds(n, SUB, stride=SUB), :]
-                r = r + parts2[c, pl.ds(n, SUB, stride=SUB), :]
-            dy = dy8[:, lanes]
-            u = u8[:, lanes]
-            du_ref[pl.ds(base, SUB), lanes] = step8[:, lanes] * x + table_ref[SKIP : SKIP + 1, lanes] * dy
-            d = (u * x + LN2 * r) * jax.nn.sigmoid(pre8[:, lanes])
-            ddtp[pl.ds(base, SUB), lanes] = d
-            drow_ref[:SUB, lanes] += d
-            drow_ref[SUB:, lanes] += dy * u
         return 0
 
     lax.fori_loop(0, groups, group, 0)
-    low = ddtp[...].astype(BF)
-    ddtp_ref[...] = low
+    for c in range(chunks):
+        lanes = slice(c * LANE, (c + 1) * LANE)
+        x = parts[c, pl.ds(0, block, stride=SUB), :]
+        r = parts2[c, pl.ds(0, block, stride=SUB), :]
+        for n in range(1, SUB):
+            x = x + parts[c, pl.ds(n, block, stride=SUB), :]
+            r = r + parts2[c, pl.ds(n, block, stride=SUB), :]
+        dy, u, step = dy_ref[:, lanes], u_ref[:, lanes], step_ref[:, lanes]
+        du_ref[:, lanes] = step * x + table_ref[SKIP : SKIP + 1, lanes] * dy
+        d = (u * x + LN2 * r) * jax.nn.sigmoid(pre[:, lanes])
+        ddtp_ref[:, lanes] = d.astype(BF)
+        drow_ref[:SUB, lanes] += jnp.sum(d.reshape(groups, SUB, LANE), axis=0)
+        drow_ref[SUB:, lanes] += jnp.sum((dy * u).reshape(groups, SUB, LANE), axis=0)
+    low = ddtp_ref[...]
     own[pl.ds(pl.multiple_of(back * block, block), block), :] = product(low, dt_ref[...])
 
     @pl.when(first)
@@ -596,9 +598,9 @@
         out_specs=[tok, tok, pl.BlockSpec((ITEM, LANE), lambda i, t: (begin + i, 0)), whole(out_shape[3]), whole(out_shape[4])],
         out_shape=out_shape,
         scratch_shapes=[
-            pltpu.VMEM((block, width), F32), pltpu.VMEM((N, width), F32), pltpu.VMEM((block // SUB, 2 * N, LANE), F32),
-            pltpu.VMEM((block, width), F32), pltpu.VMEM((N, width), F32),
-            pltpu.VMEM((chunks, SUB * SUB, LANE), F32), pltpu.VMEM((chunks, SUB * SUB, LANE), F32),
+            *[pltpu.VMEM((block, width), F32)] * 3, pltpu.VMEM((N, width), F32),
+            pltpu.VMEM((block // SUB, 2 * N, LANE), F32), pltpu.VMEM((N, width), F32),
+            *[pltpu.VMEM((chunks, block * SUB, LANE), F32)] * 2,
             pltpu.VMEM((2 * N * PITCH, LANE), F32), pltpu.VMEM((LANE, ITEM), F32), pltpu.VMEM((ITEM, LANE), F32),
         ],
         input_output_aliases={7 + k: k for k in range(len(kept))},
@@ -839,19 +841,19 @@
     dy, dz_low, o_own, o_far, gate_full, early = gates(h_low, dfinal_all, mod, y, rest)
     bits = group_bits(n_fsdp)[::-1]
     kept, drates, drows, came, o_came = [], [], [], None, None
-    for i in range(calls):
+    for i, (begin, some) in enumerate(((0, 1), (1, items - 2), (items - 1, 1))):
         partial = ring_partial(early, i, came, drates[-1:])
         came = ring_send(partial)
         *kept, drate, drow = scan_backward(
-            i * part, part, u, proj, dy, states, dt_full, table, kept, [*partial, *([] if i else [o_far])]
+            begin, some, u, proj, dy, states, dt_full, table, kept, [*partial, *([] if i else [o_far])]
         )
         drates.append(drate)
         drows.append(drow)
         if i == 0:
             o_came = swap(o_far, bits[0], n_fsdp)
-    beside = came
-    partial = ring_partial(early, calls, came, drates[-1:])
-    came = ring_send(partial)
+    beside, calls = came, len(drates)
+    leaving = ring_partial(early, calls, came, drates[-1:])
+    came = ring_send(leaving)
     du_scan, ddtp_low, dproj = kept
 
     dproj, other = group_sum(hold(dproj, *beside), n_fsdp)
@@ -859,31 +861,43 @@
         o_own, o_far = fold(o_own, o_came, [other])
         o_came = swap(o_far, bit, n_fsdp)
     o_own = o_own.astype(F32) + o_came.astype(F32)
+
+    def to_owners(early_sum):
+        sums = early_sum[:, :D].astype(BF), early_sum[:, D:].astype(BF)
+        return sums, (moved(sums[0], "dp", [(q, q + half) for q in range(half)]), moved(sums[1], ALL, back))
+
+    if half == calls + 1:
+        early_sum = ring_last(early, came)
+        leaving, arrived = to_owners(early_sum)
+    else:
+        arrived = came
     dh, dh_far, late = mix_back(
         h_low, xs, du_scan, ddtp_low, u_low, proj, dproj, dz_low, x_full, table, stream_full, gate_full,
-        drates, drows, ring_sizes(rows, n_dp), [o_far, *partial]
+        drates, drows, ring_sizes(rows, n_dp), [o_far, *leaving]
     )
-    dh_far, *late[-2:] = [hold(v, *came, o_came) for v in (dh_far, *late[-2:])]
-    for i in range(calls + 1, half):
-        came = ring_send(ring_partial(early, i, came, late[-1:]))
-    early_sum = ring_last(early, came)
-    last_early, came, dh_came = came, None, None
+    dh_far, *late[-2:] = [hold(v, *arrived, o_came) for v in (dh_far, *late[-2:])]
+    came, dh_came = None, None
     for i in range(half):
         if 0 < i < len(bits):
             dh, dh_far = fold(dh, dh_came, [])
-        after = [dh_far] if i == 1 else last_early if i == 2 else [dh_came] if i == half - 1 else []
+        after = [dh_far] if i == 1 else [dh_came] if i == half - 1 else []
         came = ring_send(ring_partial(late, i, came, after))
         if i < len(bits):
             dh_came = swap(dh_far, bits[i], n_fsdp)
     dh = dh + dh_came.astype(F32)
     late_sum = ring_last(late, came)
+    if half == calls + 1:
+        (gate_sum, _), (gate_moved, out_share) = leaving, arrived
+    else:
+        came = arrived
+        for i in range(calls + 1, half):
+            came = ring_send(ring_partial(early, i, came, [late_sum]))
+        early_sum = ring_last(early, came)
+        (gate_sum, _), (gate_moved, out_share) = to_owners(early_sum)
     squares = jnp.sum(early_sum * early_sum) + jnp.sum(late_sum * late_sum)
     small = moved(late_sum[:, D:].astype(BF), ALL, back).astype(F32)
     small_t = small[:, LANE:].T
     late_sum = late_sum[:, :D].astype(BF)
-    gate_sum = early_sum[:, :D].astype(BF)
-    gate_moved = moved(hold(gate_sum, late_sum), "dp", [(q, q + half) for q in range(half)])
-    out_share = moved(hold(early_sum[:, D:].astype(BF), late_sum), ALL, back)
     late_moved = moved(late_sum, "dp", [(q + half, q) for q in range(half)])
     in_share = jnp.concatenate(
         [jnp.where(low_half, late_sum, gate_moved), jnp.where(low_half, late_moved, gate_sum)], axis=0

time: 413 us -> 403 us (0.976)
  the two profiles are of different devices: /device:TPU:2 before, /device:TPU:0 now
where the time goes in v4:
time: 403 us; the launch traced here: 402 us
  Pallas kernels  188 us (47%)
  waiting for transfers between devices  80.8 us (20%)
  starting transfers between devices  79.4 us (20%)
  other arithmetic  24 us (6%)
  local copies, waits for them, and re-layouts  20.3 us (5%)
  between operations  7.37 us (2%)
    pallas_call x3, Pallas kernels, scan_backward(): pl.pallas_call(scan_backward_body, grid=(count, steps), in_specs=[tok, pl...  66.5 us
    ppermute x56, starting transfers between devices, moved(): lax.ppermute(with_layout_constraint(v, Layout(tuple(range(v.ndim)))), axe...  61 us
    ppermute x56, waiting for transfers between devices, moved(): lax.ppermute(with_layout_constraint(v, Layout(tuple(range(v.ndim)))), axe...  59.1 us
    pallas_call x2, Pallas kernels, scan_forward(): pl.pallas_call(scan_forward_body, grid=(count, steps), in_specs=[tok, pl....  32.6 us
    pallas_call x1, Pallas kernels, gates(): pl.pallas_call(lambda *refs: gates_body(items, len(blocks), *refs), grid=...  23.1 us
    all_to_all x4, waiting for transfers between devices, exchange(): return lax.all_to_all(v, ALL, 0, 0, tiled=True)  21.7 us
    pallas_call x1, Pallas kernels, mix_back(): pl.pallas_call(lambda *refs: mix_back_body(calls, len(blocks), *refs), gr...  20.8 us
    all_to_all x4, starting transfers between devices, exchange(): return lax.all_to_all(v, ALL, 0, 0, tiled=True)  18.4 us
  transfers between devices with their start and end apart: 60, of which 19 were waited for; matrix products, arithmetic and copies ran while one was open for 7% of the time, Pallas kernels for 37%

profile of v4, /device:TPU:0, one launch (start us, length us, event | category | flops | bytes accessed | tf_op | source)
XLA Modules:
  0.0 402.0 jit_solution(16424484368901568155)
XLA Ops:
  2.3 4.1 %collective-permute-start = (bf16[96,1536]{1,0:T(8,128)(2,1)S(1)}, bf16[96,1536]{1,0:T(8,128)(2,1)S(1)}, u32[]{:S(2)}, u32[]{:S(2)}) collective-permute-start(bf16[96,1536]{1,0:T(8,128)(2,1)S(1)} %broadcast_select_fusion.5.refs_0_), channel_id=1, source_target_pairs={{0,16},{4,20},{8,24},{12,28},{16,0},{20,4},{24,8},{28,12},{1,17},{... | collective-permute-start | bytes 884744 | tf_op jit(solution)/shard_map/ppermute | solution.py:682
  10.0 6.6 %all-to-all-start = ((s32[32,1,1]{2,1,0:T(1,128)}), s32[32,1,1]{2,1,0:T(1,128)S(1)}, u32[]{:S(2)}, u32[]{:S(2)}) async-start(s32[32,1,1]{2,1,0:T(1,128)} %bitcast.43), calls=%async_computation | async-start | bytes 32768 | tf_op jit(solution)/shard_map/all_to_all | solution.py:766
  19.9 3.9 all-to-all-done
  33.2 8.2 %all-to-all-done.1.refs_0_ = f32[32,4,144]{2,1,0:T(4,128)S(1)} async-done(((f32[32,4,144]{2,1,0:T(4,128)}), f32[32,4,144]{2,1,0:T(4,128)S(1)}, u32[]{:S(2)}, u32[]{:S(2)}) %all-to-all-start.1) | async-done | bytes 73760 | tf_op jit(solution)/shard_map/all_to_all | solution.py:766
  45.4 7.0 %collective-permute-done.9.refs_9_ = bf16[96,1792]{1,0:T(8,128)(2,1)} collective-permute-done((bf16[96,1792]{1,0:T(8,128)(2,1)}, bf16[96,1792]{1,0:T(8,128)(2,1)}, u32[]{:S(2)}, u32[]{:S(2)}) %collective-permute-start.9) | collective-permute-done | bytes 344096 | tf_op jit(solution)/shard_map/ppermute | solution.py:682
  57.8 3.9 collective-permute-done.11.refs_11_
  73.1 5.8 %collective-permute-done.12.refs_12_ = bf16[96,1792]{1,0:T(8,128)(2,1)S(1)} collective-permute-done((bf16[96,1792]{1,0:T(8,128)(2,1)}, bf16[96,1792]{1,0:T(8,128)(2,1)S(1)}, u32[]{:S(2)}, u32[]{:S(2)}) %collective-permute-start.12) | collective-permute-done | bytes 344096 | tf_op jit(solution)/shard_map/ppermute | solution.py:682
  79.6 11.9 %mix.1 = (bf16[1024,1536]{1,0:T(8,128)(2,1)}, f32[1024,768]{1,0:T(8,128)}, f32[1024,768]{1,0:T(8,128)}, bf16[1024,768]{1,0:T(8,128)(2,1)}, f32[1024,128]{1,0:T(8...) custom-call(f32[4,4608]{1,0:T(4,128)} %broadcast_select_fusion.6.ref, ...), custom_call_target="tpu_custom_call" | custom-call | flops 11000000512 | bytes 11000000 | tf_op jit(solution)/shard_map/mix/pallas_call | solution.py:220
  102.1 4.2 %collective-permute-done.21 = f32[512,128]{1,0:T(8,128)S(1)} collective-permute-done((f32[512,128]{1,0:T(8,128)S(1)}, f32[512,128]{1,0:T(8,128)S(1)}, u32[]{:S(2)}, u32[]{:S(2)}) %collective-permute-start.21) | collective-permute-done | bytes 262176 | tf_op jit(solution)/shard_map/ppermute | solution.py:682
  106.5 8.6 %collective-permute-done.23.refs_0_.refs_10_ = bf16[96,3072]{1,0:T(8,128)(2,1)S(1)} collective-permute-done((bf16[96,3072]{1,0:T(8,128)(2,1)}, bf16[96,3072]{1,0:T(8,128)(2,1)S(1)}, u32[]{:S(2)}, u32[]{:S(2)}) %collective-permute-start.23) | collective-permute-done | bytes 589856 | tf_op jit(solution)/shard_map/ppermute | solution.py:682
  118.4 16.5 %scan_forward.2 = (f32[1024,768]{1,0:T(8,128)}, f32[16384,768]{1,0:T(8,128)}) custom-call(f32[1024,768]{1,0:T(8,128)} %get-tuple-element.121.u_ref, f32[1024,128]{1,0:T(8,128)} %pad_maximum_fusion.2.proj_ref.refs_5_, bf16[768,128]{1,0:T(8,128)(2,1)} %get-tuple-element.123.dt_ref, f32[32,768]{1,0:T(8,128)} %get-tuple-element.124.table_ref.refs_9_, ...), custom_call_target="tpu_custom_call" | custom-call | flops 16000000000 | bytes 16000000 | tf_op jit(solution)/shard_map/scan_forward/pallas_call | solution.py:460
  137.7 16.1 %scan_forward.3 = (f32[1024,768]{1,0:T(8,128)}, f32[16384,768]{1,0:T(8,128)}) custom-call(f32[1024,768]{1,0:T(8,128)} %get-tuple-element.121.u_ref, f32[1024,128]{1,0:T(8,128)} %pad_maximum_fusion.2.proj_ref.refs_5_, bf16[768,128]{1,0:T(8,128)(2,1)} %get-tuple-element.123.dt_ref, ...), custom_call_target="tpu_custom_call", output_to_operand_aliasing={{0}: (4, {}), {1}: (5, {})} | custom-call | flops 16000000000 | bytes 16000000 | tf_op jit(solution)/shard_map/scan_forward/pallas_call | solution.py:460
  154.7 23.1 %gates.1 = (f32[1024,768]{1,0:T(8,128)}, bf16[1024,768]{1,0:T(8,128)(2,1)}, bf16[512,1536]{1,0:T(8,128)(2,1)}, bf16[512,1536]{1,0:T(8,128)(2,1)}, bf16[768,1536]...) custom-call(bf16[1024,1536]{1,0:T(8,128)(2,1)} %get-tuple-element.12, ...), custom_call_target="tpu_custom_call" | custom-call | flops 24000000000 | bytes 24000000 | tf_op jit(solution)/shard_map/gates/pallas_call | solution.py:294
  179.9 17.5 %scan_backward.3 = (f32[1024,768]{1,0:T(8,128)}, bf16[1024,768]{1,0:T(8,128)(2,1)}, f32[1024,128]{1,0:T(8,128)}, f32[16,768]{1,0:T(8,128)}, f32[16,768]{1,0:T(8,128)}) custom-call(f32[1024,768]{1,0:T(8,128)} %get-tuple-element.121.u_ref, f32[1024,128]{1,0:T(8,128)} %pad_maximum_fusion.2.proj_ref.refs_5_, f32[1024,768]{1,0:T(8,128)} %get-tuple-element.130.dy_ref, ...), custom_call_target="tpu_custom_call" | custom-call | flops 15000000512 | bytes 15000000 | tf_op jit(solution)/shard_map/scan_backward/pallas_call | solution.py:588
  202.7 31.5 %scan_backward.4 = (f32[1024,768]{1,0:T(8,128)}, bf16[1024,768]{1,0:T(8,128)(2,1)}, f32[1024,128]{1,0:T(8,128)}, f32[16,768]{1,0:T(8,128)}, f32[16,768]{1,0:T(8,128)}) custom-call(f32[1024,768]{1,0:T(8,128)} %get-tuple-element.121.u_ref, f32[1024,128]{1,0:T(8,128)} %pad_maximum_fusion.2.proj_ref.refs_5_, ...), custom_call_target="tpu_custom_call", output_to_operand_aliasing={{0}: (7, {}), {1}: (8, {}), {2}: (9, {})} | custom-call | flops 30000001024 | bytes 30000000 | tf_op jit(solution)/shard_map/scan_backward/pallas_call | solution.py:588
  240.0 17.5 %scan_backward.5 = (f32[1024,768]{1,0:T(8,128)}, bf16[1024,768]{1,0:T(8,128)(2,1)}, f32[1024,128]{1,0:T(8,128)}, f32[16,768]{1,0:T(8,128)}, f32[16,768]{1,0:T(8,128)}) custom-call(f32[1024,768]{1,0:T(8,128)} %get-tuple-element.121.u_ref, f32[1024,128]{1,0:T(8,128)} %pad_maximum_fusion.2.proj_ref.refs_5_, ...), custom_call_target="tpu_custom_call", output_to_operand_aliasing={{0}: (7, {}), {1}: (8, {}), {2}: (9, {})} | custom-call | flops 15000000512 | bytes 15000000 | tf_op jit(solution)/shard_map/scan_backward/pallas_call | solution.py:588
  275.1 5.5 %collective-permute-done.40 = bf16[96,3072]{1,0:T(8,128)(2,1)S(1)} collective-permute-done((bf16[96,3072]{1,0:T(8,128)(2,1)}, bf16[96,3072]{1,0:T(8,128)(2,1)S(1)}, u32[]{:S(2)}, u32[]{:S(2)}) %collective-permute-start.40) | collective-permute-done | bytes 589856 | tf_op jit(solution)/shard_map/ppermute | solution.py:682
  286.2 20.8 %mix_back.1 = (f32[512,1536]{1,0:T(8,128)}, bf16[512,1536]{1,0:T(8,128)(2,1)}, bf16[96,1792]{1,0:T(8,128)(2,1)}, bf16[96,1792]{1,0:T(8,128)(2,1)}, bf16[96,1792]...) custom-call(bf16[1024,1536]{1,0:T(8,128)(2,1)} %get-tuple-element.12, ...), custom_call_target="tpu_custom_call" | custom-call | flops 19000000512 | bytes 19000000 | tf_op jit(solution)/shard_map/mix_back/pallas_call | solution.py:378
  325.3 7.5 %collective-permute-done.48.up_ref = bf16[96,1792]{1,0:T(8,128)(2,1)S(1)} collective-permute-done((bf16[96,1792]{1,0:T(8,128)(2,1)}, bf16[96,1792]{1,0:T(8,128)(2,1)S(1)}, u32[]{:S(2)}, u32[]{:S(2)}) %collective-permute-start.48) | collective-permute-done | bytes 344096 | tf_op jit(solution)/shard_map/ppermute | solution.py:682
  339.1 6.5 %collective-permute-done.50.up_ref = bf16[96,1792]{1,0:T(8,128)(2,1)S(1)} collective-permute-done((bf16[96,1792]{1,0:T(8,128)(2,1)}, bf16[96,1792]{1,0:T(8,128)(2,1)S(1)}, u32[]{:S(2)}, u32[]{:S(2)}) %collective-permute-start.50) | collective-permute-done | bytes 344096 | tf_op jit(solution)/shard_map/ppermute | solution.py:682
  353.4 4.2 %fusion.10 = (bf16[1536]{0:T(1024)(128)(2,1)S(1)}, f32[256,1536]{1,0:T(8,128)}, f32[256,1536]{1,0:T(8,128)}) fusion(f32[256,1536]{1,0:T(8,128)} %get-tuple-element.151, bf16[256,1536]{1,0:T(8,128)(2,1)S(1)} %copy-done.3, f32[1536]{0:T(1024)S(1)} %get-tuple-element.218, bf16[256,1536]{1,0:T(8,128)(2,1)S(1)} %copy-done.1, f32[256]{0:T(256)S(1)} %get-tuple-element.242, ...), kind=kLoop, calls=%fused_computation.16 | loop fusion | flops 7469568 | bytes 9456896 | tf_op jit(solution)/shard_map/reduce_sum | solution.py:913
  375.5 4.9 %all-to-all-start.3 = ((f32[32,1,128]{2,1,0:T(1,128)}), f32[32,1,128]{2,1,0:T(1,128)S(1)}, u32[]{:S(2)}, u32[]{:S(2)}) async-start(f32[32,1,128]{2,1,0:T(1,128)} %broadcast_in_dim.63), calls=%async_computation.3 | async-start | bytes 32768 | tf_op jit(solution)/shard_map/all_to_all | solution.py:766
  381.8 5.7 %all-to-all-done.3 = f32[32,1,128]{2,1,0:T(1,128)S(1)} async-done(((f32[32,1,128]{2,1,0:T(1,128)}), f32[32,1,128]{2,1,0:T(1,128)S(1)}, u32[]{:S(2)}, u32[]{:S(2)}) %all-to-all-start.3) | async-done | bytes 16416 | tf_op jit(solution)/shard_map/all_to_all | solution.py:766
  389.7 11.2 %update.1 = (f32[144,1536]{1,0:T(8,128)}, f32[144,1536]{1,0:T(8,128)}, f32[144,1536]{1,0:T(8,128)}, f32[144,1536]{1,0:T(8,128)}, f32[192,1536]{1,0:T(8,128)}, /*...) custom-call(f32[1,1]{1,0:T(1,128)} %bitcast.10.factor_ref, ...), custom_call_target="tpu_custom_call" | custom-call | flops 11000000512 | bytes 11000000 | tf_op jit(solution)/shard_map/update/pallas_call | solution.py:649
  (312 shorter events, 141.8 us)
Async XLA Ops:
  2.3 23.2 %collective-permute-start = (bf16[96,1536]{1,0:T(8,128)(2,1)S(1)}, bf16[96,1536]{1,0:T(8,128)(2,1)S(1)}, u32[]{:S(2)}, u32[]{:S(2)}) collective-permute-start(bf16[96,1536]{1,0:T(8,128)(2,1)S(1)} %broadcast_select_fusion.5.refs_0_), channel_id=1, source_target_pairs={{0,16},{4,20},{8,24},{12,28},{16,0},{20,4},{24,8},{28,12},{1,17},{... | collective-permute-start | bytes 884744 | tf_op jit(solution)/shard_map/ppermute | solution.py:682
  7.3 18.3 %collective-permute-start.5 = (bf16[96,256]{1,0:T(8,128)(2,1)}, bf16[96,256]{1,0:T(8,128)(2,1)S(1)}, u32[]{:S(2)}, u32[]{:S(2)}) collective-permute-start(bf16[96,256]{1,0:T(8,128)(2,1)} %hold.14), channel_id=1, source_target_pairs={{0,0},{1,16},{2,1},{3,17},{4,2},{5,18},{6,3},{7,19},{8,4},{9,20},{... | collective-permute-start | bytes 147464 | tf_op jit(solution)/shard_map/ppermute | solution.py:682
  16.7 45.7 %collective-permute-start.2 = (bf16[256,1536]{1,0:T(8,128)(2,1)S(1)}, bf16[256,1536]{1,0:T(8,128)(2,1)}, u32[]{:S(2)}, u32[]{:S(2)}) collective-permute-start(bf16[256,1536]{1,0:T(8,128)(2,1)S(1)} %copy-done), channel_id=1, source_target_pairs={{0,2},{1,3},{2,0},{3,1},{4,6},{5,7},{6,4},{7,5},{8,10},{9,11},{10,... | collective-permute-start | bytes 2359304 | tf_op jit(solution)/shard_map/ppermute | solution.py:682
  26.4 17.8 %collective-permute-start.6 = (bf16[96,1792]{1,0:T(8,128)(2,1)}, bf16[96,1792]{1,0:T(8,128)(2,1)}, u32[]{:S(2)}, u32[]{:S(2)}) collective-permute-start(bf16[96,1792]{1,0:T(8,128)(2,1)} %pad_maximum_fusion.4.refs_5_), channel_id=1, source_target_pairs={{0,8},{8,16},{16,24},{24,28},{28,20},{20,12},{12,4},{4,0},{1,9},{9... | collective-permute-start | bytes 1032200 | tf_op jit(solution)/shard_map/ppermute | solution.py:682
  27.0 16.4 %collective-permute-start.7 = (bf16[96,1792]{1,0:T(8,128)(2,1)}, bf16[96,1792]{1,0:T(8,128)(2,1)}, u32[]{:S(2)}, u32[]{:S(2)}) collective-permute-start(bf16[96,1792]{1,0:T(8,128)(2,1)} %pad_maximum_fusion.4.refs_5_), channel_id=1, source_target_pairs={{0,4},{8,0},{16,8},{24,16},{28,24},{20,28},{12,20},{4,12},{1,5},{9... | collective-permute-start | bytes 1032200 | tf_op jit(solution)/shard_map/ppermute | solution.py:682
  42.1 20.8 %collective-permute-start.15 = (bf16[256,1536]{1,0:T(8,128)(2,1)}, bf16[256,1536]{1,0:T(8,128)(2,1)}, u32[]{:S(2)}, u32[]{:S(2)}) collective-permute-start(bf16[256,1536]{1,0:T(8,128)(2,1)} %hold.17.refs_14_.refs_3_), channel_id=1, source_target_pairs={{0,2},{1,3},{2,0},{3,1},{4,6},{5,7},{6,4},{7,5},{8,10},{9,11},{10,... | collective-permute-start | bytes 2359304 | tf_op jit(solution)/shard_map/ppermute | solution.py:682
  71.0 20.5 %collective-permute-start.18 = (bf16[96,3072]{1,0:T(8,128)(2,1)}, bf16[96,3072]{1,0:T(8,128)(2,1)S(1)}, u32[]{:S(2)}, u32[]{:S(2)}) collective-permute-start(bf16[96,3072]{1,0:T(8,128)(2,1)} %hold.16.refs_13_.refs_7_), channel_id=1, source_target_pairs={{0,8},{8,16},{16,24},{24,28},{28,20},{20,12},{12,4},{4,0},{1,9},{9... | collective-permute-start | bytes 1769480 | tf_op jit(solution)/shard_map/ppermute | solution.py:682
  71.3 20.2 %collective-permute-start.19 = (bf16[96,3072]{1,0:T(8,128)(2,1)}, bf16[96,3072]{1,0:T(8,128)(2,1)S(1)}, u32[]{:S(2)}, u32[]{:S(2)}) collective-permute-start(bf16[96,3072]{1,0:T(8,128)(2,1)} %hold.16.refs_13_.refs_7_), channel_id=1, source_target_pairs={{0,4},{8,0},{16,8},{24,16},{28,24},{20,28},{12,20},{4,12},{1,5},{9... | collective-permute-start | bytes 1769480 | tf_op jit(solution)/shard_map/ppermute | solution.py:682
  115.1 19.9 %collective-permute-start.25 = (bf16[96,3072]{1,0:T(8,128)(2,1)S(1)}, bf16[96,3072]{1,0:T(8,128)(2,1)S(1)}, u32[]{:S(2)}, u32[]{:S(2)}) collective-permute-start(bf16[96,3072]{1,0:T(8,128)(2,1)S(1)} %collective-permute-done.23.refs_0_.refs_10_), channel_id=1, source_target_pairs={{0,8},{8,16},{16,24},{24,28},{28,20},{20,12},{12,4},{4,0},{1,9},{9... | collective-permute-start | bytes 1769480 | tf_op jit(solution)/shard_map/ppermute | solution.py:682
  117.4 19.5 %collective-permute-start.26 = (bf16[96,3072]{1,0:T(8,128)(2,1)S(1)}, bf16[96,3072]{1,0:T(8,128)(2,1)S(1)}, u32[]{:S(2)}, u32[]{:S(2)}) collective-permute-start(bf16[96,3072]{1,0:T(8,128)(2,1)S(1)} %collective-permute-done.24.refs_1_.refs_11_), channel_id=1, source_target_pairs={{0,4},{8,0},{16,8},{24,16},{28,24},{20,28},{12,20},{4,12},{1,5},{9... | collective-permute-start | bytes 1769480 | tf_op jit(solution)/shard_map/ppermute | solution.py:682
  135.0 18.9 %collective-permute-start.27 = (bf16[48,3072]{1,0:T(8,128)(2,1)S(1)}, bf16[48,3072]{1,0:T(8,128)(2,1)S(1)}, u32[]{:S(2)}, u32[]{:S(2)}) collective-permute-start(bf16[48,3072]{1,0:T(8,128)(2,1)S(1)} %slice.109), channel_id=1, source_target_pairs={{0,8},{8,16},{16,24},{24,28},{28,20},{20,12},{12,4},{4,0},{1,9},{9... | collective-permute-start | bytes 884744 | tf_op jit(solution)/shard_map/ppermute | solution.py:682
  137.0 16.9 %collective-permute-start.28 = (bf16[48,3072]{1,0:T(8,128)(2,1)S(1)}, bf16[48,3072]{1,0:T(8,128)(2,1)S(1)}, u32[]{:S(2)}, u32[]{:S(2)}) collective-permute-start(bf16[48,3072]{1,0:T(8,128)(2,1)S(1)} %slice.110), channel_id=1, source_target_pairs={{0,4},{8,0},{16,8},{24,16},{28,24},{20,28},{12,20},{4,12},{1,5},{9... | collective-permute-start | bytes 884744 | tf_op jit(solution)/shard_map/ppermute | solution.py:682
  177.8 19.6 %collective-permute-start.30 = (bf16[48,3072]{1,0:T(8,128)(2,1)}, bf16[48,3072]{1,0:T(8,128)(2,1)S(1)}, u32[]{:S(2)}, u32[]{:S(2)}) collective-permute-start(bf16[48,3072]{1,0:T(8,128)(2,1)} %get-tuple-element.132.refs_0_), channel_id=1, source_target_pairs={{0,8},{8,16},{16,24},{24,28},{28,20},{20,12},{12,4},{4,0},{1,9},{9... | collective-permute-start | bytes 884744 | tf_op jit(solution)/shard_map/ppermute | solution.py:682
  179.3 18.1 %collective-permute-start.31 = (bf16[48,3072]{1,0:T(8,128)(2,1)}, bf16[48,3072]{1,0:T(8,128)(2,1)S(1)}, u32[]{:S(2)}, u32[]{:S(2)}) collective-permute-start(bf16[48,3072]{1,0:T(8,128)(2,1)} %get-tuple-element.133.refs_1_), channel_id=1, source_target_pairs={{0,4},{8,0},{16,8},{24,16},{28,24},{20,28},{12,20},{4,12},{1,5},{9... | collective-permute-start | bytes 884744 | tf_op jit(solution)/shard_map/ppermute | solution.py:682
  179.9 90.8 %collective-permute-start.29 = (bf16[512,1536]{1,0:T(8,128)(2,1)}, bf16[512,1536]{1,0:T(8,128)(2,1)}, u32[]{:S(2)}, u32[]{:S(2)}) collective-permute-start(bf16[512,1536]{1,0:T(8,128)(2,1)} %get-tuple-element.129.refs_2_), channel_id=1, source_target_pairs={{0,1},{1,0},{2,3},{3,2},{4,5},{5,4},{6,7},{7,6},{8,9},{9,8},{10,11... | collective-permute-start | bytes 4718600 | tf_op jit(solution)/shard_map/ppermute | solution.py:682
  200.7 33.5 %collective-permute-start.32 = (bf16[96,3072]{1,0:T(8,128)(2,1)}, bf16[96,3072]{1,0:T(8,128)(2,1)S(1)}, u32[]{:S(2)}, u32[]{:S(2)}) collective-permute-start(bf16[96,3072]{1,0:T(8,128)(2,1)} %get-tuple-element.140.refs_3_), channel_id=1, source_target_pairs={{0,8},{8,16},{16,24},{24,28},{28,20},{20,12},{12,4},{4,0},{1,9},{9... | collective-permute-start | bytes 1769480 | tf_op jit(solution)/shard_map/ppermute | solution.py:682
  202.2 32.0 %collective-permute-start.33 = (bf16[96,3072]{1,0:T(8,128)(2,1)}, bf16[96,3072]{1,0:T(8,128)(2,1)S(1)}, u32[]{:S(2)}, u32[]{:S(2)}) collective-permute-start(bf16[96,3072]{1,0:T(8,128)(2,1)} %get-tuple-element.141.refs_4_), channel_id=1, source_target_pairs={{0,4},{8,0},{16,8},{24,16},{28,24},{20,28},{12,20},{4,12},{1,5},{9... | collective-permute-start | bytes 1769480 | tf_op jit(solution)/shard_map/ppermute | solution.py:682
  238.0 19.5 %collective-permute-start.34 = (bf16[96,3072]{1,0:T(8,128)(2,1)}, bf16[96,3072]{1,0:T(8,128)(2,1)S(1)}, u32[]{:S(2)}, u32[]{:S(2)}) collective-permute-start(bf16[96,3072]{1,0:T(8,128)(2,1)} %get-tuple-element.148.refs_3_), channel_id=1, source_target_pairs={{0,8},{8,16},{16,24},{24,28},{28,20},{20,12},{12,4},{4,0},{1,9},{9... | collective-permute-start | bytes 1769480 | tf_op jit(solution)/shard_map/ppermute | solution.py:682
  239.5 18.1 %collective-permute-start.35 = (bf16[96,3072]{1,0:T(8,128)(2,1)}, bf16[96,3072]{1,0:T(8,128)(2,1)S(1)}, u32[]{:S(2)}, u32[]{:S(2)}) collective-permute-start(bf16[96,3072]{1,0:T(8,128)(2,1)} %get-tuple-element.149.refs_4_), channel_id=1, source_target_pairs={{0,4},{8,0},{16,8},{24,16},{28,24},{20,28},{12,20},{4,12},{1,5},{9... | collective-permute-start | bytes 1769480 | tf_op jit(solution)/shard_map/ppermute | solution.py:682
  274.7 32.3 %collective-permute-start.38 = (bf16[256,1536]{1,0:T(8,128)(2,1)}, bf16[256,1536]{1,0:T(8,128)(2,1)S(1)}, u32[]{:S(2)}, u32[]{:S(2)}) collective-permute-start(bf16[256,1536]{1,0:T(8,128)(2,1)} %get-tuple-element.152.refs_18_), channel_id=1, source_target_pairs={{0,2},{1,3},{2,0},{3,1},{4,6},{5,7},{6,4},{7,5},{8,10},{9,11},{10,... | collective-permute-start | bytes 2359304 | tf_op jit(solution)/shard_map/ppermute | solution.py:682
  282.8 24.2 %collective-permute-start.42 = (bf16[96,1536]{1,0:T(8,128)(2,1)S(1)}, bf16[96,1536]{1,0:T(8,128)(2,1)S(1)}, u32[]{:S(2)}, u32[]{:S(2)}) collective-permute-start(bf16[96,1536]{1,0:T(8,128)(2,1)S(1)} %get-tuple-element.231.refs_19_), channel_id=1, source_target_pairs={{0,16},{4,20},{8,24},{12,28},{1,17},{5,21},{9,25},{13,29},{2,18},{... | collective-permute-start | bytes 884744 | tf_op jit(solution)/shard_map/ppermute | solution.py:682
  284.7 22.3 %collective-permute-start.43 = (bf16[96,1536]{1,0:T(8,128)(2,1)S(1)}, bf16[96,1536]{1,0:T(8,128)(2,1)S(1)}, u32[]{:S(2)}, u32[]{:S(2)}) collective-permute-start(bf16[96,1536]{1,0:T(8,128)(2,1)S(1)} %get-tuple-element.230.refs_20_), channel_id=1, source_target_pairs={{0,0},{16,1},{1,2},{17,3},{2,4},{18,5},{3,6},{19,7},{4,8},{20,9},{... | collective-permute-start | bytes 884744 | tf_op jit(solution)/shard_map/ppermute | solution.py:682
  324.5 21.4 %collective-permute-start.45 = (bf16[256,1536]{1,0:T(8,128)(2,1)S(1)}, bf16[256,1536]{1,0:T(8,128)(2,1)S(1)}, u32[]{:S(2)}, u32[]{:S(2)}) collective-permute-start(bf16[256,1536]{1,0:T(8,128)(2,1)S(1)} %copy-done.43), channel_id=1, source_target_pairs={{0,2},{1,3},{2,0},{3,1},{4,6},{5,7},{6,4},{7,5},{8,10},{9,11},{10,... | collective-permute-start | bytes 2359304 | tf_op jit(solution)/shard_map/ppermute | solution.py:682
  365.1 23.7 %collective-permute-start.54 = (bf16[96,1536]{1,0:T(8,128)(2,1)}, bf16[96,1536]{1,0:T(8,128)(2,1)S(1)}, u32[]{:S(2)}, u32[]{:S(2)}) collective-permute-start(bf16[96,1536]{1,0:T(8,128)(2,1)} %get-tuple-element.233.refs_0_), channel_id=1, source_target_pairs={{16,0},{20,4},{24,8},{28,12},{17,1},{21,5},{25,9},{29,13},{18,2},{... | collective-permute-start | bytes 884744 | tf_op jit(solution)/shard_map/ppermute | solution.py:682
  (95 other events, 630.5 us)

commit v5 on v4

--- a/solution.py
+++ b/solution.py
@@ -817,13 +817,13 @@
     mod_cols = product(cond_all, ada_weight.astype(BF)).reshape(n_dp, 1, items, ada_cols)
     mod_cols = jnp.broadcast_to(mod_cols, (n_dp, n_fsdp, items, ada_cols)).reshape(devices, items, ada_cols)
     mod = exchange(hold(mod_cols, tick(stream_own, n_fsdp)))
-    dfinal_all = group_gather(hold(dfinal_own.reshape(count * ITEM, D), mod), n_fsdp)
     mod = jnp.swapaxes(mod, 0, 1).reshape(n_fsdp, count, 3 * D)
     mod = jnp.take(mod, jnp.array(offsets, jnp.int32) ^ f, axis=0).reshape(items, 3 * D)
 
     stream = [stream_own]
     for came in ring_gather_steps(stream_own, n_dp, False):
         stream += came
+    dfinal_all = group_gather(hold(dfinal_own.reshape(count * ITEM, D), stream[2]), n_fsdp)
     out_own = moved(hold(out_weight.astype(BF), stream[half - 1]), ALL, forth)
     rest_own = hold(jnp.concatenate([gate_own, out_own], axis=1), tick(stream[-2], n_fsdp))
     rest_steps = list(ring_gather_steps(rest_own, n_dp, True))

time: 403 us -> 400 us (level)
    all_to_all x4, waiting for transfers between devices: 21.7 us -> 16.2 us  [exchange(): return lax.all_to_all(v, ALL, 0, 0, tiled=True)]
  transfers between devices with their start and end apart: 60 -> 60, of which waited for: 19 -> 19; matrix products, arithmetic and copies ran while one was open for 7% -> 6% of each run, Pallas kernels for 37% -> 37%
where the time goes in v5:
time: 400 us; the launch traced here: 398 us
  Pallas kernels  188 us (47%)
  starting transfers between devices  82.3 us (21%)
  waiting for transfers between devices  77.1 us (19%)
  other arithmetic  23.2 us (6%)
  local copies, waits for them, and re-layouts  18.4 us (5%)
  between operations  7.39 us (2%)
    pallas_call x3, Pallas kernels, scan_backward(): pl.pallas_call(scan_backward_body, grid=(count, steps), in_specs=[tok, pl...  66.5 us
    ppermute x56, starting transfers between devices, moved(): lax.ppermute(with_layout_constraint(v, Layout(tuple(range(v.ndim)))), axe...  62.2 us
    ppermute x56, waiting for transfers between devices, moved(): lax.ppermute(with_layout_constraint(v, Layout(tuple(range(v.ndim)))), axe...  60.8 us
    pallas_call x2, Pallas kernels, scan_forward(): pl.pallas_call(scan_forward_body, grid=(count, steps), in_specs=[tok, pl....  32.6 us
    pallas_call x1, Pallas kernels, gates(): pl.pallas_call(lambda *refs: gates_body(items, len(blocks), *refs), grid=...  23.1 us
    pallas_call x1, Pallas kernels, mix_back(): pl.pallas_call(lambda *refs: mix_back_body(calls, len(blocks), *refs), gr...  20.8 us
    all_to_all x4, starting transfers between devices, exchange(): return lax.all_to_all(v, ALL, 0, 0, tiled=True)  20.1 us
    all_to_all x4, waiting for transfers between devices, exchange(): return lax.all_to_all(v, ALL, 0, 0, tiled=True)  16.2 us
  transfers between devices with their start and end apart: 60, of which 19 were waited for; matrix products, arithmetic and copies ran while one was open for 6% of the time, Pallas kernels for 37%

profile of v5, /device:TPU:0, one launch (start us, length us, event | category | flops | bytes accessed | tf_op | source)
XLA Modules:
  0.0 398.4 jit_solution(13747601655519168155)
XLA Ops:
  10.0 6.6 %all-to-all-start = ((s32[32,1,1]{2,1,0:T(1,128)}), s32[32,1,1]{2,1,0:T(1,128)S(1)}, u32[]{:S(2)}, u32[]{:S(2)}) async-start(s32[32,1,1]{2,1,0:T(1,128)} %bitcast.43), calls=%async_computation | async-start | bytes 32768 | tf_op jit(solution)/shard_map/all_to_all | solution.py:766
  23.4 6.5 %collective-permute-done.6.refs_6_ = bf16[96,1792]{1,0:T(8,128)(2,1)} collective-permute-done((bf16[96,1792]{1,0:T(8,128)(2,1)S(1)}, bf16[96,1792]{1,0:T(8,128)(2,1)}, u32[]{:S(2)}, u32[]{:S(2)}) %collective-permute-start.6) | collective-permute-done | bytes 344096 | tf_op jit(solution)/shard_map/ppermute | solution.py:682
  35.8 6.8 %collective-permute-done.9.refs_9_ = bf16[96,1792]{1,0:T(8,128)(2,1)} collective-permute-done((bf16[96,1792]{1,0:T(8,128)(2,1)}, bf16[96,1792]{1,0:T(8,128)(2,1)}, u32[]{:S(2)}, u32[]{:S(2)}) %collective-permute-start.9) | collective-permute-done | bytes 344096 | tf_op jit(solution)/shard_map/ppermute | solution.py:682
  45.6 4.6 %all-to-all-start.1 = ((f32[32,4,144]{2,1,0:T(4,128)}), f32[32,4,144]{2,1,0:T(4,128)S(1)}, u32[]{:S(2)}, u32[]{:S(2)}) async-start(f32[32,4,144]{2,1,0:T(4,128)} %hold.13), calls=%async_computation.1 | async-start | bytes 262144 | tf_op jit(solution)/shard_map/all_to_all | solution.py:766
  51.9 6.7 %all-to-all-done.1 = f32[32,4,144]{2,1,0:T(4,128)S(1)} async-done(((f32[32,4,144]{2,1,0:T(4,128)}), f32[32,4,144]{2,1,0:T(4,128)S(1)}, u32[]{:S(2)}, u32[]{:S(2)}) %all-to-all-start.1) | async-done | bytes 73760 | tf_op jit(solution)/shard_map/all_to_all | solution.py:766
  61.8 4.7 %collective-permute-start.12 = (bf16[96,1792]{1,0:T(8,128)(2,1)}, bf16[96,1792]{1,0:T(8,128)(2,1)S(1)}, u32[]{:S(2)}, u32[]{:S(2)}) collective-permute-start(bf16[96,1792]{1,0:T(8,128)(2,1)} %collective-permute-done.10.refs_10_), channel_id=1, source_target_pairs={{0,8},{8,16},{16,24},{24,28},{28,20},{20,12},{12,4},{4,0},{1,9},{9... | collective-permute-start | bytes 1032200 | tf_op jit(solution)/shard_map/ppermute | solution.py:682
  69.4 5.8 %collective-permute-done.12.refs_12_ = bf16[96,1792]{1,0:T(8,128)(2,1)S(1)} collective-permute-done((bf16[96,1792]{1,0:T(8,128)(2,1)}, bf16[96,1792]{1,0:T(8,128)(2,1)S(1)}, u32[]{:S(2)}, u32[]{:S(2)}) %collective-permute-start.12) | collective-permute-done | bytes 344096 | tf_op jit(solution)/shard_map/ppermute | solution.py:682
  75.9 11.9 %mix.1 = (bf16[1024,1536]{1,0:T(8,128)(2,1)}, f32[1024,768]{1,0:T(8,128)}, f32[1024,768]{1,0:T(8,128)}, bf16[1024,768]{1,0:T(8,128)(2,1)}, f32[1024,128]{1,0:T(8...) custom-call(f32[4,4608]{1,0:T(4,128)} %broadcast_select_fusion.6.ref, ...), custom_call_target="tpu_custom_call" | custom-call | flops 11000000512 | bytes 11000000 | tf_op jit(solution)/shard_map/mix/pallas_call | solution.py:220
  97.6 4.2 %collective-permute-done.21 = f32[512,128]{1,0:T(8,128)S(1)} collective-permute-done((f32[512,128]{1,0:T(8,128)S(1)}, f32[512,128]{1,0:T(8,128)S(1)}, u32[]{:S(2)}, u32[]{:S(2)}) %collective-permute-start.21) | collective-permute-done | bytes 262176 | tf_op jit(solution)/shard_map/ppermute | solution.py:682
  101.9 8.6 %collective-permute-done.23.refs_0_.refs_10_ = bf16[96,3072]{1,0:T(8,128)(2,1)S(1)} collective-permute-done((bf16[96,3072]{1,0:T(8,128)(2,1)}, bf16[96,3072]{1,0:T(8,128)(2,1)S(1)}, u32[]{:S(2)}, u32[]{:S(2)}) %collective-permute-start.23) | collective-permute-done | bytes 589856 | tf_op jit(solution)/shard_map/ppermute | solution.py:682
  113.9 16.5 %scan_forward.2 = (f32[1024,768]{1,0:T(8,128)}, f32[16384,768]{1,0:T(8,128)}) custom-call(f32[1024,768]{1,0:T(8,128)} %get-tuple-element.121.u_ref, f32[1024,128]{1,0:T(8,128)} %pad_maximum_fusion.2.proj_ref.refs_5_, bf16[768,128]{1,0:T(8,128)(2,1)} %get-tuple-element.123.dt_ref, f32[32,768]{1,0:T(8,128)} %get-tuple-element.124.table_ref.refs_9_, ...), custom_call_target="tpu_custom_call" | custom-call | flops 16000000000 | bytes 16000000 | tf_op jit(solution)/shard_map/scan_forward/pallas_call | solution.py:460
  133.2 16.1 %scan_forward.3 = (f32[1024,768]{1,0:T(8,128)}, f32[16384,768]{1,0:T(8,128)}) custom-call(f32[1024,768]{1,0:T(8,128)} %get-tuple-element.121.u_ref, f32[1024,128]{1,0:T(8,128)} %pad_maximum_fusion.2.proj_ref.refs_5_, bf16[768,128]{1,0:T(8,128)(2,1)} %get-tuple-element.123.dt_ref, ...), custom_call_target="tpu_custom_call", output_to_operand_aliasing={{0}: (4, {}), {1}: (5, {})} | custom-call | flops 16000000000 | bytes 16000000 | tf_op jit(solution)/shard_map/scan_forward/pallas_call | solution.py:460
  150.2 23.1 %gates.1 = (f32[1024,768]{1,0:T(8,128)}, bf16[1024,768]{1,0:T(8,128)(2,1)}, bf16[512,1536]{1,0:T(8,128)(2,1)}, bf16[512,1536]{1,0:T(8,128)(2,1)}, bf16[768,1536]...) custom-call(bf16[1024,1536]{1,0:T(8,128)(2,1)} %get-tuple-element.12, ...), custom_call_target="tpu_custom_call" | custom-call | flops 24000000000 | bytes 24000000 | tf_op jit(solution)/shard_map/gates/pallas_call | solution.py:294
  175.3 17.5 %scan_backward.3 = (f32[1024,768]{1,0:T(8,128)}, bf16[1024,768]{1,0:T(8,128)(2,1)}, f32[1024,128]{1,0:T(8,128)}, f32[16,768]{1,0:T(8,128)}, f32[16,768]{1,0:T(8,128)}) custom-call(f32[1024,768]{1,0:T(8,128)} %get-tuple-element.121.u_ref, f32[1024,128]{1,0:T(8,128)} %pad_maximum_fusion.2.proj_ref.refs_5_, f32[1024,768]{1,0:T(8,128)} %get-tuple-element.130.dy_ref, ...), custom_call_target="tpu_custom_call" | custom-call | flops 15000000512 | bytes 15000000 | tf_op jit(solution)/shard_map/scan_backward/pallas_call | solution.py:588
  198.2 31.5 %scan_backward.4 = (f32[1024,768]{1,0:T(8,128)}, bf16[1024,768]{1,0:T(8,128)(2,1)}, f32[1024,128]{1,0:T(8,128)}, f32[16,768]{1,0:T(8,128)}, f32[16,768]{1,0:T(8,128)}) custom-call(f32[1024,768]{1,0:T(8,128)} %get-tuple-element.121.u_ref, f32[1024,128]{1,0:T(8,128)} %pad_maximum_fusion.2.proj_ref.refs_5_, ...), custom_call_target="tpu_custom_call", output_to_operand_aliasing={{0}: (7, {}), {1}: (8, {}), {2}: (9, {})} | custom-call | flops 30000001024 | bytes 30000000 | tf_op jit(solution)/shard_map/scan_backward/pallas_call | solution.py:588
  235.5 17.5 %scan_backward.5 = (f32[1024,768]{1,0:T(8,128)}, bf16[1024,768]{1,0:T(8,128)(2,1)}, f32[1024,128]{1,0:T(8,128)}, f32[16,768]{1,0:T(8,128)}, f32[16,768]{1,0:T(8,128)}) custom-call(f32[1024,768]{1,0:T(8,128)} %get-tuple-element.121.u_ref, f32[1024,128]{1,0:T(8,128)} %pad_maximum_fusion.2.proj_ref.refs_5_, ...), custom_call_target="tpu_custom_call", output_to_operand_aliasing={{0}: (7, {}), {1}: (8, {}), {2}: (9, {})} | custom-call | flops 15000000512 | bytes 15000000 | tf_op jit(solution)/shard_map/scan_backward/pallas_call | solution.py:588
  270.5 5.5 %collective-permute-done.40 = bf16[96,3072]{1,0:T(8,128)(2,1)S(1)} collective-permute-done((bf16[96,3072]{1,0:T(8,128)(2,1)}, bf16[96,3072]{1,0:T(8,128)(2,1)S(1)}, u32[]{:S(2)}, u32[]{:S(2)}) %collective-permute-start.40) | collective-permute-done | bytes 589856 | tf_op jit(solution)/shard_map/ppermute | solution.py:682
  281.9 20.8 %mix_back.1 = (f32[512,1536]{1,0:T(8,128)}, bf16[512,1536]{1,0:T(8,128)(2,1)}, bf16[96,1792]{1,0:T(8,128)(2,1)}, bf16[96,1792]{1,0:T(8,128)(2,1)}, bf16[96,1792]...) custom-call(bf16[1024,1536]{1,0:T(8,128)(2,1)} %get-tuple-element.12, ...), custom_call_target="tpu_custom_call" | custom-call | flops 19000000512 | bytes 19000000 | tf_op jit(solution)/shard_map/mix_back/pallas_call | solution.py:378
  321.9 7.0 %collective-permute-done.48.up_ref = bf16[96,1792]{1,0:T(8,128)(2,1)S(1)} collective-permute-done((bf16[96,1792]{1,0:T(8,128)(2,1)}, bf16[96,1792]{1,0:T(8,128)(2,1)S(1)}, u32[]{:S(2)}, u32[]{:S(2)}) %collective-permute-start.48) | collective-permute-done | bytes 344096 | tf_op jit(solution)/shard_map/ppermute | solution.py:682
  335.1 6.8 %collective-permute-done.50.up_ref = bf16[96,1792]{1,0:T(8,128)(2,1)S(1)} collective-permute-done((bf16[96,1792]{1,0:T(8,128)(2,1)}, bf16[96,1792]{1,0:T(8,128)(2,1)S(1)}, u32[]{:S(2)}, u32[]{:S(2)}) %collective-permute-start.50) | collective-permute-done | bytes 344096 | tf_op jit(solution)/shard_map/ppermute | solution.py:682
  349.6 4.2 %fusion.10 = (bf16[1536]{0:T(1024)(128)(2,1)S(1)}, f32[256,1536]{1,0:T(8,128)}, f32[256,1536]{1,0:T(8,128)}) fusion(f32[256,1536]{1,0:T(8,128)} %get-tuple-element.151, bf16[256,1536]{1,0:T(8,128)(2,1)S(1)} %copy-done.3, f32[1536]{0:T(1024)S(1)} %get-tuple-element.218, bf16[256,1536]{1,0:T(8,128)(2,1)S(1)} %copy-done.1, f32[256]{0:T(256)S(1)} %get-tuple-element.242, ...), kind=kLoop, calls=%fused_computation.16 | loop fusion | flops 7469568 | bytes 9456896 | tf_op jit(solution)/shard_map/reduce_sum | solution.py:913
  371.8 4.9 %all-to-all-start.3 = ((f32[32,1,128]{2,1,0:T(1,128)}), f32[32,1,128]{2,1,0:T(1,128)S(1)}, u32[]{:S(2)}, u32[]{:S(2)}) async-start(f32[32,1,128]{2,1,0:T(1,128)} %broadcast_in_dim.63), calls=%async_computation.3 | async-start | bytes 32768 | tf_op jit(solution)/shard_map/all_to_all | solution.py:766
  378.1 5.7 %all-to-all-done.3 = f32[32,1,128]{2,1,0:T(1,128)S(1)} async-done(((f32[32,1,128]{2,1,0:T(1,128)}), f32[32,1,128]{2,1,0:T(1,128)S(1)}, u32[]{:S(2)}, u32[]{:S(2)}) %all-to-all-start.3) | async-done | bytes 16416 | tf_op jit(solution)/shard_map/all_to_all | solution.py:766
  386.1 11.2 %update.1 = (f32[144,1536]{1,0:T(8,128)}, f32[144,1536]{1,0:T(8,128)}, f32[144,1536]{1,0:T(8,128)}, f32[144,1536]{1,0:T(8,128)}, f32[192,1536]{1,0:T(8,128)}, /*...) custom-call(f32[1,1]{1,0:T(1,128)} %bitcast.10.factor_ref, ...), custom_call_target="tpu_custom_call" | custom-call | flops 11000000512 | bytes 11000000 | tf_op jit(solution)/shard_map/update/pallas_call | solution.py:649
  (312 shorter events, 136.3 us)
Async XLA Ops:
  2.2 18.0 %collective-permute-start = (bf16[96,1536]{1,0:T(8,128)(2,1)S(1)}, bf16[96,1536]{1,0:T(8,128)(2,1)S(1)}, u32[]{:S(2)}, u32[]{:S(2)}) collective-permute-start(bf16[96,1536]{1,0:T(8,128)(2,1)S(1)} %broadcast_select_fusion.5.refs_0_), channel_id=1, source_target_pairs={{0,16},{4,20},{8,24},{12,28},{16,0},{20,4},{24,8},{28,12},{1,17},{... | collective-permute-start | bytes 884744 | tf_op jit(solution)/shard_map/ppermute | solution.py:682
  10.0 23.4 %all-to-all-start = ((s32[32,1,1]{2,1,0:T(1,128)}), s32[32,1,1]{2,1,0:T(1,128)S(1)}, u32[]{:S(2)}, u32[]{:S(2)}) async-start(s32[32,1,1]{2,1,0:T(1,128)} %bitcast.43), calls=%async_computation | async-start | bytes 32768 | tf_op jit(solution)/shard_map/all_to_all | solution.py:766
  16.6 42.9 %collective-permute-start.2 = (bf16[256,1536]{1,0:T(8,128)(2,1)S(1)}, bf16[256,1536]{1,0:T(8,128)(2,1)}, u32[]{:S(2)}, u32[]{:S(2)}) collective-permute-start(bf16[256,1536]{1,0:T(8,128)(2,1)S(1)} %copy-done), channel_id=1, source_target_pairs={{0,2},{1,3},{2,0},{3,1},{4,6},{5,7},{6,4},{7,5},{8,10},{9,11},{10,... | collective-permute-start | bytes 2359304 | tf_op jit(solution)/shard_map/ppermute | solution.py:682
  33.7 26.8 %collective-permute-start.15 = (bf16[256,1536]{1,0:T(8,128)(2,1)}, bf16[256,1536]{1,0:T(8,128)(2,1)}, u32[]{:S(2)}, u32[]{:S(2)}) collective-permute-start(bf16[256,1536]{1,0:T(8,128)(2,1)} %hold.17.refs_14_.refs_3_), channel_id=1, source_target_pairs={{0,2},{1,3},{2,0},{3,1},{4,6},{5,7},{6,4},{7,5},{8,10},{9,11},{10,... | collective-permute-start | bytes 2359304 | tf_op jit(solution)/shard_map/ppermute | solution.py:682
  42.6 16.8 %collective-permute-start.11 = (bf16[96,1792]{1,0:T(8,128)(2,1)}, bf16[96,1792]{1,0:T(8,128)(2,1)S(1)}, u32[]{:S(2)}, u32[]{:S(2)}) collective-permute-start(bf16[96,1792]{1,0:T(8,128)(2,1)} %collective-permute-done.9.refs_9_), channel_id=1, source_target_pairs={{0,4},{8,0},{16,8},{24,16},{28,24},{20,28},{12,20},{4,12},{1,5},{9... | collective-permute-start | bytes 1032200 | tf_op jit(solution)/shard_map/ppermute | solution.py:682
  42.9 17.2 %collective-permute-start.10 = (bf16[96,1792]{1,0:T(8,128)(2,1)S(1)}, bf16[96,1792]{1,0:T(8,128)(2,1)}, u32[]{:S(2)}, u32[]{:S(2)}) collective-permute-start(bf16[96,1792]{1,0:T(8,128)(2,1)S(1)} %collective-permute-done.8.refs_0_.refs_8_), channel_id=1, source_target_pairs={{0,8},{8,16},{16,24},{24,28},{28,20},{20,12},{12,4},{4,0},{1,9},{9... | collective-permute-start | bytes 1032200 | tf_op jit(solution)/shard_map/ppermute | solution.py:682
  67.3 20.5 %collective-permute-start.18 = (bf16[96,3072]{1,0:T(8,128)(2,1)}, bf16[96,3072]{1,0:T(8,128)(2,1)S(1)}, u32[]{:S(2)}, u32[]{:S(2)}) collective-permute-start(bf16[96,3072]{1,0:T(8,128)(2,1)} %hold.16.refs_13_.refs_7_), channel_id=1, source_target_pairs={{0,8},{8,16},{16,24},{24,28},{28,20},{20,12},{12,4},{4,0},{1,9},{9... | collective-permute-start | bytes 1769480 | tf_op jit(solution)/shard_map/ppermute | solution.py:682
  67.4 20.5 %collective-permute-start.19 = (bf16[96,3072]{1,0:T(8,128)(2,1)}, bf16[96,3072]{1,0:T(8,128)(2,1)S(1)}, u32[]{:S(2)}, u32[]{:S(2)}) collective-permute-start(bf16[96,3072]{1,0:T(8,128)(2,1)} %hold.16.refs_13_.refs_7_), channel_id=1, source_target_pairs={{0,4},{8,0},{16,8},{24,16},{28,24},{20,28},{12,20},{4,12},{1,5},{9... | collective-permute-start | bytes 1769480 | tf_op jit(solution)/shard_map/ppermute | solution.py:682
  110.5 19.9 %collective-permute-start.25 = (bf16[96,3072]{1,0:T(8,128)(2,1)S(1)}, bf16[96,3072]{1,0:T(8,128)(2,1)S(1)}, u32[]{:S(2)}, u32[]{:S(2)}) collective-permute-start(bf16[96,3072]{1,0:T(8,128)(2,1)S(1)} %collective-permute-done.23.refs_0_.refs_10_), channel_id=1, source_target_pairs={{0,8},{8,16},{16,24},{24,28},{28,20},{20,12},{12,4},{4,0},{1,9},{9... | collective-permute-start | bytes 1769480 | tf_op jit(solution)/shard_map/ppermute | solution.py:682
  112.9 19.5 %collective-permute-start.26 = (bf16[96,3072]{1,0:T(8,128)(2,1)S(1)}, bf16[96,3072]{1,0:T(8,128)(2,1)S(1)}, u32[]{:S(2)}, u32[]{:S(2)}) collective-permute-start(bf16[96,3072]{1,0:T(8,128)(2,1)S(1)} %collective-permute-done.24.refs_1_.refs_11_), channel_id=1, source_target_pairs={{0,4},{8,0},{16,8},{24,16},{28,24},{20,28},{12,20},{4,12},{1,5},{9... | collective-permute-start | bytes 1769480 | tf_op jit(solution)/shard_map/ppermute | solution.py:682
  130.4 18.9 %collective-permute-start.27 = (bf16[48,3072]{1,0:T(8,128)(2,1)S(1)}, bf16[48,3072]{1,0:T(8,128)(2,1)S(1)}, u32[]{:S(2)}, u32[]{:S(2)}) collective-permute-start(bf16[48,3072]{1,0:T(8,128)(2,1)S(1)} %slice.109), channel_id=1, source_target_pairs={{0,8},{8,16},{16,24},{24,28},{28,20},{20,12},{12,4},{4,0},{1,9},{9... | collective-permute-start | bytes 884744 | tf_op jit(solution)/shard_map/ppermute | solution.py:682
  132.4 16.9 %collective-permute-start.28 = (bf16[48,3072]{1,0:T(8,128)(2,1)S(1)}, bf16[48,3072]{1,0:T(8,128)(2,1)S(1)}, u32[]{:S(2)}, u32[]{:S(2)}) collective-permute-start(bf16[48,3072]{1,0:T(8,128)(2,1)S(1)} %slice.110), channel_id=1, source_target_pairs={{0,4},{8,0},{16,8},{24,16},{28,24},{20,28},{12,20},{4,12},{1,5},{9... | collective-permute-start | bytes 884744 | tf_op jit(solution)/shard_map/ppermute | solution.py:682
  173.2 19.6 %collective-permute-start.30 = (bf16[48,3072]{1,0:T(8,128)(2,1)}, bf16[48,3072]{1,0:T(8,128)(2,1)S(1)}, u32[]{:S(2)}, u32[]{:S(2)}) collective-permute-start(bf16[48,3072]{1,0:T(8,128)(2,1)} %get-tuple-element.132.refs_0_), channel_id=1, source_target_pairs={{0,8},{8,16},{16,24},{24,28},{28,20},{20,12},{12,4},{4,0},{1,9},{9... | collective-permute-start | bytes 884744 | tf_op jit(solution)/shard_map/ppermute | solution.py:682
  174.8 18.1 %collective-permute-start.31 = (bf16[48,3072]{1,0:T(8,128)(2,1)}, bf16[48,3072]{1,0:T(8,128)(2,1)S(1)}, u32[]{:S(2)}, u32[]{:S(2)}) collective-permute-start(bf16[48,3072]{1,0:T(8,128)(2,1)} %get-tuple-element.133.refs_1_), channel_id=1, source_target_pairs={{0,4},{8,0},{16,8},{24,16},{28,24},{20,28},{12,20},{4,12},{1,5},{9... | collective-permute-start | bytes 884744 | tf_op jit(solution)/shard_map/ppermute | solution.py:682
  175.3 90.8 %collective-permute-start.29 = (bf16[512,1536]{1,0:T(8,128)(2,1)}, bf16[512,1536]{1,0:T(8,128)(2,1)}, u32[]{:S(2)}, u32[]{:S(2)}) collective-permute-start(bf16[512,1536]{1,0:T(8,128)(2,1)} %get-tuple-element.129.refs_2_), channel_id=1, source_target_pairs={{0,1},{1,0},{2,3},{3,2},{4,5},{5,4},{6,7},{7,6},{8,9},{9,8},{10,11... | collective-permute-start | bytes 4718600 | tf_op jit(solution)/shard_map/ppermute | solution.py:682
  196.2 33.5 %collective-permute-start.32 = (bf16[96,3072]{1,0:T(8,128)(2,1)}, bf16[96,3072]{1,0:T(8,128)(2,1)S(1)}, u32[]{:S(2)}, u32[]{:S(2)}) collective-permute-start(bf16[96,3072]{1,0:T(8,128)(2,1)} %get-tuple-element.140.refs_3_), channel_id=1, source_target_pairs={{0,8},{8,16},{16,24},{24,28},{28,20},{20,12},{12,4},{4,0},{1,9},{9... | collective-permute-start | bytes 1769480 | tf_op jit(solution)/shard_map/ppermute | solution.py:682
  197.7 32.0 %collective-permute-start.33 = (bf16[96,3072]{1,0:T(8,128)(2,1)}, bf16[96,3072]{1,0:T(8,128)(2,1)S(1)}, u32[]{:S(2)}, u32[]{:S(2)}) collective-permute-start(bf16[96,3072]{1,0:T(8,128)(2,1)} %get-tuple-element.141.refs_4_), channel_id=1, source_target_pairs={{0,4},{8,0},{16,8},{24,16},{28,24},{20,28},{12,20},{4,12},{1,5},{9... | collective-permute-start | bytes 1769480 | tf_op jit(solution)/shard_map/ppermute | solution.py:682
  233.4 19.5 %collective-permute-start.34 = (bf16[96,3072]{1,0:T(8,128)(2,1)}, bf16[96,3072]{1,0:T(8,128)(2,1)S(1)}, u32[]{:S(2)}, u32[]{:S(2)}) collective-permute-start(bf16[96,3072]{1,0:T(8,128)(2,1)} %get-tuple-element.148.refs_3_), channel_id=1, source_target_pairs={{0,8},{8,16},{16,24},{24,28},{28,20},{20,12},{12,4},{4,0},{1,9},{9... | collective-permute-start | bytes 1769480 | tf_op jit(solution)/shard_map/ppermute | solution.py:682
  234.9 18.1 %collective-permute-start.35 = (bf16[96,3072]{1,0:T(8,128)(2,1)}, bf16[96,3072]{1,0:T(8,128)(2,1)S(1)}, u32[]{:S(2)}, u32[]{:S(2)}) collective-permute-start(bf16[96,3072]{1,0:T(8,128)(2,1)} %get-tuple-element.149.refs_4_), channel_id=1, source_target_pairs={{0,4},{8,0},{16,8},{24,16},{28,24},{20,28},{12,20},{4,12},{1,5},{9... | collective-permute-start | bytes 1769480 | tf_op jit(solution)/shard_map/ppermute | solution.py:682
  270.2 32.6 %collective-permute-start.38 = (bf16[256,1536]{1,0:T(8,128)(2,1)}, bf16[256,1536]{1,0:T(8,128)(2,1)S(1)}, u32[]{:S(2)}, u32[]{:S(2)}) collective-permute-start(bf16[256,1536]{1,0:T(8,128)(2,1)} %get-tuple-element.152.refs_18_), channel_id=1, source_target_pairs={{0,2},{1,3},{2,0},{3,1},{4,6},{5,7},{6,4},{7,5},{8,10},{9,11},{10,... | collective-permute-start | bytes 2359304 | tf_op jit(solution)/shard_map/ppermute | solution.py:682
  278.2 24.5 %collective-permute-start.42 = (bf16[96,1536]{1,0:T(8,128)(2,1)S(1)}, bf16[96,1536]{1,0:T(8,128)(2,1)S(1)}, u32[]{:S(2)}, u32[]{:S(2)}) collective-permute-start(bf16[96,1536]{1,0:T(8,128)(2,1)S(1)} %get-tuple-element.231.refs_19_), channel_id=1, source_target_pairs={{0,16},{4,20},{8,24},{12,28},{1,17},{5,21},{9,25},{13,29},{2,18},{... | collective-permute-start | bytes 884744 | tf_op jit(solution)/shard_map/ppermute | solution.py:682
  280.4 22.3 %collective-permute-start.43 = (bf16[96,1536]{1,0:T(8,128)(2,1)S(1)}, bf16[96,1536]{1,0:T(8,128)(2,1)S(1)}, u32[]{:S(2)}, u32[]{:S(2)}) collective-permute-start(bf16[96,1536]{1,0:T(8,128)(2,1)S(1)} %get-tuple-element.230.refs_20_), channel_id=1, source_target_pairs={{0,0},{16,1},{1,2},{17,3},{2,4},{18,5},{3,6},{19,7},{4,8},{20,9},{... | collective-permute-start | bytes 884744 | tf_op jit(solution)/shard_map/ppermute | solution.py:682
  320.3 21.6 %collective-permute-start.45 = (bf16[256,1536]{1,0:T(8,128)(2,1)S(1)}, bf16[256,1536]{1,0:T(8,128)(2,1)S(1)}, u32[]{:S(2)}, u32[]{:S(2)}) collective-permute-start(bf16[256,1536]{1,0:T(8,128)(2,1)S(1)} %copy-done.43), channel_id=1, source_target_pairs={{0,2},{1,3},{2,0},{3,1},{4,6},{5,7},{6,4},{7,5},{8,10},{9,11},{10,... | collective-permute-start | bytes 2359304 | tf_op jit(solution)/shard_map/ppermute | solution.py:682
  361.5 23.7 %collective-permute-start.54 = (bf16[96,1536]{1,0:T(8,128)(2,1)}, bf16[96,1536]{1,0:T(8,128)(2,1)S(1)}, u32[]{:S(2)}, u32[]{:S(2)}) collective-permute-start(bf16[96,1536]{1,0:T(8,128)(2,1)} %get-tuple-element.233.refs_0_), channel_id=1, source_target_pairs={{16,0},{20,4},{24,8},{28,12},{17,1},{21,5},{25,9},{29,13},{18,2},{... | collective-permute-start | bytes 884744 | tf_op jit(solution)/shard_map/ppermute | solution.py:682
  (95 other events, 670.4 us)

commit v6 on v5

--- a/solution.py
+++ b/solution.py
@@ -466,7 +466,7 @@
         scratch_shapes=[
             *[pltpu.VMEM((block, width), F32)] * 3, pltpu.VMEM((N, width), F32),
             pltpu.VMEM((block // SUB, 2 * N, LANE), F32),
-            pltpu.VMEM((N, width), F32), pltpu.VMEM((chunks, block * SUB, LANE), F32),
+            pltpu.VMEM((N, width), F32), pltpu.VMEM((chunks, (block + 1) * SUB, LANE), F32),
         ],
         input_output_aliases={4 + k: k for k in range(len(kept))},
         compiler_params=PARAMS,
@@ -600,8 +600,8 @@
         scratch_shapes=[
             *[pltpu.VMEM((block, width), F32)] * 3, pltpu.VMEM((N, width), F32),
             pltpu.VMEM((block // SUB, 2 * N, LANE), F32), pltpu.VMEM((N, width), F32),
-            *[pltpu.VMEM((chunks, block * SUB, LANE), F32)] * 2,
-            pltpu.VMEM((2 * N * PITCH, LANE), F32), pltpu.VMEM((LANE, ITEM), F32), pltpu.VMEM((ITEM, LANE), F32),
+            *[pltpu.VMEM((chunks, (block + 1) * SUB, LANE), F32)] * 2,
+            pltpu.VMEM(((2 * N + 1) * PITCH, LANE), F32), pltpu.VMEM((LANE, ITEM), F32), pltpu.VMEM((ITEM, LANE), F32),
         ],
         input_output_aliases={7 + k: k for k in range(len(kept))},
         compiler_params=PARAMS,

time: 400 us -> 402 us (level)
  transfers between devices with their start and end apart: 60 -> 60, of which waited for: 19 -> 19; matrix products, arithmetic and copies ran while one was open for 6% -> 6% of each run, Pallas kernels for 37% -> 38%
where the time goes in v6:
time: 402 us; the launch traced here: 401 us
  Pallas kernels  190 us (47%)
  starting transfers between devices  82.3 us (20%)
  waiting for transfers between devices  77.1 us (19%)
  other arithmetic  23.2 us (6%)
  local copies, waits for them, and re-layouts  18.4 us (5%)
  between operations  7.38 us (2%)
    pallas_call x3, Pallas kernels, scan_backward(): pl.pallas_call(scan_backward_body, grid=(count, steps), in_specs=[tok, pl...  68.9 us
    ppermute x56, starting transfers between devices, moved(): lax.ppermute(with_layout_constraint(v, Layout(tuple(range(v.ndim)))), axe...  62.2 us
    ppermute x56, waiting for transfers between devices, moved(): lax.ppermute(with_layout_constraint(v, Layout(tuple(range(v.ndim)))), axe...  60.9 us
    pallas_call x2, Pallas kernels, scan_forward(): pl.pallas_call(scan_forward_body, grid=(count, steps), in_specs=[tok, pl....  32.5 us
    pallas_call x1, Pallas kernels, gates(): pl.pallas_call(lambda *refs: gates_body(items, len(blocks), *refs), grid=...  23.1 us
    pallas_call x1, Pallas kernels, mix_back(): pl.pallas_call(lambda *refs: mix_back_body(calls, len(blocks), *refs), gr...  20.7 us
    all_to_all x4, starting transfers between devices, exchange(): return lax.all_to_all(v, ALL, 0, 0, tiled=True)  20.1 us
    all_to_all x4, waiting for transfers between devices, exchange(): return lax.all_to_all(v, ALL, 0, 0, tiled=True)  16.2 us
  transfers between devices with their start and end apart: 60, of which 19 were waited for; matrix products, arithmetic and copies ran while one was open for 6% of the time, Pallas kernels for 38%

profile of v6, /device:TPU:0, one launch (start us, length us, event | category | flops | bytes accessed | tf_op | source)
XLA Modules:
  0.0 400.6 jit_solution(669357044628365692)
XLA Ops:
  10.0 6.6 %all-to-all-start = ((s32[32,1,1]{2,1,0:T(1,128)}), s32[32,1,1]{2,1,0:T(1,128)S(1)}, u32[]{:S(2)}, u32[]{:S(2)}) async-start(s32[32,1,1]{2,1,0:T(1,128)} %bitcast.43), calls=%async_computation | async-start | bytes 32768 | tf_op jit(solution)/shard_map/all_to_all | solution.py:766
  23.4 6.5 %collective-permute-done.6.refs_6_ = bf16[96,1792]{1,0:T(8,128)(2,1)} collective-permute-done((bf16[96,1792]{1,0:T(8,128)(2,1)S(1)}, bf16[96,1792]{1,0:T(8,128)(2,1)}, u32[]{:S(2)}, u32[]{:S(2)}) %collective-permute-start.6) | collective-permute-done | bytes 344096 | tf_op jit(solution)/shard_map/ppermute | solution.py:682
  35.8 6.8 %collective-permute-done.9.refs_9_ = bf16[96,1792]{1,0:T(8,128)(2,1)} collective-permute-done((bf16[96,1792]{1,0:T(8,128)(2,1)}, bf16[96,1792]{1,0:T(8,128)(2,1)}, u32[]{:S(2)}, u32[]{:S(2)}) %collective-permute-start.9) | collective-permute-done | bytes 344096 | tf_op jit(solution)/shard_map/ppermute | solution.py:682
  45.6 4.6 %all-to-all-start.1 = ((f32[32,4,144]{2,1,0:T(4,128)}), f32[32,4,144]{2,1,0:T(4,128)S(1)}, u32[]{:S(2)}, u32[]{:S(2)}) async-start(f32[32,4,144]{2,1,0:T(4,128)} %hold.13), calls=%async_computation.1 | async-start | bytes 262144 | tf_op jit(solution)/shard_map/all_to_all | solution.py:766
  51.9 6.7 %all-to-all-done.1 = f32[32,4,144]{2,1,0:T(4,128)S(1)} async-done(((f32[32,4,144]{2,1,0:T(4,128)}), f32[32,4,144]{2,1,0:T(4,128)S(1)}, u32[]{:S(2)}, u32[]{:S(2)}) %all-to-all-start.1) | async-done | bytes 73760 | tf_op jit(solution)/shard_map/all_to_all | solution.py:766
  61.8 4.7 %collective-permute-start.12 = (bf16[96,1792]{1,0:T(8,128)(2,1)}, bf16[96,1792]{1,0:T(8,128)(2,1)S(1)}, u32[]{:S(2)}, u32[]{:S(2)}) collective-permute-start(bf16[96,1792]{1,0:T(8,128)(2,1)} %collective-permute-done.10.refs_10_), channel_id=1, source_target_pairs={{0,8},{8,16},{16,24},{24,28},{28,20},{20,12},{12,4},{4,0},{1,9},{9... | collective-permute-start | bytes 1032200 | tf_op jit(solution)/shard_map/ppermute | solution.py:682
  69.4 5.8 %collective-permute-done.12.refs_12_ = bf16[96,1792]{1,0:T(8,128)(2,1)S(1)} collective-permute-done((bf16[96,1792]{1,0:T(8,128)(2,1)}, bf16[96,1792]{1,0:T(8,128)(2,1)S(1)}, u32[]{:S(2)}, u32[]{:S(2)}) %collective-permute-start.12) | collective-permute-done | bytes 344096 | tf_op jit(solution)/shard_map/ppermute | solution.py:682
  75.9 11.9 %mix.1 = (bf16[1024,1536]{1,0:T(8,128)(2,1)}, f32[1024,768]{1,0:T(8,128)}, f32[1024,768]{1,0:T(8,128)}, bf16[1024,768]{1,0:T(8,128)(2,1)}, f32[1024,128]{1,0:T(8...) custom-call(f32[4,4608]{1,0:T(4,128)} %broadcast_select_fusion.6.ref, ...), custom_call_target="tpu_custom_call" | custom-call | flops 11000000512 | bytes 11000000 | tf_op jit(solution)/shard_map/mix/pallas_call | solution.py:220
  97.6 4.2 %collective-permute-done.21 = f32[512,128]{1,0:T(8,128)S(1)} collective-permute-done((f32[512,128]{1,0:T(8,128)S(1)}, f32[512,128]{1,0:T(8,128)S(1)}, u32[]{:S(2)}, u32[]{:S(2)}) %collective-permute-start.21) | collective-permute-done | bytes 262176 | tf_op jit(solution)/shard_map/ppermute | solution.py:682
  101.9 8.6 %collective-permute-done.23.refs_0_.refs_10_ = bf16[96,3072]{1,0:T(8,128)(2,1)S(1)} collective-permute-done((bf16[96,3072]{1,0:T(8,128)(2,1)}, bf16[96,3072]{1,0:T(8,128)(2,1)S(1)}, u32[]{:S(2)}, u32[]{:S(2)}) %collective-permute-start.23) | collective-permute-done | bytes 589856 | tf_op jit(solution)/shard_map/ppermute | solution.py:682
  113.9 16.5 %scan_forward.2 = (f32[1024,768]{1,0:T(8,128)}, f32[16384,768]{1,0:T(8,128)}) custom-call(f32[1024,768]{1,0:T(8,128)} %get-tuple-element.121.u_ref, f32[1024,128]{1,0:T(8,128)} %pad_maximum_fusion.2.proj_ref.refs_5_, bf16[768,128]{1,0:T(8,128)(2,1)} %get-tuple-element.123.dt_ref, f32[32,768]{1,0:T(8,128)} %get-tuple-element.124.table_ref.refs_9_, ...), custom_call_target="tpu_custom_call" | custom-call | flops 16000000000 | bytes 16000000 | tf_op jit(solution)/shard_map/scan_forward/pallas_call | solution.py:460
  133.1 16.1 %scan_forward.3 = (f32[1024,768]{1,0:T(8,128)}, f32[16384,768]{1,0:T(8,128)}) custom-call(f32[1024,768]{1,0:T(8,128)} %get-tuple-element.121.u_ref, f32[1024,128]{1,0:T(8,128)} %pad_maximum_fusion.2.proj_ref.refs_5_, bf16[768,128]{1,0:T(8,128)(2,1)} %get-tuple-element.123.dt_ref, ...), custom_call_target="tpu_custom_call", output_to_operand_aliasing={{0}: (4, {}), {1}: (5, {})} | custom-call | flops 16000000000 | bytes 16000000 | tf_op jit(solution)/shard_map/scan_forward/pallas_call | solution.py:460
  150.0 23.1 %gates.1 = (f32[1024,768]{1,0:T(8,128)}, bf16[1024,768]{1,0:T(8,128)(2,1)}, bf16[512,1536]{1,0:T(8,128)(2,1)}, bf16[512,1536]{1,0:T(8,128)(2,1)}, bf16[768,1536]...) custom-call(bf16[1024,1536]{1,0:T(8,128)(2,1)} %get-tuple-element.12, ...), custom_call_target="tpu_custom_call" | custom-call | flops 24000000000 | bytes 24000000 | tf_op jit(solution)/shard_map/gates/pallas_call | solution.py:294
  175.2 18.1 %scan_backward.3 = (f32[1024,768]{1,0:T(8,128)}, bf16[1024,768]{1,0:T(8,128)(2,1)}, f32[1024,128]{1,0:T(8,128)}, f32[16,768]{1,0:T(8,128)}, f32[16,768]{1,0:T(8,128)}) custom-call(f32[1024,768]{1,0:T(8,128)} %get-tuple-element.121.u_ref, f32[1024,128]{1,0:T(8,128)} %pad_maximum_fusion.2.proj_ref.refs_5_, f32[1024,768]{1,0:T(8,128)} %get-tuple-element.130.dy_ref, ...), custom_call_target="tpu_custom_call" | custom-call | flops 15000000512 | bytes 15000000 | tf_op jit(solution)/shard_map/scan_backward/pallas_call | solution.py:588
  198.7 32.7 %scan_backward.4 = (f32[1024,768]{1,0:T(8,128)}, bf16[1024,768]{1,0:T(8,128)(2,1)}, f32[1024,128]{1,0:T(8,128)}, f32[16,768]{1,0:T(8,128)}, f32[16,768]{1,0:T(8,128)}) custom-call(f32[1024,768]{1,0:T(8,128)} %get-tuple-element.121.u_ref, f32[1024,128]{1,0:T(8,128)} %pad_maximum_fusion.2.proj_ref.refs_5_, ...), custom_call_target="tpu_custom_call", output_to_operand_aliasing={{0}: (7, {}), {1}: (8, {}), {2}: (9, {})} | custom-call | flops 30000001024 | bytes 30000000 | tf_op jit(solution)/shard_map/scan_backward/pallas_call | solution.py:588
  237.1 18.1 %scan_backward.5 = (f32[1024,768]{1,0:T(8,128)}, bf16[1024,768]{1,0:T(8,128)(2,1)}, f32[1024,128]{1,0:T(8,128)}, f32[16,768]{1,0:T(8,128)}, f32[16,768]{1,0:T(8,128)}) custom-call(f32[1024,768]{1,0:T(8,128)} %get-tuple-element.121.u_ref, f32[1024,128]{1,0:T(8,128)} %pad_maximum_fusion.2.proj_ref.refs_5_, ...), custom_call_target="tpu_custom_call", output_to_operand_aliasing={{0}: (7, {}), {1}: (8, {}), {2}: (9, {})} | custom-call | flops 15000000512 | bytes 15000000 | tf_op jit(solution)/shard_map/scan_backward/pallas_call | solution.py:588
  272.8 5.5 %collective-permute-done.40 = bf16[96,3072]{1,0:T(8,128)(2,1)S(1)} collective-permute-done((bf16[96,3072]{1,0:T(8,128)(2,1)}, bf16[96,3072]{1,0:T(8,128)(2,1)S(1)}, u32[]{:S(2)}, u32[]{:S(2)}) %collective-permute-start.40) | collective-permute-done | bytes 589856 | tf_op jit(solution)/shard_map/ppermute | solution.py:682
  284.2 20.7 %mix_back.1 = (f32[512,1536]{1,0:T(8,128)}, bf16[512,1536]{1,0:T(8,128)(2,1)}, bf16[96,1792]{1,0:T(8,128)(2,1)}, bf16[96,1792]{1,0:T(8,128)(2,1)}, bf16[96,1792]...) custom-call(bf16[1024,1536]{1,0:T(8,128)(2,1)} %get-tuple-element.12, ...), custom_call_target="tpu_custom_call" | custom-call | flops 19000000512 | bytes 19000000 | tf_op jit(solution)/shard_map/mix_back/pallas_call | solution.py:378
  324.1 7.0 %collective-permute-done.48.up_ref = bf16[96,1792]{1,0:T(8,128)(2,1)S(1)} collective-permute-done((bf16[96,1792]{1,0:T(8,128)(2,1)}, bf16[96,1792]{1,0:T(8,128)(2,1)S(1)}, u32[]{:S(2)}, u32[]{:S(2)}) %collective-permute-start.48) | collective-permute-done | bytes 344096 | tf_op jit(solution)/shard_map/ppermute | solution.py:682
  337.4 6.8 %collective-permute-done.50.up_ref = bf16[96,1792]{1,0:T(8,128)(2,1)S(1)} collective-permute-done((bf16[96,1792]{1,0:T(8,128)(2,1)}, bf16[96,1792]{1,0:T(8,128)(2,1)S(1)}, u32[]{:S(2)}, u32[]{:S(2)}) %collective-permute-start.50) | collective-permute-done | bytes 344096 | tf_op jit(solution)/shard_map/ppermute | solution.py:682
  351.8 4.2 %fusion.10 = (bf16[1536]{0:T(1024)(128)(2,1)S(1)}, f32[256,1536]{1,0:T(8,128)}, f32[256,1536]{1,0:T(8,128)}) fusion(f32[256,1536]{1,0:T(8,128)} %get-tuple-element.151, bf16[256,1536]{1,0:T(8,128)(2,1)S(1)} %copy-done.3, f32[1536]{0:T(1024)S(1)} %get-tuple-element.218, bf16[256,1536]{1,0:T(8,128)(2,1)S(1)} %copy-done.1, f32[256]{0:T(256)S(1)} %get-tuple-element.242, ...), kind=kLoop, calls=%fused_computation.16 | loop fusion | flops 7469568 | bytes 9456896 | tf_op jit(solution)/shard_map/reduce_sum | solution.py:913
  374.1 4.9 %all-to-all-start.3 = ((f32[32,1,128]{2,1,0:T(1,128)}), f32[32,1,128]{2,1,0:T(1,128)S(1)}, u32[]{:S(2)}, u32[]{:S(2)}) async-start(f32[32,1,128]{2,1,0:T(1,128)} %broadcast_in_dim.63), calls=%async_computation.3 | async-start | bytes 32768 | tf_op jit(solution)/shard_map/all_to_all | solution.py:766
  380.4 5.7 %all-to-all-done.3 = f32[32,1,128]{2,1,0:T(1,128)S(1)} async-done(((f32[32,1,128]{2,1,0:T(1,128)}), f32[32,1,128]{2,1,0:T(1,128)S(1)}, u32[]{:S(2)}, u32[]{:S(2)}) %all-to-all-start.3) | async-done | bytes 16416 | tf_op jit(solution)/shard_map/all_to_all | solution.py:766
  388.3 11.2 %update.1 = (f32[144,1536]{1,0:T(8,128)}, f32[144,1536]{1,0:T(8,128)}, f32[144,1536]{1,0:T(8,128)}, f32[144,1536]{1,0:T(8,128)}, f32[192,1536]{1,0:T(8,128)}, /*...) custom-call(f32[1,1]{1,0:T(1,128)} %bitcast.10.factor_ref, ...), custom_call_target="tpu_custom_call" | custom-call | flops 11000000512 | bytes 11000000 | tf_op jit(solution)/shard_map/update/pallas_call | solution.py:649
  (312 shorter events, 136.3 us)
Async XLA Ops:
  2.2 18.0 %collective-permute-start = (bf16[96,1536]{1,0:T(8,128)(2,1)S(1)}, bf16[96,1536]{1,0:T(8,128)(2,1)S(1)}, u32[]{:S(2)}, u32[]{:S(2)}) collective-permute-start(bf16[96,1536]{1,0:T(8,128)(2,1)S(1)} %broadcast_select_fusion.5.refs_0_), channel_id=1, source_target_pairs={{0,16},{4,20},{8,24},{12,28},{16,0},{20,4},{24,8},{28,12},{1,17},{... | collective-permute-start | bytes 884744 | tf_op jit(solution)/shard_map/ppermute | solution.py:682
  10.0 23.4 %all-to-all-start = ((s32[32,1,1]{2,1,0:T(1,128)}), s32[32,1,1]{2,1,0:T(1,128)S(1)}, u32[]{:S(2)}, u32[]{:S(2)}) async-start(s32[32,1,1]{2,1,0:T(1,128)} %bitcast.43), calls=%async_computation | async-start | bytes 32768 | tf_op jit(solution)/shard_map/all_to_all | solution.py:766
  16.6 42.9 %collective-permute-start.2 = (bf16[256,1536]{1,0:T(8,128)(2,1)S(1)}, bf16[256,1536]{1,0:T(8,128)(2,1)}, u32[]{:S(2)}, u32[]{:S(2)}) collective-permute-start(bf16[256,1536]{1,0:T(8,128)(2,1)S(1)} %copy-done), channel_id=1, source_target_pairs={{0,2},{1,3},{2,0},{3,1},{4,6},{5,7},{6,4},{7,5},{8,10},{9,11},{10,... | collective-permute-start | bytes 2359304 | tf_op jit(solution)/shard_map/ppermute | solution.py:682
  33.7 26.8 %collective-permute-start.15 = (bf16[256,1536]{1,0:T(8,128)(2,1)}, bf16[256,1536]{1,0:T(8,128)(2,1)}, u32[]{:S(2)}, u32[]{:S(2)}) collective-permute-start(bf16[256,1536]{1,0:T(8,128)(2,1)} %hold.17.refs_14_.refs_3_), channel_id=1, source_target_pairs={{0,2},{1,3},{2,0},{3,1},{4,6},{5,7},{6,4},{7,5},{8,10},{9,11},{10,... | collective-permute-start | bytes 2359304 | tf_op jit(solution)/shard_map/ppermute | solution.py:682
  42.6 16.8 %collective-permute-start.11 = (bf16[96,1792]{1,0:T(8,128)(2,1)}, bf16[96,1792]{1,0:T(8,128)(2,1)S(1)}, u32[]{:S(2)}, u32[]{:S(2)}) collective-permute-start(bf16[96,1792]{1,0:T(8,128)(2,1)} %collective-permute-done.9.refs_9_), channel_id=1, source_target_pairs={{0,4},{8,0},{16,8},{24,16},{28,24},{20,28},{12,20},{4,12},{1,5},{9... | collective-permute-start | bytes 1032200 | tf_op jit(solution)/shard_map/ppermute | solution.py:682
  42.9 17.2 %collective-permute-start.10 = (bf16[96,1792]{1,0:T(8,128)(2,1)S(1)}, bf16[96,1792]{1,0:T(8,128)(2,1)}, u32[]{:S(2)}, u32[]{:S(2)}) collective-permute-start(bf16[96,1792]{1,0:T(8,128)(2,1)S(1)} %collective-permute-done.8.refs_0_.refs_8_), channel_id=1, source_target_pairs={{0,8},{8,16},{16,24},{24,28},{28,20},{20,12},{12,4},{4,0},{1,9},{9... | collective-permute-start | bytes 1032200 | tf_op jit(solution)/shard_map/ppermute | solution.py:682
  67.3 20.5 %collective-permute-start.18 = (bf16[96,3072]{1,0:T(8,128)(2,1)}, bf16[96,3072]{1,0:T(8,128)(2,1)S(1)}, u32[]{:S(2)}, u32[]{:S(2)}) collective-permute-start(bf16[96,3072]{1,0:T(8,128)(2,1)} %hold.16.refs_13_.refs_7_), channel_id=1, source_target_pairs={{0,8},{8,16},{16,24},{24,28},{28,20},{20,12},{12,4},{4,0},{1,9},{9... | collective-permute-start | bytes 1769480 | tf_op jit(solution)/shard_map/ppermute | solution.py:682
  67.4 20.5 %collective-permute-start.19 = (bf16[96,3072]{1,0:T(8,128)(2,1)}, bf16[96,3072]{1,0:T(8,128)(2,1)S(1)}, u32[]{:S(2)}, u32[]{:S(2)}) collective-permute-start(bf16[96,3072]{1,0:T(8,128)(2,1)} %hold.16.refs_13_.refs_7_), channel_id=1, source_target_pairs={{0,4},{8,0},{16,8},{24,16},{28,24},{20,28},{12,20},{4,12},{1,5},{9... | collective-permute-start | bytes 1769480 | tf_op jit(solution)/shard_map/ppermute | solution.py:682
  110.5 19.8 %collective-permute-start.25 = (bf16[96,3072]{1,0:T(8,128)(2,1)S(1)}, bf16[96,3072]{1,0:T(8,128)(2,1)S(1)}, u32[]{:S(2)}, u32[]{:S(2)}) collective-permute-start(bf16[96,3072]{1,0:T(8,128)(2,1)S(1)} %collective-permute-done.23.refs_0_.refs_10_), channel_id=1, source_target_pairs={{0,8},{8,16},{16,24},{24,28},{28,20},{20,12},{12,4},{4,0},{1,9},{9... | collective-permute-start | bytes 1769480 | tf_op jit(solution)/shard_map/ppermute | solution.py:682
  112.9 19.5 %collective-permute-start.26 = (bf16[96,3072]{1,0:T(8,128)(2,1)S(1)}, bf16[96,3072]{1,0:T(8,128)(2,1)S(1)}, u32[]{:S(2)}, u32[]{:S(2)}) collective-permute-start(bf16[96,3072]{1,0:T(8,128)(2,1)S(1)} %collective-permute-done.24.refs_1_.refs_11_), channel_id=1, source_target_pairs={{0,4},{8,0},{16,8},{24,16},{28,24},{20,28},{12,20},{4,12},{1,5},{9... | collective-permute-start | bytes 1769480 | tf_op jit(solution)/shard_map/ppermute | solution.py:682
  130.4 18.8 %collective-permute-start.27 = (bf16[48,3072]{1,0:T(8,128)(2,1)S(1)}, bf16[48,3072]{1,0:T(8,128)(2,1)S(1)}, u32[]{:S(2)}, u32[]{:S(2)}) collective-permute-start(bf16[48,3072]{1,0:T(8,128)(2,1)S(1)} %slice.109), channel_id=1, source_target_pairs={{0,8},{8,16},{16,24},{24,28},{28,20},{20,12},{12,4},{4,0},{1,9},{9... | collective-permute-start | bytes 884744 | tf_op jit(solution)/shard_map/ppermute | solution.py:682
  132.4 16.9 %collective-permute-start.28 = (bf16[48,3072]{1,0:T(8,128)(2,1)S(1)}, bf16[48,3072]{1,0:T(8,128)(2,1)S(1)}, u32[]{:S(2)}, u32[]{:S(2)}) collective-permute-start(bf16[48,3072]{1,0:T(8,128)(2,1)S(1)} %slice.110), channel_id=1, source_target_pairs={{0,4},{8,0},{16,8},{24,16},{28,24},{20,28},{12,20},{4,12},{1,5},{9... | collective-permute-start | bytes 884744 | tf_op jit(solution)/shard_map/ppermute | solution.py:682
  173.1 20.2 %collective-permute-start.30 = (bf16[48,3072]{1,0:T(8,128)(2,1)}, bf16[48,3072]{1,0:T(8,128)(2,1)S(1)}, u32[]{:S(2)}, u32[]{:S(2)}) collective-permute-start(bf16[48,3072]{1,0:T(8,128)(2,1)} %get-tuple-element.132.refs_0_), channel_id=1, source_target_pairs={{0,8},{8,16},{16,24},{24,28},{28,20},{20,12},{12,4},{4,0},{1,9},{9... | collective-permute-start | bytes 884744 | tf_op jit(solution)/shard_map/ppermute | solution.py:682
  174.7 18.7 %collective-permute-start.31 = (bf16[48,3072]{1,0:T(8,128)(2,1)}, bf16[48,3072]{1,0:T(8,128)(2,1)S(1)}, u32[]{:S(2)}, u32[]{:S(2)}) collective-permute-start(bf16[48,3072]{1,0:T(8,128)(2,1)} %get-tuple-element.133.refs_1_), channel_id=1, source_target_pairs={{0,4},{8,0},{16,8},{24,16},{28,24},{20,28},{12,20},{4,12},{1,5},{9... | collective-permute-start | bytes 884744 | tf_op jit(solution)/shard_map/ppermute | solution.py:682
  175.2 93.2 %collective-permute-start.29 = (bf16[512,1536]{1,0:T(8,128)(2,1)}, bf16[512,1536]{1,0:T(8,128)(2,1)}, u32[]{:S(2)}, u32[]{:S(2)}) collective-permute-start(bf16[512,1536]{1,0:T(8,128)(2,1)} %get-tuple-element.129.refs_2_), channel_id=1, source_target_pairs={{0,1},{1,0},{2,3},{3,2},{4,5},{5,4},{6,7},{7,6},{8,9},{9,8},{10,11... | collective-permute-start | bytes 4718600 | tf_op jit(solution)/shard_map/ppermute | solution.py:682
  196.6 34.7 %collective-permute-start.32 = (bf16[96,3072]{1,0:T(8,128)(2,1)}, bf16[96,3072]{1,0:T(8,128)(2,1)S(1)}, u32[]{:S(2)}, u32[]{:S(2)}) collective-permute-start(bf16[96,3072]{1,0:T(8,128)(2,1)} %get-tuple-element.140.refs_3_), channel_id=1, source_target_pairs={{0,8},{8,16},{16,24},{24,28},{28,20},{20,12},{12,4},{4,0},{1,9},{9... | collective-permute-start | bytes 1769480 | tf_op jit(solution)/shard_map/ppermute | solution.py:682
  198.1 33.2 %collective-permute-start.33 = (bf16[96,3072]{1,0:T(8,128)(2,1)}, bf16[96,3072]{1,0:T(8,128)(2,1)S(1)}, u32[]{:S(2)}, u32[]{:S(2)}) collective-permute-start(bf16[96,3072]{1,0:T(8,128)(2,1)} %get-tuple-element.141.refs_4_), channel_id=1, source_target_pairs={{0,4},{8,0},{16,8},{24,16},{28,24},{20,28},{12,20},{4,12},{1,5},{9... | collective-permute-start | bytes 1769480 | tf_op jit(solution)/shard_map/ppermute | solution.py:682
  235.1 20.1 %collective-permute-start.34 = (bf16[96,3072]{1,0:T(8,128)(2,1)}, bf16[96,3072]{1,0:T(8,128)(2,1)S(1)}, u32[]{:S(2)}, u32[]{:S(2)}) collective-permute-start(bf16[96,3072]{1,0:T(8,128)(2,1)} %get-tuple-element.148.refs_3_), channel_id=1, source_target_pairs={{0,8},{8,16},{16,24},{24,28},{28,20},{20,12},{12,4},{4,0},{1,9},{9... | collective-permute-start | bytes 1769480 | tf_op jit(solution)/shard_map/ppermute | solution.py:682
  236.6 18.6 %collective-permute-start.35 = (bf16[96,3072]{1,0:T(8,128)(2,1)}, bf16[96,3072]{1,0:T(8,128)(2,1)S(1)}, u32[]{:S(2)}, u32[]{:S(2)}) collective-permute-start(bf16[96,3072]{1,0:T(8,128)(2,1)} %get-tuple-element.149.refs_4_), channel_id=1, source_target_pairs={{0,4},{8,0},{16,8},{24,16},{28,24},{20,28},{12,20},{4,12},{1,5},{9... | collective-permute-start | bytes 1769480 | tf_op jit(solution)/shard_map/ppermute | solution.py:682
  272.4 32.6 %collective-permute-start.38 = (bf16[256,1536]{1,0:T(8,128)(2,1)}, bf16[256,1536]{1,0:T(8,128)(2,1)S(1)}, u32[]{:S(2)}, u32[]{:S(2)}) collective-permute-start(bf16[256,1536]{1,0:T(8,128)(2,1)} %get-tuple-element.152.refs_18_), channel_id=1, source_target_pairs={{0,2},{1,3},{2,0},{3,1},{4,6},{5,7},{6,4},{7,5},{8,10},{9,11},{10,... | collective-permute-start | bytes 2359304 | tf_op jit(solution)/shard_map/ppermute | solution.py:682
  280.5 24.5 %collective-permute-start.42 = (bf16[96,1536]{1,0:T(8,128)(2,1)S(1)}, bf16[96,1536]{1,0:T(8,128)(2,1)S(1)}, u32[]{:S(2)}, u32[]{:S(2)}) collective-permute-start(bf16[96,1536]{1,0:T(8,128)(2,1)S(1)} %get-tuple-element.231.refs_19_), channel_id=1, source_target_pairs={{0,16},{4,20},{8,24},{12,28},{1,17},{5,21},{9,25},{13,29},{2,18},{... | collective-permute-start | bytes 884744 | tf_op jit(solution)/shard_map/ppermute | solution.py:682
  282.7 22.3 %collective-permute-start.43 = (bf16[96,1536]{1,0:T(8,128)(2,1)S(1)}, bf16[96,1536]{1,0:T(8,128)(2,1)S(1)}, u32[]{:S(2)}, u32[]{:S(2)}) collective-permute-start(bf16[96,1536]{1,0:T(8,128)(2,1)S(1)} %get-tuple-element.230.refs_20_), channel_id=1, source_target_pairs={{0,0},{16,1},{1,2},{17,3},{2,4},{18,5},{3,6},{19,7},{4,8},{20,9},{... | collective-permute-start | bytes 884744 | tf_op jit(solution)/shard_map/ppermute | solution.py:682
  322.5 21.6 %collective-permute-start.45 = (bf16[256,1536]{1,0:T(8,128)(2,1)S(1)}, bf16[256,1536]{1,0:T(8,128)(2,1)S(1)}, u32[]{:S(2)}, u32[]{:S(2)}) collective-permute-start(bf16[256,1536]{1,0:T(8,128)(2,1)S(1)} %copy-done.43), channel_id=1, source_target_pairs={{0,2},{1,3},{2,0},{3,1},{4,6},{5,7},{6,4},{7,5},{8,10},{9,11},{10,... | collective-permute-start | bytes 2359304 | tf_op jit(solution)/shard_map/ppermute | solution.py:682
  363.8 23.7 %collective-permute-start.54 = (bf16[96,1536]{1,0:T(8,128)(2,1)}, bf16[96,1536]{1,0:T(8,128)(2,1)S(1)}, u32[]{:S(2)}, u32[]{:S(2)}) collective-permute-start(bf16[96,1536]{1,0:T(8,128)(2,1)} %get-tuple-element.233.refs_0_), channel_id=1, source_target_pairs={{16,0},{20,4},{24,8},{28,12},{17,1},{21,5},{25,9},{29,13},{18,2},{... | collective-permute-start | bytes 884744 | tf_op jit(solution)/shard_map/ppermute | solution.py:682
  (95 other events, 670.4 us)
